TPU v7x, 128 devices: a whole 4x4x4 slice. The times are simulated.
128 devices in a mesh: section: 2 (over core), seq: 8 (over x, z_hi), wshard: 8 (over y, z_lo).
Axes of the slice: x: 4, y: 4, z: 4 (z_hi: 2, z_lo: 2; z = z_hi * 2 + z_lo), core: 2. Of those that a mesh axis runs over, the one named last changes fastest.
Arguments:
- tokens: bfloat16 [16, 1024, 1024], P('wshard', 'seq'), may hold values from -6 to 6
- positions: int32 [16, 1024], P('wshard'), may hold values from 0 to 1021, as said below
- w_qkv: bfloat16 [2, 1024, 3072], P('section', 'wshard'), may hold values from -0.1875 to 0.1875
- b_qkv: bfloat16 [2, 3072], P('section', 'wshard'), may hold values from -1.1953125 to 1.1953125
- w_dense: bfloat16 [2, 1024, 1024], P('section', 'wshard'), may hold values from -3 to 3
- b_dense: bfloat16 [2, 1024], P('section', 'wshard'), may hold values from -1.1953125 to 1.1953125
- w_up: bfloat16 [2, 1024, 4096], P('section', 'wshard'), may hold values from -0.1875 to 0.1875
- b_up: bfloat16 [2, 4096], P('section', 'wshard'), may hold values from -1.1953125 to 1.1953125
- w_down: bfloat16 [2, 4096, 1024], P('section', 'wshard'), may hold values from -0.09375 to 0.09375
- b_down: bfloat16 [2, 1024], P('section', 'wshard'), may hold values from -1.1953125 to 1.1953125
- norm1_gain: bfloat16 [2, 1024], P('section', 'wshard'), may hold values from 0.5 to 1.5
- norm1_shift: bfloat16 [2, 1024], P('section', 'wshard'), may hold values from -1.1953125 to 1.1953125
- norm2_gain: bfloat16 [2, 1024], P('section', 'wshard'), may hold values from 0.5 to 1.5
- norm2_shift: bfloat16 [2, 1024], P('section', 'wshard'), may hold values from -1.1953125 to 1.1953125
- cotangent: bfloat16 [16, 1024, 1024], P('wshard', 'seq'), may hold values from -6 to 6
Outputs:
- hidden: bfloat16 [2, 16, 1024, 1024], P('section', 'wshard', 'seq')
- in_grads: float32 [2, 16, 1024, 1024], P('section', 'wshard', 'seq')
- grad_w_qkv: float32 [2, 1024, 3072], P('section', 'wshard')
- grad_b_qkv: float32 [2, 2048], P('section', 'wshard')
- grad_b_values: float32 [2, 1024], P('section', 'wshard')
- grad_w_dense: float32 [2, 1024, 1024], P('section', 'wshard')
- grad_b_dense: float32 [2, 1024], P('section', 'wshard')
- grad_w_up: float32 [2, 1024, 4096], P('section', 'wshard')
- grad_b_up: float32 [2, 4096], P('section', 'wshard')
- grad_w_down: float32 [2, 4096, 1024], P('section', 'wshard')
- grad_b_down: float32 [2, 1024], P('section', 'wshard')
- grad_norm1_gain: float32 [2, 1024], P('section', 'wshard')
- grad_norm1_shift: float32 [2, 1024], P('section', 'wshard')
- grad_norm2_gain: float32 [2, 1024], P('section', 'wshard')
- grad_norm2_shift: float32 [2, 1024], P('section', 'wshard')
Inputs may be any that keep to these rules, and one draw needn't show every extreme that they name: Each sequence packs three documents; positions count from 0 at each document's first token and rise by one; the middle document begins within the first 128 tokens (the first 4 where 128 is smaller) and ends within the last 128 tokens (the last 4 where 128 is smaller).
All inputs are finite; a program needn't handle non-finite values.
Results may differ from a plain program's by a relative error of at most 0.018.
Values may be sent and summed in bfloat16 or wider, within the bound.
No kernel may reach another device: no remote copies, remote signals or barrier semaphores. Data moves between devices by JAX's collectives and lax.ppermute only.
A program may use at most 256 MiB of HBM per device.

v0:
```python
import math

import jax
import jax.numpy as jnp
from jax import lax
from jax.sharding import PartitionSpec as P

HEAD = 64
ROT = 16
FF = 4096


NORM_EPS = 1e-05


def passed_along(block, axis, distance):
    devices = range(lax.axis_size(axis))
    route = [(i - distance, i) for i in devices if i - distance in devices]
    return lax.ppermute(block, axis, route)


def norm_rows(values, gain, shift):
    centre = jnp.mean(values, axis=-1, keepdims=True)
    centred = values - centre
    spread = jnp.mean(centred * centred, axis=-1, keepdims=True)
    return centred * lax.rsqrt(spread + NORM_EPS) * gain + shift


def rotate(values, places):
    half_width = ROT // 2
    frequency = 1.0 / 10000.0 ** (jnp.arange(half_width).astype(jnp.float32) * 2.0 / ROT)
    angles = places.astype(jnp.float32)[:, None] * frequency[None, :]
    cosine = jnp.concatenate([jnp.cos(angles), jnp.cos(angles)], axis=-1)[:, None, :]
    sine_part = jnp.concatenate([jnp.sin(angles), jnp.sin(angles)], axis=-1)[:, None, :]
    leading = values[..., :ROT]
    turned = jnp.concatenate([-leading[..., half_width:], leading[..., :half_width]], axis=-1)
    return jnp.concatenate([leading * cosine + turned * sine_part, values[..., ROT:]], axis=-1)


def unrotate(grad_rot, places):
    _, pull = jax.vjp(lambda moved: rotate(moved, places), grad_rot)
    return pull(grad_rot)[0]


def gelu_exact(values):
    return jax.nn.gelu(values, approximate=False)


def product(left, right):
    return jnp.dot(left, right, preferred_element_type=jnp.float32)


def product_left(left, right):
    return lax.dot_general(
        left, right, (((0,), (0,)), ((), ())), preferred_element_type=jnp.float32
    )


def product_right(left, right):
    return lax.dot_general(
        left, right, (((1,), (1,)), ((), ())), preferred_element_type=jnp.float32
    )


def block_scores(query_block, keys_rot, place_block, offset, length):
    block_rows = query_block.shape[0]
    query_rows = offset + jnp.arange(block_rows, dtype=jnp.int32)
    key_rows = jnp.arange(length, dtype=jnp.int32)
    behind = key_rows[None, :] <= query_rows[:, None]
    inside = query_rows[:, None] - key_rows[None, :] <= place_block[:, None]
    scaling = 1.0 / math.sqrt(HEAD)
    scores = (
        jnp.einsum("qhd,khd->hqk", query_block, keys_rot, preferred_element_type=jnp.float32)
        * scaling
    )
    return jnp.where((behind & inside)[None], scores, -1e30)


def attend_forward(queries, keys_rot, values, places):
    length = queries.shape[0]
    block_rows = min(512, length)

    def one_block(carried, offset):
        query_block = lax.dynamic_slice_in_dim(queries, offset, block_rows, 0)
        place_block = lax.dynamic_slice_in_dim(places, offset, block_rows, 0)
        scores = block_scores(query_block, keys_rot, place_block, offset, length)
        highest = jnp.max(scores, axis=-1, keepdims=True)
        exponent = jnp.exp(scores - highest)
        denominator = jnp.sum(exponent, axis=-1, keepdims=True)
        attn_probs = (exponent / denominator).astype(jnp.bfloat16)
        mixed = jnp.einsum("hqk,khd->qhd", attn_probs, values, preferred_element_type=jnp.float32)
        return (carried, (mixed, (highest + jnp.log(denominator))[..., 0]))

    offsets = jnp.arange(length // block_rows, dtype=jnp.int32) * block_rows
    _, (mixed, log_total) = lax.scan(one_block, 0, offsets)
    return (mixed.reshape(queries.shape), log_total)


def attend_backward(queries, keys_rot, values, places, log_total, grad_mixed):
    length = queries.shape[0]
    block_rows = min(512, length)
    scaling = 1.0 / math.sqrt(HEAD)

    def one_block(carried, element):
        grad_keys, grad_values = carried
        offset, total_block = element
        query_block = lax.dynamic_slice_in_dim(queries, offset, block_rows, 0)
        place_block = lax.dynamic_slice_in_dim(places, offset, block_rows, 0)
        grad_block = lax.dynamic_slice_in_dim(grad_mixed, offset, block_rows, 0)
        scores = block_scores(query_block, keys_rot, place_block, offset, length)
        probs = jnp.exp(scores - total_block[..., None])
        probs_low = probs.astype(jnp.bfloat16)
        grad_probs = jnp.einsum(
            "qhd,khd->hqk", grad_block, values, preferred_element_type=jnp.float32
        )
        centre = jnp.sum(grad_probs * probs, axis=-1, keepdims=True)
        grad_scores = (probs * (grad_probs - centre)).astype(jnp.bfloat16)
        grad_query = (
            jnp.einsum("hqk,khd->qhd", grad_scores, keys_rot, preferred_element_type=jnp.float32)
            * scaling
        )
        grad_keys = (
            grad_keys
            + jnp.einsum(
                "hqk,qhd->khd", grad_scores, query_block, preferred_element_type=jnp.float32
            )
            * scaling
        )
        grad_values = grad_values + jnp.einsum(
            "hqk,qhd->khd", probs_low, grad_block, preferred_element_type=jnp.float32
        )
        return ((grad_keys, grad_values), grad_query)

    offsets = jnp.arange(length // block_rows, dtype=jnp.int32) * block_rows
    empty = jnp.zeros(queries.shape, jnp.float32)
    (grad_keys, grad_values), grad_queries = lax.scan(
        one_block, (empty, empty), (offsets, log_total)
    )
    return (grad_queries.reshape(queries.shape), grad_keys, grad_values)


def split_heads(by_heads, places):
    length = by_heads.shape[0]
    heads_per = by_heads.shape[3] // HEAD
    queries = rotate(by_heads[:, 0, 0].astype(jnp.float32).reshape(length, heads_per, HEAD), places)
    keys_rot = rotate(
        by_heads[:, 1, 0].astype(jnp.float32).reshape(length, heads_per, HEAD), places
    )
    values = by_heads[:, 2, 0].reshape(length, heads_per, HEAD)
    return (queries.astype(jnp.bfloat16), keys_rot.astype(jnp.bfloat16), values)


def layer_forward(layer_in, places, weights):
    (
        w_qkv,
        b_qkv,
        w_dense,
        b_dense,
        w_up,
        b_up,
        w_down,
        b_down,
        gain_one,
        shift_one,
        gain_two,
        shift_two,
    ) = weights
    tok_rows = layer_in.shape[0]
    groups = lax.axis_size("seq")
    normed_one = norm_rows(
        layer_in, gain_one.astype(jnp.float32), shift_one.astype(jnp.float32)
    ).astype(jnp.bfloat16)
    projected = (product(normed_one, w_qkv) + b_qkv.astype(jnp.float32)).astype(jnp.bfloat16)
    by_heads = lax.all_to_all(
        projected.reshape(tok_rows, 3, groups, -1), "seq", split_axis=2, concat_axis=0, tiled=True
    )
    queries, keys_rot, values = split_heads(by_heads, places)
    mixed, log_total = attend_forward(queries, keys_rot, values, places)
    length = mixed.shape[0]
    mixed = mixed.astype(jnp.bfloat16).reshape(length, 1, -1)
    merged = lax.all_to_all(mixed, "seq", split_axis=0, concat_axis=1, tiled=True).reshape(
        tok_rows, -1
    )
    normed_two = norm_rows(
        layer_in, gain_two.astype(jnp.float32), shift_two.astype(jnp.float32)
    ).astype(jnp.bfloat16)
    middle = product(normed_two, w_up) + b_up.astype(jnp.float32)
    activated = gelu_exact(middle).astype(jnp.bfloat16)
    result = (
        layer_in
        + product(merged, w_dense)
        + b_dense.astype(jnp.float32)
        + product(activated, w_down)
        + b_down.astype(jnp.float32)
    )
    return (result, (by_heads, log_total, merged, middle))


def layer_backward(layer_in, places, weights, stored, incoming):
    (
        w_qkv,
        b_qkv,
        w_dense,
        b_dense,
        w_up,
        b_up,
        w_down,
        b_down,
        gain_one,
        shift_one,
        gain_two,
        shift_two,
    ) = weights
    by_heads, log_total, merged, middle = stored
    tok_rows = layer_in.shape[0]
    groups = lax.axis_size("seq")
    gain_first = gain_one.astype(jnp.float32)
    shift_first = shift_one.astype(jnp.float32)
    gain_second = gain_two.astype(jnp.float32)
    shift_second = shift_two.astype(jnp.float32)
    normed_one = norm_rows(layer_in, gain_first, shift_first).astype(jnp.bfloat16)
    normed_two = norm_rows(layer_in, gain_second, shift_second).astype(jnp.bfloat16)
    activated = gelu_exact(middle).astype(jnp.bfloat16)
    upstream = incoming.astype(jnp.float32)
    grad_w_down = product_left(activated, incoming)
    grad_b_down = jnp.sum(upstream, axis=0)
    grad_activated = product_right(incoming, w_down)
    _, pull_gelu = jax.vjp(gelu_exact, middle)
    grad_middle = pull_gelu(grad_activated)[0].astype(jnp.bfloat16)
    grad_w_up = product_left(normed_two, grad_middle)
    grad_b_up = jnp.sum(grad_middle.astype(jnp.float32), axis=0)
    grad_normed_two = product_right(grad_middle, w_up)
    grad_w_dense = product_left(merged, incoming)
    grad_merged = product_right(incoming, w_dense).astype(jnp.bfloat16)
    grad_heads = lax.all_to_all(
        grad_merged.reshape(tok_rows, groups, -1), "seq", split_axis=1, concat_axis=0, tiled=True
    )
    queries, keys_rot, values = split_heads(by_heads, places)
    length = queries.shape[0]
    grad_heads = grad_heads.reshape(values.shape)
    grad_queries, grad_keys, grad_values = attend_backward(
        queries, keys_rot, values, places, log_total, grad_heads
    )
    grad_queries = unrotate(grad_queries, places).reshape(length, -1)
    grad_keys = unrotate(grad_keys, places).reshape(length, -1)
    grad_stack = jnp.stack([grad_queries, grad_keys, grad_values.reshape(length, -1)], axis=1)
    grad_stack = grad_stack[:, :, None, :].astype(jnp.bfloat16)
    grad_projected = lax.all_to_all(
        grad_stack, "seq", split_axis=0, concat_axis=2, tiled=True
    ).reshape(tok_rows, -1)
    grad_w_qkv = product_left(normed_one, grad_projected)
    grad_b_qkv = jnp.sum(grad_projected.astype(jnp.float32), axis=0)
    grad_normed_one = product_right(grad_projected, w_qkv)
    _, pull_one = jax.vjp(norm_rows, layer_in, gain_first, shift_first)
    input_one, grad_gain_one, grad_shift_one = pull_one(grad_normed_one)
    _, pull_two = jax.vjp(norm_rows, layer_in, gain_second, shift_second)
    input_two, grad_gain_two, grad_shift_two = pull_two(grad_normed_two)
    grad_input = upstream + input_one + input_two
    terms = (
        grad_w_qkv,
        grad_b_qkv,
        grad_w_dense,
        grad_b_down,
        grad_w_up,
        grad_b_up,
        grad_w_down,
        grad_b_down,
        grad_gain_one,
        grad_shift_one,
        grad_gain_two,
        grad_shift_two,
    )
    return (grad_input, terms)


def reorder(gradient, outer, inner):
    total_rows = gradient.shape[0]
    split_view = gradient.reshape(
        (outer, inner, total_rows // (outer * inner)) + gradient.shape[1:]
    )
    return jnp.swapaxes(split_view, 0, 1).reshape(gradient.shape)


def shards(
    tokens,
    positions,
    w_qkv,
    b_qkv,
    w_dense,
    b_dense,
    w_up,
    b_up,
    w_down,
    b_down,
    norm1_gain,
    norm1_shift,
    norm2_gain,
    norm2_shift,
    cotangent,
):
    section_no = lax.axis_index("section")
    gathered = (
        lax.all_gather(w_qkv, "wshard", axis=1, tiled=True),
        lax.all_gather(b_qkv, "wshard", axis=1, tiled=True),
        lax.all_gather(w_dense, "wshard", axis=1, tiled=True),
        lax.all_gather(b_dense, "wshard", axis=1, tiled=True),
        lax.all_gather(w_up, "wshard", axis=1, tiled=True),
        lax.all_gather(b_up, "wshard", axis=1, tiled=True),
        lax.all_gather(w_down, "wshard", axis=1, tiled=True),
        lax.all_gather(b_down, "wshard", axis=1, tiled=True),
        lax.all_gather(norm1_gain, "wshard", axis=1, tiled=True),
        lax.all_gather(norm1_shift, "wshard", axis=1, tiled=True),
        lax.all_gather(norm2_gain, "wshard", axis=1, tiled=True),
        lax.all_gather(norm2_shift, "wshard", axis=1, tiled=True),
    )
    weights = tuple((member[0] for member in gathered))
    batches = tokens.shape[0]
    tok_rows = tokens.shape[1]
    model_width = tokens.shape[2]
    length = positions.shape[1]
    groups = lax.axis_size("seq")
    slice_width = model_width // groups
    block_rows = min(512, length)
    heads_per = slice_width // HEAD
    saved = (
        jnp.zeros((batches + 1, tok_rows, model_width), jnp.float32),
        jnp.zeros((batches + 1, length, 3, 1, slice_width), jnp.bfloat16),
        jnp.zeros((batches + 1, length // block_rows, heads_per, block_rows), jnp.float32),
        jnp.zeros((batches + 1, tok_rows, model_width), jnp.bfloat16),
        jnp.zeros((batches + 1, tok_rows, FF), jnp.float32),
        jnp.zeros((batches + 1, tok_rows, model_width), jnp.bfloat16),
    )
    arrived = jnp.zeros((tok_rows, model_width), jnp.bfloat16)

    def forward_tick(moment, carried):
        arrived, saved = carried
        batch_no = moment - section_no
        active = (batch_no >= 0) & (batch_no < batches)
        target = jnp.where(active, batch_no, batches)
        chosen = jnp.clip(batch_no, 0, batches - 1)
        own_rows = lax.dynamic_index_in_dim(tokens, chosen, 0, keepdims=False)
        layer_in = jnp.where(section_no == 0, own_rows, arrived).astype(jnp.float32)
        places = lax.dynamic_index_in_dim(positions, chosen, 0, keepdims=False)
        result, stored = layer_forward(layer_in, places, weights)
        result_low = result.astype(jnp.bfloat16)
        fresh = (layer_in, stored[0], stored[1], stored[2], stored[3], result_low)
        saved = tuple(
            (
                lax.dynamic_update_index_in_dim(buffer, value_now, target, 0)
                for buffer, value_now in zip(saved, fresh)
            )
        )
        arrived = passed_along(result_low, "section", 1)
        return (arrived, saved)

    arrived, saved = lax.fori_loop(0, batches + 1, forward_tick, (arrived, saved))
    gathered_back = (
        lax.all_gather(w_qkv, "wshard", axis=1, tiled=True),
        lax.all_gather(b_qkv, "wshard", axis=1, tiled=True),
        lax.all_gather(w_dense, "wshard", axis=1, tiled=True),
        lax.all_gather(b_dense, "wshard", axis=1, tiled=True),
        lax.all_gather(w_up, "wshard", axis=1, tiled=True),
        lax.all_gather(b_up, "wshard", axis=1, tiled=True),
        lax.all_gather(w_down, "wshard", axis=1, tiled=True),
        lax.all_gather(b_down, "wshard", axis=1, tiled=True),
        lax.all_gather(norm1_gain, "wshard", axis=1, tiled=True),
        lax.all_gather(norm1_shift, "wshard", axis=1, tiled=True),
        lax.all_gather(norm2_gain, "wshard", axis=1, tiled=True),
        lax.all_gather(norm2_shift, "wshard", axis=1, tiled=True),
    )
    weights_back = tuple((member[0] for member in gathered_back))
    gradients = tuple((jnp.zeros(member.shape, jnp.float32) for member in weights_back))
    input_grads = jnp.zeros((batches + 1, tok_rows, model_width), jnp.float32)
    returned = jnp.zeros((tok_rows, model_width), jnp.bfloat16)

    def backward_tick(moment, carried):
        returned, gradients, input_grads = carried
        batch_no = moment - 1 + section_no
        active = (batch_no >= 0) & (batch_no < batches)
        target = jnp.where(active, batch_no, batches)
        chosen = jnp.clip(batch_no, 0, batches - 1)
        own_rows = lax.dynamic_index_in_dim(cotangent, chosen, 0, keepdims=False)
        incoming = jnp.where(section_no == 1, own_rows, returned)
        incoming = jnp.where(active, incoming, jnp.zeros_like(incoming))
        stored = tuple(
            (lax.dynamic_index_in_dim(buffer, chosen, 0, keepdims=False) for buffer in saved[:5])
        )
        places = lax.dynamic_index_in_dim(positions, chosen, 0, keepdims=False)
        grad_input, terms = layer_backward(stored[0], places, weights_back, stored[1:], incoming)
        gradients = tuple((running + term for running, term in zip(gradients, terms)))
        sent = grad_input.astype(jnp.bfloat16)
        kept_grad = jnp.where(section_no == 1, sent.astype(jnp.float32), grad_input)
        input_grads = lax.dynamic_update_index_in_dim(input_grads, kept_grad, target, 0)
        returned = passed_along(sent, "section", -1)
        return (returned, gradients, input_grads)

    returned, gradients, input_grads = lax.fori_loop(
        0, batches + 1, backward_tick, (returned, gradients, input_grads)
    )
    members = (
        gradients[0],
        gradients[1][: 2 * model_width],
        gradients[1][2 * model_width :],
        gradients[2],
        gradients[3],
        gradients[4],
        gradients[5],
        gradients[6],
        gradients[7],
        gradients[8],
        gradients[9],
        gradients[10],
        gradients[11],
    )
    shard_count = lax.axis_size("wshard")
    ordered = tuple((reorder(member, shard_count, groups) for member in members))
    summed = (
        lax.psum_scatter(ordered[0], ("seq", "wshard"), scatter_dimension=0, tiled=True),
        lax.psum_scatter(ordered[1], ("seq", "wshard"), scatter_dimension=0, tiled=True),
        lax.psum_scatter(ordered[2], ("seq", "wshard"), scatter_dimension=0, tiled=True),
        lax.psum_scatter(ordered[3], ("seq", "wshard"), scatter_dimension=0, tiled=True),
        lax.psum_scatter(ordered[4], ("seq", "wshard"), scatter_dimension=0, tiled=True),
        lax.psum_scatter(ordered[5], ("seq", "wshard"), scatter_dimension=0, tiled=True),
        lax.psum_scatter(ordered[6], ("seq", "wshard"), scatter_dimension=0, tiled=True),
        lax.psum_scatter(ordered[7], ("seq", "wshard"), scatter_dimension=0, tiled=True),
        lax.psum_scatter(ordered[8], ("seq", "wshard"), scatter_dimension=0, tiled=True),
        lax.psum_scatter(ordered[9], ("seq", "wshard"), scatter_dimension=0, tiled=True),
        lax.psum_scatter(ordered[10], ("seq", "wshard"), scatter_dimension=0, tiled=True),
        lax.psum_scatter(ordered[11], ("seq", "wshard"), scatter_dimension=0, tiled=True),
        lax.psum_scatter(ordered[12], ("seq", "wshard"), scatter_dimension=0, tiled=True),
    )
    summed = (
        lax.all_gather(summed[0].astype(jnp.bfloat16), "seq", axis=0, tiled=True).astype(
            jnp.float32
        ),
        lax.all_gather(summed[1].astype(jnp.bfloat16), "seq", axis=0, tiled=True).astype(
            jnp.float32
        ),
        lax.all_gather(summed[2].astype(jnp.bfloat16), "seq", axis=0, tiled=True).astype(
            jnp.float32
        ),
        lax.all_gather(summed[3].astype(jnp.bfloat16), "seq", axis=0, tiled=True).astype(
            jnp.float32
        ),
        lax.all_gather(summed[4].astype(jnp.bfloat16), "seq", axis=0, tiled=True).astype(
            jnp.float32
        ),
        lax.all_gather(summed[5].astype(jnp.bfloat16), "seq", axis=0, tiled=True).astype(
            jnp.float32
        ),
        lax.all_gather(summed[6].astype(jnp.bfloat16), "seq", axis=0, tiled=True).astype(
            jnp.float32
        ),
        lax.all_gather(summed[7].astype(jnp.bfloat16), "seq", axis=0, tiled=True).astype(
            jnp.float32
        ),
        lax.all_gather(summed[8].astype(jnp.bfloat16), "seq", axis=0, tiled=True).astype(
            jnp.float32
        ),
        lax.all_gather(summed[9].astype(jnp.bfloat16), "seq", axis=0, tiled=True).astype(
            jnp.float32
        ),
        lax.all_gather(summed[10].astype(jnp.bfloat16), "seq", axis=0, tiled=True).astype(
            jnp.float32
        ),
        lax.all_gather(summed[11].astype(jnp.bfloat16), "seq", axis=0, tiled=True).astype(
            jnp.float32
        ),
        lax.all_gather(summed[12].astype(jnp.bfloat16), "seq", axis=0, tiled=True).astype(
            jnp.float32
        ),
    )
    hidden = saved[5][:batches][None]
    in_grads = input_grads[:batches][None]
    return (
        hidden,
        in_grads,
        summed[0][None],
        summed[1][None],
        summed[2][None],
        summed[3][None],
        summed[4][None],
        summed[5][None],
        summed[6][None],
        summed[7][None],
        summed[8][None],
        summed[9][None],
        summed[10][None],
        summed[11][None],
        summed[12][None],
    )


def solution(mesh):
    in_specs = (
        P("wshard", "seq", None),
        P("wshard", None),
        P("section", "wshard", None),
        P("section", "wshard"),
        P("section", "wshard", None),
        P("section", "wshard"),
        P("section", "wshard", None),
        P("section", "wshard"),
        P("section", "wshard", None),
        P("section", "wshard"),
        P("section", "wshard"),
        P("section", "wshard"),
        P("section", "wshard"),
        P("section", "wshard"),
        P("wshard", "seq", None),
    )
    out_specs = (
        P("section", "wshard", "seq", None),
        P("section", "wshard", "seq", None),
        P("section", "wshard", None),
        P("section", "wshard"),
        P("section", "wshard"),
        P("section", "wshard", None),
        P("section", "wshard"),
        P("section", "wshard", None),
        P("section", "wshard"),
        P("section", "wshard", None),
        P("section", "wshard"),
        P("section", "wshard"),
        P("section", "wshard"),
        P("section", "wshard"),
        P("section", "wshard"),
    )
    return jax.shard_map(shards, mesh=mesh, in_specs=in_specs, out_specs=out_specs, check_vma=False)
```

profile of v0, /device:TPU:9, one launch (start us, length us, event | category | flops | bytes accessed | tf_op | source)
XLA Modules:
  0.0 2952.2 jit_solution(15208796267357596845)
XLA Ops:
  37.3 21.8 all_gather.86
  71.6 19.2 all_gather.89
  91.4 17.9 all_gather.90
  109.9 29.0 all_gather.92
  155.6 39.8 %all-gather.7.cloned.1.call-done = bf16[1,1024,3072]{2,1,0:T(8,128)(2,1)} async-done(((bf16[1,128,3072]{2,1,0:T(8,128)(2,1)}), bf16[1,1024,3072]{2,1,0:T(8,128)(2,1)}) %all-gather.7.cloned.1.call-update) | async-done | bytes 6291472 | tf_op jit(solution)/shard_map/all_gather | solution.py:303
  195.4 171.5 %all-gather.11.cloned.1.call-done = bf16[1,1024,4096]{2,1,0:T(8,128)(2,1)} async-done(((bf16[1,128,4096]{2,1,0:T(8,128)(2,1)}), bf16[1,1024,4096]{2,1,0:T(8,128)(2,1)}) %all-gather.11.cloned.1.call-update) | async-done | bytes 8388624 | tf_op jit(solution)/shard_map/all_gather | solution.py:307
  366.9 175.3 %all-gather.13.cloned.1.call-done = bf16[1,4096,1024]{2,1,0:T(8,128)(2,1)} async-done(((bf16[1,512,1024]{2,1,0:T(8,128)(2,1)}), bf16[1,4096,1024]{2,1,0:T(8,128)(2,1)}) %all-gather.13.cloned.1.call-update) | async-done | bytes 8388624 | tf_op jit(solution)/shard_map/all_gather | solution.py:309
  552.1 293.0 %while.161 = (s32[]{:T(128)}, bf16[128,1024]{1,0:T(8,128)(2,1)}, f32[3,128,1024]{2,1,0:T(8,128)}, bf16[3,1024,3,1,128]{4,1,2,3,0:T(8,128)(2,1)}, f32[3,2,2,512]{...) while((s32[]{:T(128)}, bf16[128,1024]{1,0:T(8,128)(2,1)}, ...), condition=%wide.region_7.8_spmd, body=%wide.region_0.7_spmd.sunk | while | flops 3544864256 | bytes 80419960 | solution.py:356
  594.9 20.3 while.164
  690.7 20.3 while.164
  788.9 20.3 while.164
  847.2 477.6 %while.163 = (s32[]{:T(128)}, bf16[128,1024]{1,0:T(8,128)(2,1)}, f32[1024,3072]{1,0:T(8,128)}, f32[3072]{0:T(1024)}, f32[1024,1024]{1,0:T(8,128)}, /*index=5*/f3...) while((s32[]{:T(128)}, bf16[128,1024]{1,0:T(8,128)(2,1)}, ...), condition=%wide.region_25.26_spmd.clone, body=%wide.region_8.25_spmd.clone.sunk | while | flops 7242771456 | bytes 387080352 | solution.py:397
  910.2 44.3 %while.165 = (s32[]{:T(128)}, f32[1024,2,64]{0,2,1:T(8,128)S(1)}, f32[1024,2,64]{0,2,1:T(8,128)}, f32[2,512,2,64]{1,0,3,2:T(2,128)}, s32[2]{0:T(128)S(1)}, /*ind...) while((s32[]{:T(128)}, f32[1024,2,64]{0,2,1:T(8,128)S(1)}, ...), condition=%wide.region_11.11_spmd.clone, body=%wide.region_9.10_spmd.clone.sunk | while | flops 689634816 | bytes 59283836 | solution.py:136
  1057.3 44.3 %while.165 = (s32[]{:T(128)}, f32[1024,2,64]{0,2,1:T(8,128)S(1)}, f32[1024,2,64]{0,2,1:T(8,128)}, f32[2,512,2,64]{1,0,3,2:T(2,128)}, s32[2]{0:T(128)S(1)}, /*ind...) while((s32[]{:T(128)}, f32[1024,2,64]{0,2,1:T(8,128)S(1)}, ...), condition=%wide.region_11.11_spmd.clone, body=%wide.region_9.10_spmd.clone.sunk | while | flops 689634816 | bytes 59283836 | solution.py:136
  1210.5 44.3 %while.165 = (s32[]{:T(128)}, f32[1024,2,64]{0,2,1:T(8,128)S(1)}, f32[1024,2,64]{0,2,1:T(8,128)}, f32[2,512,2,64]{1,0,3,2:T(2,128)}, s32[2]{0:T(128)S(1)}, /*ind...) while((s32[]{:T(128)}, f32[1024,2,64]{0,2,1:T(8,128)S(1)}, ...), condition=%wide.region_11.11_spmd.clone, body=%wide.region_9.10_spmd.clone.sunk | while | flops 689634816 | bytes 59283836 | solution.py:136
  1364.3 325.8 %reduce-scatter.9.cloned.1.call-done = f32[16,4096]{1,0:T(8,128)} async-done(((f32[1024,4096]{1,0:T(8,128)}), f32[16,4096]{1,0:T(8,128)}) %reduce-scatter.9.cloned.1.call-update) | async-done | bytes 262160 | tf_op jit(solution)/shard_map/reduce_scatter | solution.py:423
  1698.4 289.9 %all-reduce.26 = (bf16[2048]{0:T(1024)(128)(2,1)S(1)}, bf16[1024]{0:T(1024)(128)(2,1)S(1)}, bf16[1024]{0:T(1024)(128)(2,1)S(1)}, bf16[4096]{0:T(1024)(128)(2,1)S...) all-reduce(f32[2048]{0:T(1024)S(1)} %reshape.720, ...), channel_id=3, replica_groups=mesh['section'=2,'seq'=8,'wshard'=8] {'seq','wshard'}, use_global_device_ids=true, to_apply=%region_27.28.clone | all-reduce | flops 13312 | bytes 79872
  2011.8 16.5 reduce-scatter.7.cloned.1.call-done
  2029.1 28.0 all_gather.98
  2058.0 350.0 %reduce-scatter.5.cloned.1.call-done = f32[16,3072]{1,0:T(8,128)} async-done(((f32[1024,3072]{1,0:T(8,128)}), f32[16,3072]{1,0:T(8,128)}) %reduce-scatter.5.cloned.1.call-update) | async-done | bytes 196624 | tf_op jit(solution)/shard_map/reduce_scatter | solution.py:418
  2408.9 401.6 %reduce-scatter.11.cloned.1.call-done = f32[64,1024]{1,0:T(8,128)} async-done(((f32[4096,1024]{1,0:T(8,128)}), f32[64,1024]{1,0:T(8,128)}) %reduce-scatter.11.cloned.1.call-update) | async-done | bytes 262160 | tf_op jit(solution)/shard_map/reduce_scatter | solution.py:425
  2812.2 43.5 %all_gather.95 = bf16[128,3072]{1,0:T(8,128)(2,1)S(1)} all-gather(bf16[16,3072]{1,0:T(8,128)(2,1)S(1)} %convert_element_type.581), channel_id=1, replica_groups=mesh['section'=2,'seq'=8,'wshard'=8] {'seq'}, dimensions={0}, use_global_device_ids=true | all-gather | bytes 884736 | tf_op jit(solution)/shard_map/all_gather | solution.py:433
  2857.0 36.7 %all-gather.15.cloned.1.call-done = bf16[128,4096]{1,0:T(8,128)(2,1)} async-done(((bf16[16,4096]{1,0:T(8,128)(2,1)}), bf16[128,4096]{1,0:T(8,128)(2,1)}) %all-gather.15.cloned.1.call-update) | async-done | bytes 1048592 | tf_op jit(solution)/shard_map/all_gather | solution.py:448
  2896.5 46.0 %all-gather.17.cloned.1.call-done = bf16[512,1024]{1,0:T(8,128)(2,1)} async-done(((bf16[64,1024]{1,0:T(8,128)(2,1)}), bf16[512,1024]{1,0:T(8,128)(2,1)}) %all-gather.17.cloned.1.call-update) | async-done | bytes 1048592 | tf_op jit(solution)/shard_map/all_gather | solution.py:454
  (1039 shorter events, 868.8 us)
Async XLA Ops:
  7.3 148.3 %all-gather.9.cloned.1.call-start = ((), (), s32[]{:S(2)}) async-start(), calls=%async_computation.9 | async-start | bytes 2359296 | tf_op jit(solution)/shard_map/all_gather | solution.py:305
  8.0 187.4 %all-gather.7.cloned.1.call-start = ((), (), s32[]{:S(2)}) async-start(), calls=%async_computation.8 | async-start | bytes 7077888 | tf_op jit(solution)/shard_map/all_gather | solution.py:303
  8.7 358.2 %all-gather.11.cloned.1.call-start = ((), (), s32[]{:S(2)}) async-start(), calls=%async_computation.10 | async-start | bytes 9437184 | tf_op jit(solution)/shard_map/all_gather | solution.py:307
  9.5 532.7 %all-gather.13.cloned.1.call-start = ((), (), s32[]{:S(2)}) async-start(), calls=%async_computation.11 | async-start | bytes 9437184 | tf_op jit(solution)/shard_map/all_gather | solution.py:309
  10.1 1680.0 %reduce-scatter.9.cloned.1.call-start = ((), (), s32[]{:S(2)}) async-start(), calls=%async_computation.14 | async-start | bytes 17039360 | tf_op jit(solution)/shard_map/reduce_scatter | solution.py:423
  561.2 19.4 all-to-all-start.2
  657.7 18.8 all-to-all-start.2
  720.6 15.2 all-to-all-start.3
  755.8 18.9 all-to-all-start.2
  818.8 15.2 all-to-all-start.3
  869.5 39.7 %all-to-all-start = ((bf16[128,8,128]{2,0,1:T(8,128)(2,1)}), bf16[128,8,128]{2,0,1:T(8,128)(2,1)S(1)}, u32[]{:S(2)}, u32[]{:S(2)}) async-start(bf16[128,8,128]{2,0,1:T(8,128)(2,1)} %bitcast.415), calls=%async_computation | async-start | bytes 524288 | tf_op jit(solution)/shard_map/while/body/eval_jaxpr/all_to_all | solution.py:235
  957.9 20.3 all-to-all-start.1
  988.0 19.7 collective-permute-start
  1016.1 40.1 %all-to-all-start = ((bf16[128,8,128]{2,0,1:T(8,128)(2,1)}), bf16[128,8,128]{2,0,1:T(8,128)(2,1)S(1)}, u32[]{:S(2)}, u32[]{:S(2)}) async-start(bf16[128,8,128]{2,0,1:T(8,128)(2,1)} %bitcast.415), calls=%async_computation | async-start | bytes 524288 | tf_op jit(solution)/shard_map/while/body/eval_jaxpr/all_to_all | solution.py:235
  1105.1 24.4 all-to-all-start.1
  1139.3 21.2 collective-permute-start
  1168.9 40.5 %all-to-all-start = ((bf16[128,8,128]{2,0,1:T(8,128)(2,1)}), bf16[128,8,128]{2,0,1:T(8,128)(2,1)S(1)}, u32[]{:S(2)}, u32[]{:S(2)}) async-start(bf16[128,8,128]{2,0,1:T(8,128)(2,1)} %bitcast.415), calls=%async_computation | async-start | bytes 524288 | tf_op jit(solution)/shard_map/while/body/eval_jaxpr/all_to_all | solution.py:235
  1258.3 24.4 all-to-all-start.1
  1292.5 21.3 collective-permute-start
  1336.5 691.8 %reduce-scatter.7.cloned.1.call-start = ((), (), s32[]{:S(2)}) async-start(), calls=%async_computation.13 | async-start | bytes 4259840 | tf_op jit(solution)/shard_map/reduce_scatter | solution.py:421
  1341.3 1066.7 %reduce-scatter.5.cloned.1.call-start = ((), (), s32[]{:S(2)}) async-start(), calls=%async_computation.12 | async-start | bytes 12779520 | tf_op jit(solution)/shard_map/reduce_scatter | solution.py:418
  1352.1 1458.4 %reduce-scatter.11.cloned.1.call-start = ((), (), s32[]{:S(2)}) async-start(), calls=%async_computation.16 | async-start | bytes 17039360 | tf_op jit(solution)/shard_map/reduce_scatter | solution.py:425
  1364.2 1529.5 %all-gather.15.cloned.1.call-start = ((), (), s32[]{:S(2)}) async-start(), calls=%async_computation.15 | async-start | bytes 1179648 | tf_op jit(solution)/shard_map/all_gather | solution.py:448
  1691.7 1250.7 %all-gather.17.cloned.1.call-start = ((), (), s32[]{:S(2)}) async-start(), calls=%async_computation.17 | async-start | bytes 1179648 | tf_op jit(solution)/shard_map/all_gather | solution.py:454
  (193 other events, 6112.7 us)
Sparse Core Ops, SparseCore 0:
  9.7 52.6 all-gather.8
  64.1 131.2 all-gather.6
  197.0 169.8 all-gather.10
  368.4 173.7 all-gather.12
  1336.6 353.3 reduce-scatter.8
  1692.3 335.9 reduce-scatter.6
  2030.8 377.1 reduce-scatter.4
  2410.5 399.9 reduce-scatter.10
  2813.7 79.9 all-gather.14
  2896.1 46.2 all-gather.16
where the time goes:
time: 2960 us; the launch traced here: 2950 us
  waiting for transfers between devices  1600 us (54%)
  blocking collectives  519 us (18%)
  matrix products  326 us (11%)
  local copies, waits for them, and re-layouts  231 us (8%)
  other arithmetic  120 us (4%)
  starting transfers between devices  85.1 us (3%)
  loops' own time  52.3 us (2%)
    reduce_scatter x1, waiting for transfers between devices, shards(): lax.psum_scatter(ordered[7], ('seq', 'wshard'), scatter_dimension=0, tile...  402 us
    reduce_scatter x1, waiting for transfers between devices, shards(): lax.psum_scatter(ordered[0], ('seq', 'wshard'), scatter_dimension=0, tile...  350 us
    reduce_scatter x1, waiting for transfers between devices, shards(): lax.psum_scatter(ordered[5], ('seq', 'wshard'), scatter_dimension=0, tile...  326 us
    unnamed x2, blocking collectives  306 us
    all_gather x1, waiting for transfers between devices, shards(): lax.all_gather(w_down, 'wshard', axis=1, tiled=True)  175 us
    all_gather x1, waiting for transfers between devices, shards(): lax.all_gather(w_up, 'wshard', axis=1, tiled=True)  172 us
    dot_general x12, matrix products, product_left(): lax.dot_general(left, right, (((0,), (0,)), ((), ())), preferred_element_...  101 us
    dot_general x12, matrix products, product(): return jnp.dot(left, right, preferred_element_type=jnp.float32)  69.4 us
  transfers between devices with their start and end apart: 28, of which 18 were waited for; matrix products, arithmetic and copies ran while one was open for 10% of the time, Pallas kernels for 0%

commit v1 on v0

v1 whole, which is shorter than its diff:
```python
import math

import jax
import jax.numpy as jnp
from jax import lax
from jax.experimental import pallas as pl
from jax.experimental.pallas import tpu as pltpu
from jax.sharding import PartitionSpec as P

HEAD = 64
ROT = 16
NORM_EPS = 1e-05
BF = jnp.bfloat16
F32 = jnp.float32
AXES = ("section", "seq", "wshard")
LENGTH = 1024
WIDTH = 1024
QROWS = 256
UNIT = 64


def place_of(index):
    core, seq, shard = index // 64, (index // 8) % 8, index % 8
    return core, seq // 2, seq % 2, shard // 2, shard % 2


def index_of(core, x, zh, y, zl):
    return core * 64 + (2 * x + zh) * 8 + 2 * y + zl


def route(block, target):
    pairs = [(i, index_of(*target(*place_of(i)))) for i in range(128)]
    return lax.ppermute(block, AXES, pairs)


def along_x(block, step):
    return route(block, lambda c, x, zh, y, zl: (c, (x + step) % 4, zh, y, zl))


def along_y(block, step):
    return route(block, lambda c, x, zh, y, zl: (c, x, zh, (y + step) % 4, zl))


def across_cores(block):
    return route(block, lambda c, x, zh, y, zl: (1 - c, x, zh, y, zl))


def across_high(block):
    return route(block, lambda c, x, zh, y, zl: (c, x, 1 - zh, y, zl))


def across_low(block):
    return route(block, lambda c, x, zh, y, zl: (c, x, zh, y, 1 - zl))


def transposed(block):
    return route(block, lambda c, x, zh, y, zl: (zl, y, zh, x, c))


def pick(array, index, axis=0):
    return lax.dynamic_index_in_dim(array, index, axis, keepdims=False)


def dot(left, right):
    return jnp.dot(left, right, preferred_element_type=F32)


def dot_left(left, right):
    return lax.dot_general(left, right, (((0,), (0,)), ((), ())), preferred_element_type=F32)


def dot_right(left, right):
    return lax.dot_general(left, right, (((1,), (1,)), ((), ())), preferred_element_type=F32)


def head_lanes(rows, head):
    lanes = lax.broadcasted_iota(jnp.int32, (rows, 2 * HEAD), 1)
    return (lanes >= head * HEAD) & (lanes < (head + 1) * HEAD)


def turned(values, cosine, sine_low, sine_high):
    return (
        values * cosine
        + pltpu.roll(values, ROT // 2, 1) * sine_low
        + pltpu.roll(values, 2 * HEAD - ROT // 2, 1) * sine_high
    )


def masked_scores(query, keys, begin, block, reach):
    scores = dot_right(query, keys)
    rows = block * QROWS + lax.broadcasted_iota(jnp.int32, (QROWS, reach), 0)
    columns = lax.broadcasted_iota(jnp.int32, (QROWS, reach), 1)
    seen = (columns <= rows) & (columns >= begin)
    return jnp.where(seen, scores, -1e30)


def attend_kernel(
    where_ref, proj_ref, cos_ref, low_ref, high_ref, begin_ref, mixed_ref, q_ref, k_ref, v_ref, o_ref, lse_ref
):
    for m in range(LENGTH // UNIT):
        here = pl.ds(m * UNIT, UNIT)
        there = pl.ds(pl.multiple_of(where_ref[m] * UNIT, UNIT), UNIT)
        proj = proj_ref[there, :]
        cosine, low, high = cos_ref[here, :], low_ref[here, :], high_ref[here, :]
        query = turned(proj[:, :128].astype(F32), cosine, low, high)
        q_ref[here, :] = (query.astype(BF).astype(F32) * (1.0 / math.sqrt(HEAD))).astype(BF)
        k_ref[here, :] = turned(proj[:, 128:256].astype(F32), cosine, low, high).astype(BF)
        v_ref[here, :] = proj[:, 256:]
    for block in range(LENGTH // QROWS):
        rows = pl.ds(block * QROWS, QROWS)
        reach = (block + 1) * QROWS
        keys, values = k_ref[:reach, :], v_ref[:reach, :]
        query = q_ref[rows, :]
        begin = begin_ref[rows, :1]
        outs, logs = [], []
        for head in range(2):
            own = head_lanes(QROWS, head)
            scores = masked_scores(jnp.where(own, query, jnp.zeros_like(query)), keys, begin, block, reach)
            highest = jnp.max(scores, axis=-1, keepdims=True)
            exponent = jnp.exp(scores - highest)
            total = jnp.sum(exponent, axis=-1, keepdims=True)
            probs = (exponent * (1.0 / total)).astype(BF)
            outs.append(dot(probs, values))
            logs.append(highest + jnp.log(total))
        first = head_lanes(QROWS, 0)
        o_ref[rows, :] = jnp.where(first, outs[0], outs[1]).astype(BF)
        lse_ref[rows, :] = jnp.where(first, logs[0], logs[1])
    for m in range(LENGTH // UNIT):
        there = pl.ds(pl.multiple_of(where_ref[m] * UNIT, UNIT), UNIT)
        mixed_ref[there, :] = o_ref[pl.ds(m * UNIT, UNIT), :]


def attend_back_kernel(
    where_ref, grad_ref, cos_ref, low_ref, high_ref, begin_ref, q_ref, k_ref, v_ref, o_ref, lse_ref,
    out_ref, do_ref, dq_ref, dk_ref, dv_ref,
):
    for m in range(LENGTH // UNIT):
        there = pl.ds(pl.multiple_of(where_ref[m] * UNIT, UNIT), UNIT)
        do_ref[pl.ds(m * UNIT, UNIT), :] = grad_ref[there, :]
    for block in reversed(range(LENGTH // QROWS)):
        rows = pl.ds(block * QROWS, QROWS)
        reach = (block + 1) * QROWS
        keys, values = k_ref[:reach, :], v_ref[:reach, :]
        query, upstream, kept = q_ref[rows, :], do_ref[rows, :], o_ref[rows, :].astype(F32)
        begin = begin_ref[rows, :1]
        grads = []
        for head in range(2):
            own = head_lanes(QROWS, head)
            query_own = jnp.where(own, query, jnp.zeros_like(query))
            up_own = jnp.where(own, upstream, jnp.zeros_like(upstream))
            scores = masked_scores(query_own, keys, begin, block, reach)
            probs = jnp.exp(scores - lse_ref[rows, head * HEAD : head * HEAD + 1])
            centre = jnp.sum(up_own.astype(F32) * kept, axis=-1, keepdims=True)
            moved = (probs * (dot_right(up_own, values) - centre)).astype(BF)
            grads.append(dot(moved, keys))
            dk = dot_left(moved, query_own)
            dv = dot_left(probs.astype(BF), up_own)
            if block == LENGTH // QROWS - 1 and head == 0:
                dk_ref[...] = dk
                dv_ref[...] = dv
            else:
                dk_ref[:reach, :] += dk
                dv_ref[:reach, :] += dv
        first = head_lanes(QROWS, 0)
        dq_ref[rows, :] = jnp.where(first, grads[0], grads[1]) * (1.0 / math.sqrt(HEAD))
    for m in range(LENGTH // UNIT):
        here = pl.ds(m * UNIT, UNIT)
        there = pl.ds(pl.multiple_of(where_ref[m] * UNIT, UNIT), UNIT)
        cosine, low, high = cos_ref[here, :], -low_ref[here, :], -high_ref[here, :]
        out_ref[there, :128] = turned(dq_ref[here, :], cosine, low, high).astype(BF)
        out_ref[there, 128:256] = turned(dk_ref[here, :], cosine, low, high).astype(BF)
        out_ref[there, 256:] = dv_ref[here, :].astype(BF)


def vmem():
    return pl.BlockSpec(memory_space=pltpu.VMEM)


def attend(where, proj, tables):
    small = jax.ShapeDtypeStruct((LENGTH, 128), BF)
    return pl.pallas_call(
        attend_kernel,
        out_shape=[small, small, small, small, small, jax.ShapeDtypeStruct((LENGTH, 128), F32)],
        in_specs=[pl.BlockSpec(memory_space=pltpu.SMEM)] + [vmem()] * 5,
        out_specs=[vmem()] * 6,
        compiler_params=pltpu.CompilerParams(vmem_limit_bytes=40 * 1024 * 1024),
        cost_estimate=pl.CostEstimate(flops=2_000_000_000, bytes_accessed=6_000_000, transcendentals=1_500_000),
    )(where, proj, *tables)


def attend_back(where, grad, tables, kept):
    return pl.pallas_call(
        attend_back_kernel,
        out_shape=jax.ShapeDtypeStruct((LENGTH, 384), BF),
        in_specs=[pl.BlockSpec(memory_space=pltpu.SMEM)] + [vmem()] * 10,
        out_specs=vmem(),
        scratch_shapes=[pltpu.VMEM((LENGTH, 128), BF)] + [pltpu.VMEM((LENGTH, 128), F32)] * 3,
        compiler_params=pltpu.CompilerParams(vmem_limit_bytes=40 * 1024 * 1024),
        cost_estimate=pl.CostEstimate(flops=5_000_000_000, bytes_accessed=6_000_000, transcendentals=1_500_000),
    )(where, grad, *tables, *kept)


def rotary_tables(places):
    half = ROT // 2
    frequency = 1.0 / 10000.0 ** (jnp.arange(half).astype(F32) * 2.0 / ROT)
    angles = places.astype(F32)[:, None] * frequency[None, :]
    cosine, sine = jnp.cos(angles), jnp.sin(angles)
    rest = HEAD - ROT
    nought = jnp.zeros((LENGTH, half), F32)
    blank = jnp.zeros((LENGTH, rest), F32)
    cos_head = jnp.concatenate([cosine, cosine, jnp.ones((LENGTH, rest), F32)], axis=1)
    low_head = jnp.concatenate([nought, sine, blank], axis=1)
    high_head = jnp.concatenate([-sine, nought, blank], axis=1)
    begin = jnp.arange(LENGTH, dtype=jnp.int32) - places
    return (
        jnp.concatenate([cos_head, cos_head], axis=1),
        jnp.concatenate([low_head, low_head], axis=1),
        jnp.concatenate([high_head, high_head], axis=1),
        jnp.broadcast_to(begin[:, None], (LENGTH, 128)),
    )


def gather_rows(mine):
    own = [mine] + [along_x(mine, -r) for r in (1, 2, 3)]
    other = [across_cores(block) for block in own]
    return jnp.concatenate([rows for pair in zip(own, other) for rows in pair], axis=0), other[0]


def scatter_sum(partial):
    blocks = partial.reshape(4, 2, LENGTH // 8, WIDTH)
    total = None
    for r in (2, 1, 3, 0):
        joined = blocks[r, 0].astype(F32) + across_cores(blocks[r, 1]).astype(F32)
        if r:
            joined = along_x(joined.astype(BF), r).astype(F32)
        total = joined if total is None else total + joined
    return total


def normalized(rows):
    values = rows.astype(F32)
    centre = jnp.mean(values, axis=-1, keepdims=True)
    centred = values - centre
    spread = jnp.mean(centred * centred, axis=-1, keepdims=True)
    scale = lax.rsqrt(spread + NORM_EPS)
    return centred * scale, scale


def norm_back(grad, rows):
    unit, scale = normalized(rows)
    mean_grad = jnp.mean(grad, axis=-1, keepdims=True)
    mean_both = jnp.mean(grad * unit, axis=-1, keepdims=True)
    return scale * (grad - mean_grad - unit * mean_both)


def gelu(values):
    return 0.5 * values * (1.0 + lax.erf(values * (1.0 / math.sqrt(2.0))))


def gelu_slope(values):
    phi = jnp.exp(-0.5 * values * values) * (1.0 / math.sqrt(2.0 * math.pi))
    return 0.5 * (1.0 + lax.erf(values * (1.0 / math.sqrt(2.0)))) + values * phi


def shards(
    tokens, positions, w_qkv, b_qkv, w_dense, b_dense, w_up, b_up, w_down, b_down,
    norm1_gain, norm1_shift, norm2_gain, norm2_shift, cotangent,
):
    core = lax.axis_index("section")
    seq = lax.axis_index("seq")
    shard = lax.axis_index("wshard")
    x, zh = seq // 2, seq % 2
    y, zl = shard // 2, shard % 2
    part = 2 * x + core

    def own_rows(array):
        own = lax.dynamic_slice_in_dim(pick(array, zh), core * UNIT, UNIT, 0)
        lent = lax.dynamic_slice_in_dim(pick(array, 1 - zh), core * UNIT, UNIT, 0)
        return jnp.concatenate([own, across_high(lent)], axis=0)

    unit_no = jnp.arange(16, dtype=jnp.int32)
    where = (
        ((unit_no // 4 - x) % 4) * 4
        + jnp.bitwise_xor(unit_no % 2, core) * 2
        + jnp.bitwise_xor((unit_no // 2) % 2, zh)
    ).astype(jnp.int32)
    tables = rotary_tables(pick(positions, zh))

    def both_layers(for_self, for_other):
        other = across_cores(for_other)
        return jnp.where(core == 0, for_self, other), jnp.where(core == 0, other, for_self)

    def sliced(which):
        qkv = pick(w_qkv[0].reshape(128, 3, 8, 128), which, 2).reshape(128, 384)
        up = pick(w_up[0].reshape(128, 8, 8, 64), which, 2).reshape(128, 512)
        down = pick(w_down[0].reshape(8, 64, 1024), which, 0)
        return qkv, up, down

    mine, theirs = sliced(part), sliced(2 * x + 1 - core)
    qkv_rows = both_layers(mine[0], theirs[0])
    up_rows = both_layers(mine[1], theirs[1])
    down_rows = both_layers(mine[2], theirs[2])
    dense_rows = both_layers(w_dense[0], w_dense[0])
    vector = jnp.concatenate(
        [b_qkv[0], b_up[0], b_dense[0], b_down[0], norm1_gain[0], norm1_shift[0], norm2_gain[0], norm2_shift[0]]
    )
    vectors = both_layers(vector, vector)

    def gathered(block):
        return lax.all_gather(block, "wshard", axis=0, tiled=True)

    layers = []
    for layer in range(2):
        qkv = gathered(qkv_rows[layer])
        up = gathered(up_rows[layer])
        down = gathered(down_rows[layer])
        dense = transposed(dense_rows[layer])
        small = lax.all_gather(vectors[layer], "wshard", axis=0, tiled=False).astype(F32)
        bias_qkv = pick(small[:, :384].reshape(3, 8, 128), part, 1).reshape(384)
        bias_up = pick(small[:, 384:896].reshape(8, 8, 64), part, 1).reshape(512)
        bias_out = small[:, 896:1024].reshape(-1) + small[:, 1024:1152].reshape(-1)
        gain_one, shift_one, gain_two, shift_two = (
            small[:, 1152 + 128 * i : 1280 + 128 * i].reshape(-1) for i in range(4)
        )
        wide = jnp.concatenate(
            [
                (gain_one[:, None] * qkv.astype(F32)).astype(BF),
                (gain_two[:, None] * up.astype(F32)).astype(BF),
            ],
            axis=1,
        )
        bias = jnp.concatenate(
            [
                bias_qkv + jnp.sum(shift_one[:, None] * qkv.astype(F32), axis=0),
                bias_up + jnp.sum(shift_two[:, None] * up.astype(F32), axis=0),
            ]
        )
        layers.append((wide, bias, jnp.concatenate([down, dense], axis=0), bias_out))

    def forward(own, weights):
        wide, bias, out_weights, bias_out = weights
        rows, beside = gather_rows(own)
        unit = normalized(rows)[0].astype(BF)
        product = dot(unit, wide) + bias[None, :]
        proj, middle = product[:, :384].astype(BF), product[:, 384:]
        active = gelu(middle).astype(BF)
        mixed, *kept = attend(where, proj, tables)
        ahead = jnp.concatenate([active, mixed], axis=1)
        result = own.astype(F32) + scatter_sum(dot(ahead, out_weights).astype(BF)) + bias_out[None, :]
        return result.astype(BF), (unit, middle, ahead, kept, beside)

    def backward(own, own_input, weights, stored):
        wide, bias, out_weights, bias_out = weights
        unit, middle, ahead, kept, _ = stored
        rows, beside = gather_rows(own)
        pulled = dot_right(rows, out_weights)
        grad_middle = (pulled[:, :512] * gelu_slope(middle)).astype(BF)
        grad_proj = attend_back(where, pulled[:, 512:].astype(BF), tables, kept)
        grads = jnp.concatenate([grad_proj, grad_middle], axis=1)
        grad_unit = scatter_sum(dot_right(grads, wide).astype(BF))
        grad_input = own.astype(F32) + norm_back(grad_unit, own_input)
        out_terms = dot_left(ahead, rows).astype(BF)
        wide_terms = dot_left(unit, grads).astype(BF)
        bias_terms = jnp.concatenate(
            [
                jnp.sum(grads.astype(F32), axis=0),
                jnp.sum(lax.dynamic_slice_in_dim(rows, part * 128, 128, 1).astype(F32), axis=0),
            ]
        )
        return grad_input, (wide_terms, out_terms, bias_terms), beside

    def reduced(terms):
        wide_terms, out_terms, bias_terms = terms
        down = out_terms[:512].reshape(4, 2, 64, 1024)
        down = jnp.concatenate([down[..., :512], down[..., 512:]], axis=2)
        dense = out_terms[512:].reshape(128, 4, 2, 128).transpose(1, 2, 0, 3)
        pieces = jnp.concatenate([wide_terms.reshape(4, 2, 128, 896), down, dense], axis=3)
        tail = jnp.pad(bias_terms.astype(BF)[None, :], ((0, 15), (0, 512)))
        pieces = jnp.concatenate([pieces, jnp.broadcast_to(tail, (4, 2) + tail.shape)], axis=2)
        near = pick(pieces, zl, 1).astype(F32) + across_low(pick(pieces, 1 - zl, 1)).astype(F32)
        near = near.astype(BF)
        total = pick(near, y).astype(F32)
        for step in (1, 2, 3):
            total = total + along_y(pick(near, (y + step) % 4), step).astype(F32)
        total = total.astype(BF)
        total = (total.astype(F32) + across_high(total).astype(F32)).astype(BF)
        dense = transposed(total[:128, 1408:])
        return jnp.concatenate([total[:, :1408], jnp.pad(dense, ((0, 16), (0, 0)))], axis=1)

    def collected(first, second):
        rounds = []
        for block in (first, second):
            rounds.append(jnp.stack([block] + [along_x(block, -r) for r in (1, 2, 3)], axis=0))
        kept = jnp.where(core == 0, rounds[0], rounds[1])
        sent = across_cores(jnp.where(core == 0, rounds[1], rounds[0]))
        pair = jnp.stack([jnp.where(core == 0, kept, sent), jnp.where(core == 0, sent, kept)], axis=1)
        return jnp.roll(pair, x, axis=0).reshape(8, 144, 1536).astype(F32)

    def placed(own, beside, keeper):
        low = jnp.where(core == 0, own, beside)
        high = jnp.where(core == 0, beside, own)
        local = jnp.concatenate([low[:UNIT], high[:UNIT]], axis=0)
        lent = across_high(jnp.concatenate([low[UNIT:], high[UNIT:]], axis=0))
        return jnp.stack([jnp.where(zh == 0, local, lent), jnp.where(zh == 0, lent, local)], axis=0)

    own_tokens = own_rows(tokens)
    own_cotangent = own_rows(cotangent)
    hidden_one, stored_one = forward(own_tokens, layers[0])
    hidden_two, stored_two = forward(hidden_one, layers[1])
    grad_two, terms_two, _ = backward(own_cotangent, hidden_one, layers[1], stored_two)
    grad_mid = grad_two.astype(BF)
    grad_one, terms_one, grad_beside = backward(grad_mid, own_tokens, layers[0], stored_one)
    sums_two = reduced(terms_two)
    sums_one = reduced(terms_one)
    sums = collected(sums_one, sums_two)

    hidden = jnp.where(
        core == 0,
        placed(hidden_one, stored_two[4], 0),
        placed(hidden_two, across_cores(hidden_two), 1),
    )
    grad_low = grad_one.astype(BF)
    in_grads = jnp.where(
        core == 0,
        placed(grad_low, across_cores(grad_low), 0),
        placed(grad_mid, grad_beside, 1),
    ).astype(F32)

    gain_one, shift_one = norm1_gain[0].astype(F32), norm1_shift[0].astype(F32)
    gain_two, shift_two = norm2_gain[0].astype(F32), norm2_shift[0].astype(F32)
    raw_qkv = sums[:, :128, :384].reshape(8, 128, 3, 128).transpose(1, 2, 0, 3).reshape(128, 3072)
    raw_up = sums[:, :128, 384:896].reshape(8, 128, 8, 64).transpose(1, 2, 0, 3).reshape(128, 4096)
    down = sums[:, :128, 896:1408].reshape(8, 2, 64, 512).transpose(0, 2, 1, 3).reshape(512, 1024)
    dense = sums[:, :128, 1408:].transpose(1, 0, 2).reshape(128, 1024)
    sum_qkv = sums[:, 128, :384].reshape(8, 3, 128).transpose(1, 0, 2).reshape(3072)
    sum_up = sums[:, 128, 384:896].reshape(8, 8, 64).transpose(1, 0, 2).reshape(4096)
    sum_out = sums[:, 128, 896:1024].reshape(1024)
    grad_w_qkv = gain_one[:, None] * raw_qkv + shift_one[:, None] * sum_qkv[None, :]
    grad_w_up = gain_two[:, None] * raw_up + shift_two[:, None] * sum_up[None, :]
    qkv_wide, up_wide = w_qkv[0].astype(F32), w_up[0].astype(F32)
    grad_b_out = lax.dynamic_slice_in_dim(sum_out, 128 * shard, 128, 0)
    outs = (
        hidden,
        in_grads,
        grad_w_qkv,
        lax.dynamic_slice_in_dim(sum_qkv, 256 * shard, 256, 0),
        lax.dynamic_slice_in_dim(sum_qkv, 2048 + 128 * shard, 128, 0),
        dense,
        grad_b_out,
        grad_w_up,
        lax.dynamic_slice_in_dim(sum_up, 512 * shard, 512, 0),
        down,
        grad_b_out,
        jnp.sum(qkv_wide * raw_qkv, axis=1),
        jnp.sum(qkv_wide * sum_qkv[None, :], axis=1),
        jnp.sum(up_wide * raw_up, axis=1),
        jnp.sum(up_wide * sum_up[None, :], axis=1),
    )
    return tuple(out[None] for out in outs)


def solution(mesh):
    rows = P("section", "wshard", None)
    vector = P("section", "wshard")
    in_specs = (
        P("wshard", "seq", None),
        P("wshard", None),
        rows, vector, rows, vector, rows, vector, rows, vector, vector, vector, vector, vector,
        P("wshard", "seq", None),
    )
    out_specs = (
        P("section", "wshard", "seq", None),
        P("section", "wshard", "seq", None),
        rows, vector, vector, rows, vector, rows, vector, rows, vector, vector, vector, vector, vector,
    )
    return jax.shard_map(shards, mesh=mesh, in_specs=in_specs, out_specs=out_specs, check_vma=False)
```

time: 2960 us -> 604 us (0.20)
  waiting for transfers between devices: 1600 us -> 160 us
  blocking collectives: 519 us -> 101 us
  matrix products: 326 us -> 27.8 us
  local copies, waits for them, and re-layouts: 231 us -> 89.5 us
  other arithmetic: 120 us -> 61.2 us
  loops' own time: 52.3 us -> 0 us
  starting transfers between devices: 85.1 us -> 115 us
    reduce_scatter x4 -> x0, waiting for transfers between devices: 1090 us -> none  [the longest x1 402 us: shards(): lax.psum_scatter(ordered[7], ('seq', 'wshard'), scatter_dimension=0, tile...]
    all_gather x6 -> x4, waiting for transfers between devices: 469 us -> 0.03 us  [gathered(): return lax.all_gather(block, 'wshard', axis=0, tiled=True)]
    unnamed x2 -> x0, blocking collectives: 306 us -> none
    dot_general x78 -> x12, matrix products: 326 us -> 27.8 us  [the longest x4 11.1 us: dot_left(): lax.dot_general(left, right, (((0,), (0,)), ((), ())), preferred_element_...]
    ppermute x6 -> x90, waiting for transfers between devices: 3.33 us -> 160 us  [route(): return lax.ppermute(block, AXES, pairs)]
    all_gather x10 -> x4, blocking collectives: 213 us -> 101 us  [the longest x2 56.3 us: gathered(): return lax.all_gather(block, 'wshard', axis=0, tiled=True)]
    ppermute x6 -> x90, starting transfers between devices: 16.6 us -> 115 us  [route(): return lax.ppermute(block, AXES, pairs)]
    all_to_all x12 -> x0, starting transfers between devices: 68.1 us -> none  [the longest x3 20.1 us: layer_forward(): lax.all_to_all(projected.reshape(tok_rows, 3, groups, -1), 'seq', split_a...]
  transfers between devices with their start and end apart: 28 -> 94, of which waited for: 18 -> 27; matrix products, arithmetic and copies ran while one was open for 10% -> 19% of each run, Pallas kernels for 0% -> 2%
where the time goes in v1:
time: 604 us; the launch traced here: 593 us
  waiting for transfers between devices  160 us (26%)
  starting transfers between devices  115 us (19%)
  blocking collectives  101 us (17%)
  local copies, waits for them, and re-layouts  89.5 us (15%)
  other arithmetic  61.2 us (10%)
  matrix products  27.8 us (5%)
  Pallas kernels  22.5 us (4%)
  between operations  16.3 us (3%)
    ppermute x90, waiting for transfers between devices, route(): return lax.ppermute(block, AXES, pairs)  160 us
    ppermute x90, starting transfers between devices, route(): return lax.ppermute(block, AXES, pairs)  115 us
    all_gather x2, blocking collectives, gathered(): return lax.all_gather(block, 'wshard', axis=0, tiled=True)  56.3 us
    all_gather x2, blocking collectives, shards(): lax.all_gather(vectors[layer], 'wshard', axis=0, tiled=False).astype(F32)  44.3 us
    unnamed x259, local copies, waits for them, and re-layouts  43 us
  transfers between devices with their start and end apart: 94, of which 27 were waited for; matrix products, arithmetic and copies ran while one was open for 19% of the time, Pallas kernels for 2%

profile of v1, /device:TPU:9, one launch (start us, length us, event | category | flops | bytes accessed | tf_op | source)
XLA Modules:
  0.0 593.3 jit_solution(3215827117344921411)
XLA Ops:
  45.3 20.7 %all-gather.2 = bf16[8,1,1664]{2,1,0:T(2,128)(2,1)S(1)} all-gather(bf16[1,1,1664]{2,1,0:T(2,128)(2,1)S(1)} %reshape.707), channel_id=2, replica_groups=mesh['section'=2,'seq'=8,'wshard'=8] {'wshard'}, dimensions={0}, use_global_device_ids=true | all-gather | bytes 29952 | tf_op jit(solution)/shard_map/all_gather | solution.py:318
  66.1 23.6 %all-gather.3 = bf16[8,1,1664]{2,1,0:T(2,128)(2,1)S(1)} all-gather(bf16[1,1,1664]{2,1,0:T(2,128)(2,1)S(1)} %reshape.709), channel_id=3, replica_groups=mesh['section'=2,'seq'=8,'wshard'=8] {'wshard'}, dimensions={0}, use_global_device_ids=true | all-gather | bytes 29952 | tf_op jit(solution)/shard_map/all_gather | solution.py:318
  93.5 21.4 %all_gather.32 = bf16[1024,384]{0,1:T(8,128)(2,1)S(1)} all-gather(bf16[128,384]{0,1:T(8,128)(2,1)S(1)} %get-tuple-element.232), channel_id=1, replica_groups=mesh['section'=2,'seq'=8,'wshard'=8] {'wshard'}, dimensions={0}, use_global_device_ids=true | all-gather | bytes 884736 | tf_op jit(solution)/shard_map/all_gather | solution.py:310
  116.5 34.9 %all_gather.37 = bf16[1024,384]{0,1:T(8,128)(2,1)S(1)} all-gather(bf16[128,384]{0,1:T(8,128)(2,1)S(1)} %get-tuple-element.231), channel_id=1, replica_groups=mesh['section'=2,'seq'=8,'wshard'=8] {'wshard'}, dimensions={0}, use_global_device_ids=true | all-gather | bytes 884736 | tf_op jit(solution)/shard_map/all_gather | solution.py:310
  153.2 20.2 %collective-permute-start.1 = (bf16[128,1024]{1,0:T(8,128)(2,1)S(1)}, bf16[128,1024]{1,0:T(8,128)(2,1)}, u32[]{:S(2)}, u32[]{:S(2)}) collective-permute-start(bf16[128,1024]{1,0:T(8,128)(2,1)S(1)} %pad_maximum_fusion.24), channel_id=1, source_target_pairs={{0,64},{1,65},{2,66},{3,67},{4,68},{5,69},{6,70},{7,71},{8,72},{9,... | collective-permute-start | bytes 786440 | tf_op jit(solution)/shard_map/ppermute | solution.py:33
  223.9 5.3 shard_map.262
  252.3 8.6 %collective-permute-done.19 = bf16[128,1024]{1,0:T(8,128)(2,1)} collective-permute-done((bf16[128,1024]{1,0:T(8,128)(2,1)}, bf16[128,1024]{1,0:T(8,128)(2,1)}, u32[]{:S(2)}, u32[]{:S(2)}) %collective-permute-start.19) | collective-permute-done | bytes 262176 | tf_op jit(solution)/shard_map/ppermute | solution.py:33
  269.8 5.1 collective-permute-done.23
  289.1 5.3 shard_map.263
  294.4 6.0 %shard_map.264 = bf16[1024,384]{1,0:T(8,128)(2,1)S(1)} custom-call(s32[16]{0:T(128)S(1)} %fusion.111.where_ref, bf16[1024,128]{1,0:T(8,128)(2,1)S(1)} %slice.564.grad_ref, f32[1024,128]{1,0:T(8,128)S(1)} %concatenate.183.cos_ref, f32[1024,128]{1,0:T(8,128)S(1)} %concatenate.184.low_ref, f32[1024,128]{1,0:T(8,128)S(1)} %concatenate.185.high_ref, ...), custom_call_target="tpu_custom_call" | custom-call | flops 5000000000 | bytes 6000000 | tf_op jit(solution)/shard_map/pallas_call | solution.py:192
  332.6 4.8 collective-permute-done.50
  341.4 7.6 %collective-permute-done.33 = bf16[128,1024]{1,0:T(8,128)(2,1)S(1)} collective-permute-done((bf16[128,1024]{1,0:T(8,128)(2,1)S(1)}, bf16[128,1024]{1,0:T(8,128)(2,1)S(1)}, u32[]{:S(2)}, u32[]{:S(2)}) %collective-permute-start.33) | collective-permute-done | bytes 262176 | tf_op jit(solution)/shard_map/ppermute | solution.py:33
  365.2 16.3 %collective-permute-done.22 = bf16[128,1024]{1,0:T(8,128)(2,1)S(1)} collective-permute-done((bf16[128,1024]{1,0:T(8,128)(2,1)S(1)}, bf16[128,1024]{1,0:T(8,128)(2,1)S(1)}, u32[]{:S(2)}, u32[]{:S(2)}) %collective-permute-start.22) | collective-permute-done | bytes 262176 | tf_op jit(solution)/shard_map/ppermute | solution.py:33
  392.4 5.9 %shard_map.265 = bf16[1024,384]{1,0:T(8,128)(2,1)S(1)} custom-call(s32[16]{0:T(128)S(1)} %fusion.111.where_ref, bf16[1024,128]{1,0:T(8,128)(2,1)S(1)} %slice.563.grad_ref, f32[1024,128]{1,0:T(8,128)S(1)} %concatenate.183.cos_ref, f32[1024,128]{1,0:T(8,128)S(1)} %concatenate.184.low_ref, f32[1024,128]{1,0:T(8,128)S(1)} %concatenate.185.high_ref, ...), custom_call_target="tpu_custom_call" | custom-call | flops 5000000000 | bytes 6000000 | tf_op jit(solution)/shard_map/pallas_call | solution.py:192
  420.6 16.9 %collective-permute-done.83 = bf16[144,1536]{1,0:T(8,128)(2,1)S(1)} collective-permute-done((bf16[144,1536]{1,0:T(8,128)(2,1)S(1)}, bf16[144,1536]{1,0:T(8,128)(2,1)S(1)}, u32[]{:S(2)}, u32[]{:S(2)}) %collective-permute-start.83) | collective-permute-done | bytes 442400 | tf_op jit(solution)/shard_map/ppermute | solution.py:33
  440.3 12.1 %collective-permute-done.71 = bf16[4,144,1536]{2,1,0:T(8,128)(2,1)S(1)} collective-permute-done((bf16[4,144,1536]{2,1,0:T(8,128)(2,1)S(1)}, bf16[4,144,1536]{2,1,0:T(8,128)(2,1)S(1)}, u32[]{:S(2)}, u32[]{:S(2)}) %collective-permute-start.71) | collective-permute-done | bytes 1769504 | tf_op jit(solution)/shard_map/ppermute | solution.py:33
  453.7 8.9 %collective-permute-done.84 = bf16[144,1536]{1,0:T(8,128)(2,1)S(1)} collective-permute-done((bf16[144,1536]{1,0:T(8,128)(2,1)S(1)}, bf16[144,1536]{1,0:T(8,128)(2,1)S(1)}, u32[]{:S(2)}, u32[]{:S(2)}) %collective-permute-start.84) | collective-permute-done | bytes 442400 | tf_op jit(solution)/shard_map/ppermute | solution.py:33
  462.8 10.0 %collective-permute-done.74 = bf16[144,1536]{1,0:T(8,128)(2,1)S(1)} collective-permute-done((bf16[144,1536]{1,0:T(8,128)(2,1)S(1)}, bf16[144,1536]{1,0:T(8,128)(2,1)S(1)}, u32[]{:S(2)}, u32[]{:S(2)}) %collective-permute-start.74) | collective-permute-done | bytes 442400 | tf_op jit(solution)/shard_map/ppermute | solution.py:33
  478.9 8.3 %collective-permute-done.64 = bf16[128,1024]{1,0:T(8,128)(2,1)S(1)} collective-permute-done((bf16[128,1024]{1,0:T(8,128)(2,1)S(1)}, bf16[128,1024]{1,0:T(8,128)(2,1)S(1)}, u32[]{:S(2)}, u32[]{:S(2)}) %collective-permute-start.64) | collective-permute-done | bytes 262176 | tf_op jit(solution)/shard_map/ppermute | solution.py:33
  489.9 6.3 %collective-permute-start.76 = (bf16[128,128]{1,0:T(8,128)(2,1)S(1)}, bf16[128,128]{1,0:T(8,128)(2,1)S(1)}, u32[]{:S(2)}, u32[]{:S(2)}) collective-permute-start(bf16[128,128]{1,0:T(8,128)(2,1)S(1)} %slice.445), channel_id=1, source_target_pairs={{0,0},{1,64},{2,16},{3,80},{4,32},{5,96},{6,48},{7,112},{8,8},{9,7... | collective-permute-start | bytes 98312 | tf_op jit(solution)/shard_map/ppermute | solution.py:33
  510.3 10.3 %collective-permute-done.86 = bf16[144,1536]{1,0:T(8,128)(2,1)S(1)} collective-permute-done((bf16[144,1536]{1,0:T(8,128)(2,1)S(1)}, bf16[144,1536]{1,0:T(8,128)(2,1)S(1)}, u32[]{:S(2)}, u32[]{:S(2)}) %collective-permute-start.86) | collective-permute-done | bytes 442400 | tf_op jit(solution)/shard_map/ppermute | solution.py:33
  522.5 6.6 %collective-permute-done.79 = bf16[144,1536]{1,0:T(8,128)(2,1)S(1)} collective-permute-done((bf16[144,1536]{1,0:T(8,128)(2,1)S(1)}, bf16[144,1536]{1,0:T(8,128)(2,1)S(1)}, u32[]{:S(2)}, u32[]{:S(2)}) %collective-permute-start.79) | collective-permute-done | bytes 442400 | tf_op jit(solution)/shard_map/ppermute | solution.py:33
  530.0 7.5 %collective-permute-done.77 = bf16[144,1536]{1,0:T(8,128)(2,1)S(1)} collective-permute-done((bf16[144,1536]{1,0:T(8,128)(2,1)S(1)}, bf16[144,1536]{1,0:T(8,128)(2,1)S(1)}, u32[]{:S(2)}, u32[]{:S(2)}) %collective-permute-start.77) | collective-permute-done | bytes 442400 | tf_op jit(solution)/shard_map/ppermute | solution.py:33
  543.8 5.8 collective-permute-done.69
  (637 shorter events, 298.6 us)
Async XLA Ops:
  7.3 207.6 %all-gather.9.cloned.1.call-start = ((), (), s32[]{:S(2)}) async-start(), calls=%async_computation | async-start | bytes 1179648 | tf_op jit(solution)/shard_map/all_gather | solution.py:310
  11.6 210.8 %all-gather.11.cloned.1.call-start = ((), (), s32[]{:S(2)}) async-start(), calls=%async_computation.1 | async-start | bytes 1179648 | tf_op jit(solution)/shard_map/all_gather | solution.py:310
  24.8 156.0 %collective-permute-start.12 = (bf16[128,1024]{1,0:T(8,128)(2,1)}, bf16[128,1024]{1,0:T(8,128)(2,1)}, u32[]{:S(2)}, u32[]{:S(2)}) collective-permute-start(bf16[128,1024]{1,0:T(8,128)(2,1)} %bitcast.22), channel_id=1, source_target_pairs={{0,64},{1,65},{2,66},{3,67},{4,68},{5,69},{6,70},{7,71},{8,72},{9,... | collective-permute-start | bytes 786440 | tf_op jit(solution)/shard_map/ppermute | solution.py:33
  26.3 66.2 %collective-permute-start.9 = (bf16[128,384]{0,1:T(8,128)(2,1)}, bf16[128,384]{0,1:T(8,128)(2,1)}, u32[]{:S(2)}, u32[]{:S(2)}) collective-permute-start(bf16[128,384]{0,1:T(8,128)(2,1)} %bitcast.11), channel_id=1, source_target_pairs={{0,64},{1,65},{2,66},{3,67},{4,68},{5,69},{6,70},{7,71},{8,72},{9,... | collective-permute-start | bytes 294920 | tf_op jit(solution)/shard_map/ppermute | solution.py:33
  27.2 126.0 %collective-permute-start = (bf16[64,1024]{1,0:T(8,128)(2,1)}, bf16[64,1024]{1,0:T(8,128)(2,1)S(1)}, u32[]{:S(2)}, u32[]{:S(2)}) collective-permute-start(bf16[64,1024]{1,0:T(8,128)(2,1)} %dynamic-slice_bitcast_fusion.11), channel_id=1, source_target_pairs={{0,8},{1,9},{2,10},{3,11},{4,12},{5,13},{6,14},{7,15},{8,0},{9,1},... | collective-permute-start | bytes 393224 | tf_op jit(solution)/shard_map/ppermute | solution.py:33
  34.8 142.9 %collective-permute-start.39 = (bf16[64,1024]{1,0:T(8,128)(2,1)}, bf16[64,1024]{1,0:T(8,128)(2,1)}, u32[]{:S(2)}, u32[]{:S(2)}) collective-permute-start(bf16[64,1024]{1,0:T(8,128)(2,1)} %dynamic-slice_bitcast_fusion.8), channel_id=1, source_target_pairs={{0,8},{1,9},{2,10},{3,11},{4,12},{5,13},{6,14},{7,15},{8,0},{9,1},... | collective-permute-start | bytes 393224 | tf_op jit(solution)/shard_map/ppermute | solution.py:33
  36.6 199.6 %all-gather.15.cloned.1.call-start = ((), (), s32[]{:S(2)}) async-start(), calls=%async_computation.3 | async-start | bytes 1179648 | tf_op jit(solution)/shard_map/all_gather | solution.py:310
  93.4 157.2 %all-gather.13.cloned.1.call-start = ((), (), s32[]{:S(2)}) async-start(), calls=%async_computation.2 | async-start | bytes 1179648 | tf_op jit(solution)/shard_map/all_gather | solution.py:310
  153.2 30.2 %collective-permute-start.1 = (bf16[128,1024]{1,0:T(8,128)(2,1)S(1)}, bf16[128,1024]{1,0:T(8,128)(2,1)}, u32[]{:S(2)}, u32[]{:S(2)}) collective-permute-start(bf16[128,1024]{1,0:T(8,128)(2,1)S(1)} %pad_maximum_fusion.24), channel_id=1, source_target_pairs={{0,64},{1,65},{2,66},{3,67},{4,68},{5,69},{6,70},{7,71},{8,72},{9,... | collective-permute-start | bytes 786440 | tf_op jit(solution)/shard_map/ppermute | solution.py:33
  196.4 32.9 %collective-permute-start.13 = (bf16[128,1024]{1,0:T(8,128)(2,1)}, bf16[128,1024]{1,0:T(8,128)(2,1)}, u32[]{:S(2)}, u32[]{:S(2)}) collective-permute-start(bf16[128,1024]{1,0:T(8,128)(2,1)} %get-tuple-element.199), channel_id=1, source_target_pairs={{0,0},{1,64},{2,16},{3,80},{4,32},{5,96},{6,48},{7,112},{8,8},{9,7... | collective-permute-start | bytes 786440 | tf_op jit(solution)/shard_map/ppermute | solution.py:33
  201.9 35.8 %collective-permute-start.29 = (bf16[128,1024]{1,0:T(8,128)(2,1)}, bf16[128,1024]{1,0:T(8,128)(2,1)}, u32[]{:S(2)}, u32[]{:S(2)}) collective-permute-start(bf16[128,1024]{1,0:T(8,128)(2,1)} %get-tuple-element.198), channel_id=1, source_target_pairs={{0,0},{1,64},{2,16},{3,80},{4,32},{5,96},{6,48},{7,112},{8,8},{9,7... | collective-permute-start | bytes 786440 | tf_op jit(solution)/shard_map/ppermute | solution.py:33
  337.3 75.1 %collective-permute-start.80 = (bf16[4,144,1536]{2,1,0:T(8,128)(2,1)}, bf16[4,144,1536]{2,1,0:T(8,128)(2,1)}, u32[]{:S(2)}, u32[]{:S(2)}) collective-permute-start(bf16[4,144,1536]{2,1,0:T(8,128)(2,1)} %dynamic-slice_bitcast_fusion), channel_id=1, source_target_pairs={{0,1},{1,0},{2,3},{3,2},{4,5},{5,4},{6,7},{7,6},{8,9},{9,8},{10,11... | collective-permute-start | bytes 5308424 | tf_op jit(solution)/shard_map/ppermute | solution.py:33
  354.5 28.7 %collective-permute-start.59 = (bf16[128,1024]{1,0:T(8,128)(2,1)S(1)}, bf16[128,1024]{1,0:T(8,128)(2,1)S(1)}, u32[]{:S(2)}, u32[]{:S(2)}) collective-permute-start(bf16[128,1024]{1,0:T(8,128)(2,1)S(1)} %get-tuple-element.120), channel_id=1, source_target_pairs={{0,16},{1,17},{2,18},{3,19},{4,20},{5,21},{6,22},{7,23},{8,24},{9,... | collective-permute-start | bytes 786440 | tf_op jit(solution)/shard_map/ppermute | solution.py:33
  355.9 25.6 %collective-permute-start.22 = (bf16[128,1024]{1,0:T(8,128)(2,1)S(1)}, bf16[128,1024]{1,0:T(8,128)(2,1)S(1)}, u32[]{:S(2)}, u32[]{:S(2)}) collective-permute-start(bf16[128,1024]{1,0:T(8,128)(2,1)S(1)} %pad_maximum_fusion.26), channel_id=1, source_target_pairs={{0,8},{1,9},{2,10},{3,11},{4,12},{5,13},{6,14},{7,15},{8,0},{9,1},... | collective-permute-start | bytes 786440 | tf_op jit(solution)/shard_map/ppermute | solution.py:33
  361.3 26.0 %collective-permute-start.56 = (bf16[128,1024]{1,0:T(8,128)(2,1)S(1)}, bf16[128,1024]{1,0:T(8,128)(2,1)S(1)}, u32[]{:S(2)}, u32[]{:S(2)}) collective-permute-start(bf16[128,1024]{1,0:T(8,128)(2,1)S(1)} %collective-permute-done.55), channel_id=1, source_target_pairs={{0,64},{1,65},{2,66},{3,67},{4,68},{5,69},{6,70},{7,71},{8,72},{9,... | collective-permute-start | bytes 786440 | tf_op jit(solution)/shard_map/ppermute | solution.py:33
  362.5 24.8 %collective-permute-start.58 = (bf16[128,1024]{1,0:T(8,128)(2,1)S(1)}, bf16[128,1024]{1,0:T(8,128)(2,1)S(1)}, u32[]{:S(2)}, u32[]{:S(2)}) collective-permute-start(bf16[128,1024]{1,0:T(8,128)(2,1)S(1)} %collective-permute-done.57), channel_id=1, source_target_pairs={{0,64},{1,65},{2,66},{3,67},{4,68},{5,69},{6,70},{7,71},{8,72},{9,... | collective-permute-start | bytes 786440 | tf_op jit(solution)/shard_map/ppermute | solution.py:33
  412.3 40.2 %collective-permute-start.71 = (bf16[4,144,1536]{2,1,0:T(8,128)(2,1)S(1)}, bf16[4,144,1536]{2,1,0:T(8,128)(2,1)S(1)}, u32[]{:S(2)}, u32[]{:S(2)}) collective-permute-start(bf16[4,144,1536]{2,1,0:T(8,128)(2,1)S(1)} %dynamic-slice_bitcast_fusion.1), channel_id=1, source_target_pairs={{0,1},{1,0},{2,3},{3,2},{4,5},{5,4},{6,7},{7,6},{8,9},{9,8},{10,11... | collective-permute-start | bytes 5308424 | tf_op jit(solution)/shard_map/ppermute | solution.py:33
  418.4 59.2 %collective-permute-start.67 = (bf16[128,1024]{1,0:T(8,128)(2,1)S(1)}, bf16[128,1024]{1,0:T(8,128)(2,1)S(1)}, u32[]{:S(2)}, u32[]{:S(2)}) collective-permute-start(bf16[128,1024]{1,0:T(8,128)(2,1)S(1)} %copy-done.72), channel_id=1, source_target_pairs={{0,64},{1,65},{2,66},{3,67},{4,68},{5,69},{6,70},{7,71},{8,72},{9,... | collective-permute-start | bytes 786440 | tf_op jit(solution)/shard_map/ppermute | solution.py:33
  437.6 41.3 %collective-permute-start.66 = (bf16[128,1024]{1,0:T(8,128)(2,1)S(1)}, bf16[128,1024]{1,0:T(8,128)(2,1)S(1)}, u32[]{:S(2)}, u32[]{:S(2)}) collective-permute-start(bf16[128,1024]{1,0:T(8,128)(2,1)S(1)} %get-tuple-element.135), channel_id=1, source_target_pairs={{0,48},{1,49},{2,50},{3,51},{4,52},{5,53},{6,54},{7,55},{8,56},{9,... | collective-permute-start | bytes 786440 | tf_op jit(solution)/shard_map/ppermute | solution.py:33
  496.7 23.9 %collective-permute-start.86 = (bf16[144,1536]{1,0:T(8,128)(2,1)S(1)}, bf16[144,1536]{1,0:T(8,128)(2,1)S(1)}, u32[]{:S(2)}, u32[]{:S(2)}) collective-permute-start(bf16[144,1536]{1,0:T(8,128)(2,1)S(1)} %get-tuple-element.207), channel_id=1, source_target_pairs={{0,48},{1,49},{2,50},{3,51},{4,52},{5,53},{6,54},{7,55},{8,56},{9,... | collective-permute-start | bytes 1327112 | tf_op jit(solution)/shard_map/ppermute | solution.py:33
  499.5 29.6 %collective-permute-start.79 = (bf16[144,1536]{1,0:T(8,128)(2,1)S(1)}, bf16[144,1536]{1,0:T(8,128)(2,1)S(1)}, u32[]{:S(2)}, u32[]{:S(2)}) collective-permute-start(bf16[144,1536]{1,0:T(8,128)(2,1)S(1)} %get-tuple-element.205), channel_id=1, source_target_pairs={{0,16},{1,17},{2,18},{3,19},{4,20},{5,21},{6,22},{7,23},{8,24},{9,... | collective-permute-start | bytes 1327112 | tf_op jit(solution)/shard_map/ppermute | solution.py:33
  500.0 29.9 %collective-permute-start.78 = (bf16[144,1536]{1,0:T(8,128)(2,1)S(1)}, bf16[144,1536]{1,0:T(8,128)(2,1)S(1)}, u32[]{:S(2)}, u32[]{:S(2)}) collective-permute-start(bf16[144,1536]{1,0:T(8,128)(2,1)S(1)} %get-tuple-element.205), channel_id=1, source_target_pairs={{0,32},{1,33},{2,34},{3,35},{4,36},{5,37},{6,38},{7,39},{8,40},{9,... | collective-permute-start | bytes 1327112 | tf_op jit(solution)/shard_map/ppermute | solution.py:33
  502.6 34.9 %collective-permute-start.77 = (bf16[144,1536]{1,0:T(8,128)(2,1)S(1)}, bf16[144,1536]{1,0:T(8,128)(2,1)S(1)}, u32[]{:S(2)}, u32[]{:S(2)}) collective-permute-start(bf16[144,1536]{1,0:T(8,128)(2,1)S(1)} %get-tuple-element.205), channel_id=1, source_target_pairs={{0,48},{1,49},{2,50},{3,51},{4,52},{5,53},{6,54},{7,55},{8,56},{9,... | collective-permute-start | bytes 1327112 | tf_op jit(solution)/shard_map/ppermute | solution.py:33
  507.7 32.3 %collective-permute-start.38 = (bf16[128,1024]{1,0:T(8,128)(2,1)S(1)}, bf16[128,1024]{1,0:T(8,128)(2,1)S(1)}, u32[]{:S(2)}, u32[]{:S(2)}) collective-permute-start(bf16[128,1024]{1,0:T(8,128)(2,1)S(1)} %pad_maximum_fusion.28), channel_id=1, source_target_pairs={{0,8},{1,9},{2,10},{3,11},{4,12},{5,13},{6,14},{7,15},{8,0},{9,1},... | collective-permute-start | bytes 786440 | tf_op jit(solution)/shard_map/ppermute | solution.py:33
  (177 other events, 1897.0 us)
Sparse Core Ops, SparseCore 0:
  11.8 41.9 all-gather.8
  55.9 38.2 all-gather.10
  95.9 58.3 all-gather.14
  177.2 53.5 all-gather.12

commit v2 on v1

v2 whole, which is shorter than its diff:
```python
import math

import jax
import jax.numpy as jnp
from jax import lax
from jax.experimental import pallas as pl
from jax.experimental.pallas import tpu as pltpu
from jax.sharding import Mesh
from jax.sharding import PartitionSpec as P

HEAD = 64
ROT = 16
NORM_EPS = 1e-05
BF = jnp.bfloat16
F32 = jnp.float32
AXES = ("core", "x", "z_hi", "y", "z_lo")
SHARDS = ("y", "z_lo")
LENGTH = 1024
WIDTH = 1024
QROWS = 256
UNIT = 64


def place_of(index):
    return index // 64, (index // 16) % 4, (index // 8) % 2, (index // 2) % 4, index % 2


def index_of(core, x, zh, y, zl):
    return core * 64 + x * 16 + zh * 8 + 2 * y + zl


def route(block, target):
    targets = [target(*place_of(i)) for i in range(128)]
    pairs = [(i, index_of(*place)) for i, place in enumerate(targets) if place is not None]
    return lax.ppermute(block, AXES, pairs)


def from_all(block, axes):
    count = math.prod(lax.axis_size(axis) for axis in axes)
    return swapped(jnp.broadcast_to(block[None], (count, *block.shape)), axes)


def swapped(blocks, axes):
    return lax.all_to_all(blocks, axes, split_axis=0, concat_axis=0, tiled=True)


def along_x(block, step):
    return route(block, lambda c, x, zh, y, zl: (c, (x + step) % 4, zh, y, zl))


def along_y(block, step):
    return route(block, lambda c, x, zh, y, zl: (c, x, zh, (y + step) % 4, zl))


def across_low(block):
    return route(block, lambda c, x, zh, y, zl: (c, x, zh, y, 1 - zl))


def across_cores(block):
    return route(block, lambda c, x, zh, y, zl: (1 - c, x, zh, y, zl))


def across_high(block):
    return route(block, lambda c, x, zh, y, zl: (c, x, 1 - zh, y, zl))


def transposed(block):
    return route(block, lambda c, x, zh, y, zl: (zl, y, zh, x, c))


def pick(array, index, axis=0):
    return lax.dynamic_index_in_dim(array, index, axis, keepdims=False)


def dot(left, right):
    return jnp.dot(left, right, preferred_element_type=F32)


def dot_left(left, right):
    return lax.dot_general(left, right, (((0,), (0,)), ((), ())), preferred_element_type=F32)


def dot_right(left, right):
    return lax.dot_general(left, right, (((1,), (1,)), ((), ())), preferred_element_type=F32)


def head_lanes(rows, head):
    lanes = lax.broadcasted_iota(jnp.int32, (rows, 2 * HEAD), 1)
    return (lanes >= head * HEAD) & (lanes < (head + 1) * HEAD)


def turned(values, cosine, sine_low, sine_high):
    return (
        values * cosine
        + pltpu.roll(values, ROT // 2, 1) * sine_low
        + pltpu.roll(values, 2 * HEAD - ROT // 2, 1) * sine_high
    )


def masked_scores(query, keys, begin, block, reach):
    scores = dot_right(query, keys)
    rows = block * QROWS + lax.broadcasted_iota(jnp.int32, (QROWS, reach), 0)
    columns = lax.broadcasted_iota(jnp.int32, (QROWS, reach), 1)
    seen = (columns <= rows) & (columns >= begin)
    return jnp.where(seen, scores, -1e30)


def unit_rows(where_ref, m):
    return pl.ds(pl.multiple_of(where_ref[m] * UNIT, UNIT), UNIT)


def attend(where_ref, proj_ref, tables, mixed_ref, q_ref, k_ref, v_ref, o_ref, lse_ref):
    cos_ref, low_ref, high_ref, begin_ref = tables
    for m in range(LENGTH // UNIT):
        here = pl.ds(m * UNIT, UNIT)
        proj = proj_ref[unit_rows(where_ref, m), :]
        cosine, low, high = cos_ref[here, :], low_ref[here, :], high_ref[here, :]
        query = turned(proj[:, :128].astype(F32), cosine, low, high)
        q_ref[here, :] = (query.astype(BF).astype(F32) * (1.0 / math.sqrt(HEAD))).astype(BF)
        k_ref[here, :] = turned(proj[:, 128:256].astype(F32), cosine, low, high).astype(BF)
        v_ref[here, :] = proj[:, 256:]
    for block in range(LENGTH // QROWS):
        rows = pl.ds(block * QROWS, QROWS)
        reach = (block + 1) * QROWS
        keys, values = k_ref[:reach, :], v_ref[:reach, :]
        query = q_ref[rows, :]
        begin = begin_ref[rows, :1]
        outs, logs = [], []
        for head in range(2):
            own = head_lanes(QROWS, head)
            scores = masked_scores(jnp.where(own, query, jnp.zeros_like(query)), keys, begin, block, reach)
            highest = jnp.max(scores, axis=-1, keepdims=True)
            exponent = jnp.exp(scores - highest)
            total = jnp.sum(exponent, axis=-1, keepdims=True)
            probs = (exponent * (1.0 / total)).astype(BF)
            outs.append(dot(probs, values))
            logs.append(highest + jnp.log(total))
        first = head_lanes(QROWS, 0)
        o_ref[rows, :] = jnp.where(first, outs[0], outs[1]).astype(BF)
        lse_ref[rows, :] = jnp.where(first, logs[0], logs[1])
    for m in range(LENGTH // UNIT):
        mixed_ref[unit_rows(where_ref, m), :] = o_ref[pl.ds(m * UNIT, UNIT), :]


def attend_back(where_ref, tables, kept, do_ref, out_ref, dq_ref, dk_ref, dv_ref):
    cos_ref, low_ref, high_ref, begin_ref = tables
    q_ref, k_ref, v_ref, o_ref, lse_ref = kept
    for block in reversed(range(LENGTH // QROWS)):
        rows = pl.ds(block * QROWS, QROWS)
        reach = (block + 1) * QROWS
        keys, values = k_ref[:reach, :], v_ref[:reach, :]
        query, upstream, mixed = q_ref[rows, :], do_ref[rows, :], o_ref[rows, :].astype(F32)
        begin = begin_ref[rows, :1]
        grads = []
        for head in range(2):
            own = head_lanes(QROWS, head)
            query_own = jnp.where(own, query, jnp.zeros_like(query))
            up_own = jnp.where(own, upstream, jnp.zeros_like(upstream))
            scores = masked_scores(query_own, keys, begin, block, reach)
            probs = jnp.exp(scores - lse_ref[rows, head * HEAD : head * HEAD + 1])
            centre = jnp.sum(up_own.astype(F32) * mixed, axis=-1, keepdims=True)
            moved = (probs * (dot_right(up_own, values) - centre)).astype(BF)
            grads.append(dot(moved, keys))
            dk = dot_left(moved, query_own)
            dv = dot_left(probs.astype(BF), up_own)
            if block == LENGTH // QROWS - 1 and head == 0:
                dk_ref[...] = dk
                dv_ref[...] = dv
            else:
                dk_ref[:reach, :] += dk
                dv_ref[:reach, :] += dv
        first = head_lanes(QROWS, 0)
        dq_ref[rows, :] = jnp.where(first, grads[0], grads[1]) * (1.0 / math.sqrt(HEAD))
    for m in range(LENGTH // UNIT):
        here = pl.ds(m * UNIT, UNIT)
        there = unit_rows(where_ref, m)
        cosine, low, high = cos_ref[here, :], -low_ref[here, :], -high_ref[here, :]
        out_ref[there, :128] = turned(dq_ref[here, :], cosine, low, high).astype(BF)
        out_ref[there, 128:256] = turned(dk_ref[here, :], cosine, low, high).astype(BF)
        out_ref[there, 256:384] = dv_ref[here, :].astype(BF)


def barrier(*values):
    flat, tree = jax.tree.flatten(values)
    anywhere = pl.BlockSpec(memory_space=pl.ANY)
    flat = pl.pallas_call(
        lambda *refs: None,
        out_shape=[jax.ShapeDtypeStruct(value.shape, value.dtype) for value in flat],
        in_specs=[anywhere] * len(flat),
        out_specs=[anywhere] * len(flat),
        input_output_aliases={k: k for k in range(len(flat))},
    )(*flat)
    return jax.tree.unflatten(tree, flat)


def after(values, *others):
    flat, tree = jax.tree.flatten(values)
    others = jax.tree.leaves(others)
    anywhere = pl.BlockSpec(memory_space=pl.ANY)
    flat = pl.pallas_call(
        lambda *refs: None,
        out_shape=[jax.ShapeDtypeStruct(value.shape, value.dtype) for value in flat],
        in_specs=[anywhere] * (len(flat) + len(others)),
        out_specs=[anywhere] * len(flat),
        input_output_aliases={k: k for k in range(len(flat))},
    )(*flat, *others)
    return jax.tree.unflatten(tree, flat)


def run(body, scalars, arrays, outs, scratch=(), flops=0, bytes_accessed=4_000_000, spaces=None, limit=60):
    vmem = pl.BlockSpec(memory_space=pltpu.VMEM)
    return pl.pallas_call(
        body,
        out_shape=[jax.ShapeDtypeStruct(*out) for out in outs],
        in_specs=[pl.BlockSpec(memory_space=pltpu.SMEM)] + (spaces or [vmem] * len(arrays)),
        out_specs=[vmem] * len(outs),
        scratch_shapes=list(scratch),
        compiler_params=pltpu.CompilerParams(vmem_limit_bytes=limit * 1024 * 1024),
        cost_estimate=pl.CostEstimate(flops=flops, bytes_accessed=bytes_accessed, transcendentals=0),
    )(scalars, *arrays)


X, CORE, ZH, Y, ZL, PART, SHARD, BIAS = 0, 1, 2, 3, 4, 5, 6, 7


def lanes(start, extent=128):
    return pl.ds(pl.multiple_of(start, extent), extent)


def low_half(rows):
    return lax.broadcasted_iota(jnp.int32, (rows, 128), 1) < 64


def half_tiles(first, second):
    low = low_half(first.shape[0])
    return (
        jnp.where(low, first, pltpu.roll(second, 64, 1)),
        jnp.where(low, pltpu.roll(first, 64, 1), second),
    )


def column(row):
    return jnp.transpose(jnp.broadcast_to(row, (128, 128)))


def slice_kernel(
    at, qkv_all, up_all, down_all, dense_all, bias_qkv_all, bias_up_all, bias_dense, bias_down, gain_one, shift_one,
    gain_two, shift_two,
    qkv_self, qkv_other, rest_self, rest_other,
    qkv, up, down, dense, bias_qkv, small, rows, sems,
):
    x, core = at[X], at[CORE]
    copies = [(up_all.at[:, lanes(512 * k + 128 * x)], up.at[k]) for k in range(8)]
    copies += [(qkv_all.at[:, lanes(1024 * k + 256 * x, 256)], qkv.at[k]) for k in range(3)]
    copies.append((down_all.at[pl.ds(pl.multiple_of(128 * x, 128), 128), :], down))
    copies.append((dense_all.at[:, lanes(256 * x, 256)], dense))
    copies.append((bias_qkv_all, bias_qkv))
    copies.append((bias_up_all.at[:, lanes(128 * x)], small.at[0]))
    for k, vector in enumerate((bias_dense, bias_down, gain_one, shift_one, gain_two, shift_two)):
        copies.append((vector, small.at[1 + k]))
    copies = [pltpu.make_async_copy(*pair, sems.at[k]) for k, pair in enumerate(copies)]
    for copy in copies:
        copy.start()
    for copy in copies:
        copy.wait()
    for k in range(4):
        zero, one = half_tiles(up[2 * k].astype(F32), up[2 * k + 1].astype(F32))
        here = slice(128 * k, 128 * k + 128)
        rest_self[:, here] = jnp.where(core == 0, zero, one).astype(BF)
        rest_other[:, here] = jnp.where(core == 0, one, zero).astype(BF)
    for k in range(3):
        first, second = qkv[k, :, :128], qkv[k, :, 128:]
        here = slice(128 * k, 128 * k + 128)
        qkv_self[:128, here] = jnp.where(core == 0, first, second)
        qkv_other[:128, here] = jnp.where(core == 0, second, first)
    for k in range(2):
        first, second = down[:64, 512 * k : 512 * k + 512], down[64:, 512 * k : 512 * k + 512]
        rest_self[64 * k : 64 * k + 64, 512:] = jnp.where(core == 0, first, second)
        rest_other[64 * k : 64 * k + 64, 512:] = jnp.where(core == 0, second, first)
    first, second = dense[:, :128], dense[:, 128:]
    qkv_self[:128, 384:] = jnp.where(core == 0, first, second)
    qkv_other[:128, 384:] = jnp.where(core == 0, second, first)
    rows[...] = jnp.zeros_like(rows)
    for k in range(3):
        rows[k : k + 1, :] = bias_qkv[:, 128 * k : 128 * k + 128].astype(F32)
    for k in range(7):
        rows[3 + k : 4 + k, :] = small[k].astype(F32)
    plain = rows[...]
    number = lax.broadcasted_iota(jnp.int32, (16, 128), 0)
    moved = jnp.where(number == 3, pltpu.roll(plain, 64, 1), plain)
    for out, upper in ((qkv_self, core), (qkv_other, 1 - core)):
        out[128:, :128] = jnp.where(upper == 0, plain, moved).astype(BF)
        out[128:, 128:] = jnp.zeros((16, 384), BF)


def tables_kernel(at, places, frequency, cos_ref, low_ref, high_ref, begin_ref):
    place = jnp.transpose(jnp.broadcast_to(places[...].astype(F32), (128, LENGTH)))
    lane = lax.broadcasted_iota(jnp.int32, (LENGTH, 128), 1) % HEAD
    angles = place * frequency[...]
    sine = jnp.sin(angles)
    cos_ref[...] = jnp.where(lane < ROT, jnp.cos(angles), 1.0)
    low_ref[...] = jnp.where((lane >= ROT // 2) & (lane < ROT), sine, 0.0)
    high_ref[...] = jnp.where(lane < ROT // 2, -sine, 0.0)
    row = lax.broadcasted_iota(jnp.int32, (LENGTH, 128), 0)
    begin_ref[...] = row - place.astype(jnp.int32)


def prepare_qkv(at, blocks, wide, wide_turned, bias, bias_out, rows):
    bias[...] = jnp.zeros_like(bias)
    for shard, message in blocks:
        vectors = message[128:, :128].astype(F32)
        rows[16 * shard : 16 * shard + 16, :] = vectors
        here = slice(128 * shard, 128 * shard + 128)
        scale = column(vectors[6:7, :])
        for k in range(0, 384, 128):
            wide[here, k : k + 128] = (message[:128, k : k + 128].astype(F32) * scale).astype(BF)
        shift = jnp.broadcast_to(vectors[7:8, :], (8, 128)).astype(BF)
        bias[:, :384] += dot(shift, message[:128, :384])
    for k in range(3):
        bias[:, 128 * k : 128 * k + 128] += jnp.broadcast_to(rows[pl.ds(at[BIAS + k], 1), :], (8, 128))
    for shard in range(8):
        total = rows[16 * shard + 4 : 16 * shard + 5, :] + rows[16 * shard + 5 : 16 * shard + 6, :]
        bias_out[:, 128 * shard : 128 * shard + 128] = jnp.broadcast_to(total, (8, 128))
    wide_turned[...] = jnp.transpose(wide[...])


def prepare_up(at, blocks, rows, up, up_turned, bias):
    bias[...] = jnp.zeros_like(bias)
    for shard, message in blocks:
        vectors = rows[16 * shard : 16 * shard + 16, :]
        here = slice(128 * shard, 128 * shard + 128)
        scale = column(vectors[8:9, :])
        for k in range(0, 512, 128):
            up[here, k : k + 128] = (message[:128, k : k + 128].astype(F32) * scale).astype(BF)
        shift = jnp.broadcast_to(vectors[9:10, :], (8, 128)).astype(BF)
        bias[...] += dot(shift, message[:128, :512])
    for k in range(4):
        first = jnp.broadcast_to(rows[32 * k + 3 : 32 * k + 4, :], (8, 128))
        second = jnp.broadcast_to(rows[32 * k + 19 : 32 * k + 20, :], (8, 128))
        bias[:, 128 * k : 128 * k + 128] += half_tiles(first, second)[0]
    up_turned[...] = jnp.transpose(up[...])


def prepare_qkv_kernel(at, messages, *refs):
    prepare_qkv(at, [(k, messages.at[k]) for k in range(8)], *refs)


def prepare_rest_kernel(at, messages, vectors, up, up_turned, bias, down, down_turned):
    prepare_up(at, [(k, messages.at[k]) for k in range(8)], vectors, up, up_turned, bias)
    prepare_down([messages.at[k, :, 512:] for k in range(8)], down, down_turned)


def prepare_wide_kernel(at, messages, *outs):
    prepare_qkv(at, [(k, messages.at[k]) for k in range(8)], *outs[:5])
    prepare_up(at, [(k, messages.at[k, :, 384:]) for k in range(8)], *outs[4:])


def prepare_down(blocks, down, down_turned):
    for k, halves in enumerate(blocks):
        down[64 * k : 64 * k + 64, :512] = halves[:64, :]
        down[64 * k : 64 * k + 64, 512:] = halves[64:128, :]
    down_turned[...] = jnp.transpose(down[...])


def prepare_down_kernel(at, messages, down, down_turned):
    prepare_down([messages.at[k] for k in range(8)], down, down_turned)


QKV = [((1024, 384), BF), ((384, 1024), BF), ((8, 384), F32), ((8, 1024), F32), ((128, 128), F32)]
UP = [((1024, 512), BF), ((512, 1024), BF), ((8, 512), F32)]
DOWN = [((512, 1024), BF), ((1024, 512), BF)]


def norm_kernel(at, *refs):
    blocks, wide, bias, unit, proj = refs[:8], *refs[8:]
    for k in range(8):
        values = blocks[k][...].astype(F32)
        centred = values - jnp.mean(values, axis=-1, keepdims=True)
        spread = jnp.mean(centred * centred, axis=-1, keepdims=True)
        unit[128 * k : 128 * k + 128, :] = (centred * lax.rsqrt(spread + NORM_EPS)).astype(BF)
    for k in range(4):
        here = slice(256 * k, 256 * k + 256)
        proj[here, :] = (dot(unit[here, :], wide[...]) + bias[:1, :]).astype(BF)


def up_kernel(at, unit, up, bias, active, slope):
    for k in range(4):
        here = slice(256 * k, 256 * k + 256)
        middle = dot(unit[here, :], up[...]) + bias[:1, :]
        share = 0.5 * (1.0 + lax.erf(middle * (1.0 / math.sqrt(2.0))))
        density = jnp.exp(-0.5 * middle * middle) * (1.0 / math.sqrt(2.0 * math.pi))
        active[here, :] = (middle * share).astype(BF)
        slope[here, :] = (share + middle * density).astype(BF)


def attend_kernel(where_ref, proj, cosine, low, high, begin, mixed, *kept):
    attend(where_ref, proj, (cosine, low, high, begin), mixed, *kept)


def project_kernel(at, active, mixed, down, dense_parts, *refs):
    blocks, dense = refs[:8], refs[8]
    for k in range(8):
        dense[:, 128 * k : 128 * k + 128] = dense_parts[k]
    for k in (2, 1, 3, 0):
        here = slice(256 * k, 256 * k + 256)
        out = dot(active[here, :], down[...]) + dot(mixed[here, :], dense[...])
        blocks[2 * k][...] = out[:128].astype(BF)
        blocks[2 * k + 1][...] = out[128:].astype(BF)


def back_front_kernel(at, *refs):
    blocks, down_turned, dense_parts, slope, grad_middle, grad_mixed, dense_turned = refs[:8], *refs[8:]
    for k in range(8):
        dense_turned[128 * k : 128 * k + 128, :] = jnp.transpose(dense_parts[k])
    for k in range(8):
        here = slice(128 * k, 128 * k + 128)
        rows = blocks[k][...]
        grad_middle[here, :] = (dot(rows, down_turned[...]) * slope[here, :].astype(F32)).astype(BF)
        grad_mixed[here, :] = dot(rows, dense_turned[...]).astype(BF)


def back_attend_kernel(where_ref, grad_mixed, grad_middle, wide_turned, up_turned, cosine, low, high, begin, *refs):
    kept, blocks, grad_proj, (do_ref, dq_ref, dk_ref, dv_ref) = refs[:5], refs[5:13], refs[13], refs[14:]
    for m in range(LENGTH // UNIT):
        do_ref[pl.ds(m * UNIT, UNIT), :] = grad_mixed[unit_rows(where_ref, m), :]
    attend_back(where_ref, (cosine, low, high, begin), kept, do_ref, grad_proj, dq_ref, dk_ref, dv_ref)
    for k in (2, 1, 3, 0):
        here = slice(256 * k, 256 * k + 256)
        out = dot(grad_proj[here, :], wide_turned[...]) + dot(grad_middle[here, :], up_turned[...])
        blocks[2 * k][...] = out[:128].astype(BF)
        blocks[2 * k + 1][...] = out[128:].astype(BF)


def shard_at(at, step, beside):
    return 2 * ((at[Y] + step) % 4) + (at[ZL] + beside) % 2


def weight_terms(at, unit, grads, outward=None, order=None):
    extent = sum(grad.shape[1] for grad in grads)
    start = 640 if outward else 0
    arrays = (unit, *grads)
    scratch = []
    counts = {None: (1, 8), "y": (4, 2), "z": (2, 4)}[order]
    shapes = [((counts[1], 144, start + extent), BF)] * counts[0]
    if outward:
        active, mixed, rows, grad_middle = outward
        arrays = (*arrays, active, mixed, grad_middle, *rows)
        scratch = [pltpu.VMEM((512, 1024), F32), pltpu.VMEM((128, 1024), F32)]

    def body(at, unit, *refs):
        grad_refs, refs = refs[: len(grads)], refs[len(grads) :]
        if outward:
            (active, mixed, grad_middle), rows, refs = refs[:3], refs[3:11], refs[11:]
        outs, refs = refs[: len(shapes)], refs[len(shapes) :]
        places = []
        for step in range(4):
            for beside in range(2):
                if order == "y":
                    places.append((outs[step].at[beside], shard_at(at, step, beside)))
                elif order == "z":
                    places.append((outs[beside].at[step], shard_at(at, step, beside)))
                else:
                    places.append((outs[0].at[2 * step + beside], 2 * step + beside))
        if outward:
            down, dense = refs
            sums = jnp.zeros((1, 128), F32)
            for k in range(8):
                here = slice(128 * k, 128 * k + 128)
                block = rows[k][...]
                more_down = dot_left(active[here, :], block)
                more_dense = dot_left(mixed[here, :], block)
                if k == 0:
                    down[...] = more_down
                    dense[...] = more_dense
                else:
                    down[...] += more_down
                    dense[...] += more_dense
                sums = sums + jnp.sum(rows[k][:, lanes(128 * at[PART])].astype(F32), axis=0, keepdims=True)
            sums_up = jnp.sum(grad_middle[...].astype(F32), axis=0, keepdims=True)
            for place, shard in places:
                piece = down[pl.ds(pl.multiple_of(64 * shard, 64), 64), :].astype(BF)
                place[:64, :512] = piece[:, :512]
                place[64:128, :512] = piece[:, 512:]
                place[:128, 512:640] = dense[:, lanes(128 * shard)].astype(BF)
                place[128:, :128] = jnp.broadcast_to(sums, (16, 128)).astype(BF)
                place[128:, 128:640] = jnp.broadcast_to(sums_up, (16, 512)).astype(BF)
        at_column = start
        for grad in grad_refs:
            columns = grad.shape[1]
            here = slice(at_column, at_column + columns)
            sums = jnp.sum(grad[...].astype(F32), axis=0, keepdims=True)
            for place, shard in places:
                terms = dot_left(unit[:, lanes(128 * shard)], grad[...])
                place[:128, here] = terms.astype(BF)
                place[128:, here] = jnp.broadcast_to(sums, (16, columns)).astype(BF)
            at_column += columns

    outs = run(body, at, arrays, shapes, scratch, flops=2 * 1024 * 1024 * (extent + start))
    return outs if order else outs[0]


def final_kernel(at, *refs):
    firsts, seconds = refs[:2], refs[2:10]
    qkv, up, gain_one, shift_one, gain_two, shift_two = refs[10:16]
    grad_qkv, grad_up, grad_down, grad_dense = refs[16:20]
    bias_qk, bias_v, bias_up, bias_out, gain_a, shift_a, gain_b, shift_b = refs[20:28]
    sums, sums_qkv, sums_up, sums_out, sems = refs[28:]
    x, core, shard = at[X], at[CORE], at[SHARD]

    @pl.when(core == 0)
    def _():
        copies = [pltpu.make_async_copy(firsts[k], sums.at[k], sems.at[k]) for k in range(2)]
        for copy in copies:
            copy.start()
        for copy in copies:
            copy.wait()

    @pl.when(core == 1)
    def _():
        copies = []
        for k in range(2):
            for r in range(4):
                target = sums.at[k, (x + r) % 4]
                copies.append(pltpu.make_async_copy(seconds[4 * k + r], target, sems.at[len(copies)]))
        for copy in copies:
            copy.start()
        for copy in copies:
            copy.wait()

    def whole(beside, r, columns):
        return sums[beside, r, :128, columns].astype(F32)

    def below(beside, r, columns):
        return sums[beside, r, 128:, columns].astype(F32)

    gain_col, shift_col = column(gain_one[...].astype(F32)), column(shift_one[...].astype(F32))
    gain_col_two, shift_col_two = column(gain_two[...].astype(F32)), column(shift_two[...].astype(F32))
    totals = [jnp.zeros((128, 128), F32) for _ in range(4)]
    for r in range(4):
        column_no = r
        for half in range(2):
            beside = (core + half) % 2
            part = 2 * column_no + half
            for k in range(3):
                cols = slice(1152 + 128 * k, 1280 + 128 * k)
                raw = whole(beside, r, cols)
                total = below(beside, r, cols)[:1]
                place = lanes(1024 * k + 128 * part)
                weight = qkv[:, place].astype(F32)
                grad_qkv[:, place] = gain_col * raw + shift_col * total
                sums_qkv[pl.ds(8 * k + part, 1), :] = total
                totals[0] += weight * raw
                totals[1] += weight * total
            grad_down[pl.ds(pl.multiple_of(64 * part, 64), 64), :512] = sums[beside, r, :64, :512].astype(F32)
            grad_down[pl.ds(pl.multiple_of(64 * part, 64), 64), 512:] = sums[beside, r, 64:128, :512].astype(F32)
            grad_dense[:, lanes(128 * part)] = whole(beside, r, slice(512, 640))
            sums_out[pl.ds(part, 1), :] = below(beside, r, slice(0, 128))[:1]
        zero, one = core % 2, (core + 1) % 2
        for k in range(4):
            cols = slice(640 + 128 * k, 768 + 128 * k)
            beneath = slice(128 + 128 * k, 256 + 128 * k)
            raws = half_tiles(whole(zero, r, cols), whole(one, r, cols))
            adds = half_tiles(below(zero, r, beneath), below(one, r, beneath))
            for odd in range(2):
                raw, total = raws[odd], adds[odd][:1]
                place = lanes(1024 * k + 512 * odd + 128 * column_no)
                weight = up[:, place].astype(F32)
                grad_up[:, place] = gain_col_two * raw + shift_col_two * total
                sums_up[pl.ds(8 * k + 4 * odd + column_no, 1), :] = total
                totals[2] += weight * raw
                totals[3] += weight * total
    for out, total in zip((gain_a, shift_a, gain_b, shift_b), totals):
        out[...] = jnp.sum(jnp.transpose(total), axis=0, keepdims=True)
    for k in range(2):
        bias_qk[:, 128 * k : 128 * k + 128] = sums_qkv[pl.ds(2 * shard + k, 1), :]
    bias_v[...] = sums_qkv[pl.ds(16 + shard, 1), :]
    for k in range(4):
        bias_up[:, 128 * k : 128 * k + 128] = sums_up[pl.ds(4 * shard + k, 1), :]
    bias_out[...] = sums_out[pl.ds(shard, 1), :]


def added(*blocks):
    total = blocks[0].astype(F32)
    for block in blocks[1:]:
        total = total + block.astype(F32)
    return total


def gather_rows(mine):
    own = [mine] + [along_x(mine, -r) for r in (1, 2, 3)]
    other = [across_cores(block) for block in own]
    return [rows for pair in zip(own, other) for rows in pair]


def joined_cores(blocks):
    joined = {r: added(blocks[2 * r], across_cores(blocks[2 * r + 1])) for r in (2, 1, 3, 0)}
    return [joined[0]] + [joined[r].astype(BF) for r in (1, 2, 3)]


def joined_chips(joined):
    return added(joined[0], *(along_x(joined[r], r) for r in (1, 2, 3)))


def summed(blocks):
    return jnp.sum(blocks.astype(F32), axis=0)


def normalized(rows):
    values = rows.astype(F32)
    centre = jnp.mean(values, axis=-1, keepdims=True)
    centred = values - centre
    spread = jnp.mean(centred * centred, axis=-1, keepdims=True)
    scale = lax.rsqrt(spread + NORM_EPS)
    return centred * scale, scale


def norm_back(grad, rows):
    unit, scale = normalized(rows)
    mean_grad = jnp.mean(grad, axis=-1, keepdims=True)
    mean_both = jnp.mean(grad * unit, axis=-1, keepdims=True)
    return scale * (grad - mean_grad - unit * mean_both)


def shards(
    tokens, positions, w_qkv, b_qkv, w_dense, b_dense, w_up, b_up, w_down, b_down,
    norm1_gain, norm1_shift, norm2_gain, norm2_shift, cotangent,
):
    core, x, zh, y, zl = (lax.axis_index(axis) for axis in AXES)
    shard = 2 * y + zl
    part = 2 * x + core
    first_core = core == 0
    anywhere, vmem = pl.BlockSpec(memory_space=pl.ANY), pl.BlockSpec(memory_space=pltpu.VMEM)

    bias_rows = [16 * ((8 * k + part) // 3) + (8 * k + part) % 3 for k in range(3)]
    at = jnp.stack([x, core, zh, y, zl, part, shard] + bias_rows).astype(jnp.int32)
    unit_no = jnp.arange(16, dtype=jnp.int32)
    where = (
        ((unit_no // 4 - x) % 4) * 4
        + jnp.bitwise_xor(unit_no % 2, core) * 2
        + jnp.bitwise_xor((unit_no // 2) % 2, zh)
    ).astype(jnp.int32)

    def own_rows(array):
        own = lax.dynamic_slice_in_dim(pick(array, zh), core * UNIT, UNIT, 0)
        lent = lax.dynamic_slice_in_dim(pick(array, 1 - zh), core * UNIT, UNIT, 0)
        return jnp.concatenate([own, across_high(lent)], axis=0)

    own_tokens = own_rows(tokens)

    sliced = run(
        slice_kernel,
        at,
        (
            w_qkv[0], w_up[0], w_down[0], w_dense[0], b_qkv, b_up, b_dense, b_down,
            norm1_gain, norm1_shift, norm2_gain, norm2_shift,
        ),
        [((144, 512), BF)] * 2 + [((128, 1024), BF)] * 2,
        [
            pltpu.VMEM((3, 128, 256), BF),
            pltpu.VMEM((8, 128, 128), BF),
            pltpu.VMEM((128, 1024), BF),
            pltpu.VMEM((128, 256), BF),
            pltpu.VMEM((1, 384), BF),
            pltpu.VMEM((7, 1, 128), BF),
            pltpu.VMEM((16, 128), F32),
            pltpu.SemaphoreType.DMA((21,)),
        ],
        spaces=[pl.BlockSpec(memory_space=pltpu.HBM)] * 12,
    )
    qkv_theirs, rest_theirs = across_cores(sliced[1]), across_cores(sliced[3])
    qkv, qkv_two = jnp.where(first_core, sliced[0], qkv_theirs), jnp.where(first_core, qkv_theirs, sliced[0])
    qkv = jnp.concatenate([qkv, qkv_two[:, 384:]], axis=1)
    rest = jnp.where(first_core, sliced[2], rest_theirs)
    rest_two = jnp.where(first_core, rest_theirs, sliced[2])
    wide_two = jnp.concatenate([qkv_two[:, :384], jnp.pad(rest_two[:, :512], ((0, 16), (0, 0)))], axis=1)
    down_two = rest_two[:, 512:]

    half = ROT // 2
    frequency = 1.0 / 10000.0 ** (jnp.arange(half).astype(F32) * 2.0 / ROT)
    frequency = jnp.concatenate([jnp.tile(frequency, HEAD // half)] * 2)[None, :]
    tables = run(
        tables_kernel,
        at,
        (lax.dynamic_slice_in_dim(positions, zh, 1, 0), frequency),
        [((LENGTH, 128), F32)] * 3 + [((LENGTH, 128), jnp.int32)],
    )

    def front(rows, wide, bias):
        return run(
            norm_kernel, at, (*rows, wide, bias), [((1024, 1024), BF), ((1024, 384), BF)], flops=1_000_000_000
        )

    def front_up(unit, up, bias):
        return run(up_kernel, at, (unit, up, bias), [((1024, 512), BF)] * 2, flops=1_000_000_000)

    def attention(proj):
        outs = run(
            attend_kernel,
            where,
            (proj, *tables),
            [((1024, 128), BF)] * 5 + [((1024, 128), F32)],
            flops=4_000_000_000,
        )
        return outs[0], outs[1:]

    def project(active, mixed, down, dense):
        return run(
            project_kernel,
            at,
            (active, mixed, down, dense),
            [((128, 1024), BF)] * 8,
            [pltpu.VMEM((128, 1024), BF)],
            flops=1_500_000_000,
        )

    def back_front(rows, down_turned, dense, slope):
        return run(
            back_front_kernel,
            at,
            (*rows, down_turned, dense, slope),
            [((1024, 512), BF), ((1024, 128), BF)],
            [pltpu.VMEM((1024, 128), BF)],
            flops=1_500_000_000,
        )

    def back_attend(grad_mixed, grad_middle, qkv_turned, up_turned, kept):
        outs = run(
            back_attend_kernel,
            where,
            (grad_mixed, grad_middle, qkv_turned, up_turned, *tables, *kept),
            [((128, 1024), BF)] * 8 + [((1024, 384), BF)],
            [pltpu.VMEM((1024, 128), BF)] + [pltpu.VMEM((1024, 128), F32)] * 3,
            flops=6_000_000_000,
        )
        return outs[:8], outs[8]

    qkvs = from_all(after(qkv, own_tokens), SHARDS)
    rows_one = gather_rows(own_tokens)
    qkv_one, qkv_turned_one, qkv_bias, bias_out_one, vectors = run(prepare_qkv_kernel, at, (qkvs,), QKV)
    dense = jnp.stack([qkvs[:, :128, 384:512], qkvs[:, :128, 512:]], axis=1)
    dense = swapped(after(dense, rows_one[2::2]), ("x", "core"))
    dense_one, dense_two = dense[:, 0], dense[:, 1]
    rests = from_all(after(rest, dense_one, dense_two), SHARDS)
    unit_one, proj = front(rows_one, qkv_one, qkv_bias)
    mixed_one, kept_one = attention(proj)
    rests, wide_two = after((rests, wide_two), mixed_one)

    up_one, up_turned_one, up_bias, down_one, down_turned_one = run(
        prepare_rest_kernel, at, (rests, vectors), UP + DOWN
    )
    active_one, slope_one = front_up(unit_one, up_one, up_bias)
    wides = from_all(after(wide_two, rests), SHARDS)
    blocks = project(active_one, mixed_one, down_one, dense_one)
    joined = joined_cores(blocks)
    hidden_one = own_tokens.astype(F32) + joined_chips(joined) + bias_out_one[:1, :]
    hidden_one = hidden_one.astype(BF)
    rows_two = gather_rows(hidden_one)
    downs = from_all(after(down_two, wides), SHARDS)
    own_cotangent = own_rows(after(cotangent, rows_two[2::2]))
    qkv_two, qkv_turned_two, qkv_bias, bias_out_two, _, up_two, up_turned_two, up_bias = run(
        prepare_wide_kernel, at, (wides,), QKV + UP
    )

    grad_own = [own_cotangent] + [along_x(own_cotangent, -r) for r in (1, 2, 3)]
    unit_two, proj = front(rows_two, qkv_two, qkv_bias)
    mixed_two, kept_two = attention(proj)
    active_two, slope_two = front_up(unit_two, up_two, up_bias)
    grad_own = after(grad_own, active_two, mixed_two)
    grad_rows = [rows for block in grad_own for rows in (block, across_cores(block))]
    down_two, down_turned_two = run(prepare_down_kernel, at, (downs,), DOWN)

    grad_middle, grad_mixed = back_front(grad_rows, down_turned_two, dense_two, slope_two)
    blocks, grad_proj = back_attend(grad_mixed, grad_middle, qkv_turned_two, up_turned_two, kept_two)
    joined = joined_cores(blocks)
    unit_late = after(unit_two, joined)
    out_sums = weight_terms(at, unit_late, (), (active_two, mixed_two, grad_rows, grad_middle))
    wide_sums = weight_terms(at, unit_late, (grad_middle, grad_proj))
    joined[0] = after(joined[0], out_sums, wide_sums)
    out_sums = swapped(out_sums, SHARDS)
    grad_two = own_cotangent.astype(F32) + norm_back(joined_chips(joined), hidden_one)
    grad_mid = grad_two.astype(BF)
    grad_rows = gather_rows(grad_mid)
    grad_rows, out_sums, wide_sums = barrier(grad_rows, out_sums, wide_sums)

    wide_sums = swapped(wide_sums, SHARDS)
    grad_middle, grad_mixed = back_front(grad_rows, down_turned_one, dense_one, slope_one)
    early_sums = weight_terms(at, unit_one, (grad_middle,), (active_one, mixed_one, grad_rows, grad_middle))
    blocks, grad_proj = back_attend(grad_mixed, grad_middle, qkv_turned_one, up_turned_one, kept_one)
    blocks, grad_proj, wide_sums, early_sums = barrier(blocks, grad_proj, wide_sums, early_sums)

    def turned_dense(total):
        dense = jnp.concatenate([transposed(total[:128, 512:640]), total[128:, 512:640]], axis=0)
        return jnp.concatenate([total[:, :512], dense, total[:, 640:]], axis=1)

    def to_keeper(parts, layer):
        return route(parts, lambda c, x, zh, y, zl: (layer, x, zh, y, zl) if c != layer else None)

    early_sums = swapped(early_sums, SHARDS)
    joined = joined_cores(blocks)
    late_sums = weight_terms(at, unit_one, (grad_proj,))
    grad_one = grad_mid.astype(F32) + norm_back(joined_chips(joined), own_tokens)
    grad_low = grad_one.astype(BF)
    joined = joined_cores(project(after(active_two, late_sums), mixed_two, down_two, dense_two))
    hidden_two = hidden_one.astype(F32) + joined_chips(joined) + bias_out_two[:1, :]
    hidden_two = hidden_two.astype(BF)
    second = turned_dense(jnp.concatenate([summed(out_sums), summed(wide_sums)], axis=1).astype(BF))
    second_high = across_high(second)
    early_sums, late_sums, grad_low, hidden_two, second, second_high = barrier(
        early_sums, late_sums, grad_low, hidden_two, second, second_high
    )
    late_sums = swapped(late_sums, SHARDS)
    second = added(second, second_high).astype(BF)
    second = [second] + [along_x(second, -r) for r in (1, 2, 3)]
    early = summed(early_sums).astype(BF)
    early_high = across_high(early)
    grad_beside, hidden_beside = across_cores(grad_low), across_cores(hidden_two)
    late_sums, second, early, early_high, grad_beside, hidden_beside = barrier(
        late_sums, second, early, early_high, grad_beside, hidden_beside
    )
    late = summed(late_sums).astype(BF)
    late = added(late, across_high(late)).astype(BF)
    early = turned_dense(added(early, early_high).astype(BF))
    late, early, second = barrier(late, early, second)
    first = from_all(jnp.concatenate([early, late], axis=1), ("x",))
    second_sums = second + [to_keeper(block, 1) for block in second]

    def placed(pairs):
        local, lent = [], []
        for own, beside in pairs:
            low = jnp.where(first_core, own, beside)
            high = jnp.where(first_core, beside, own)
            local.append(jnp.concatenate([low[:UNIT], high[:UNIT]], axis=0))
            lent.append(jnp.concatenate([low[UNIT:], high[UNIT:]], axis=0))
        local, lent = jnp.stack(local), across_high(jnp.stack(lent))
        return jnp.stack([jnp.where(zh == 0, local, lent), jnp.where(zh == 0, lent, local)], axis=1)

    outputs = placed(
        [
            (jnp.where(first_core, hidden_one, hidden_two), jnp.where(first_core, rows_two[1], hidden_beside)),
            (jnp.where(first_core, grad_low, grad_mid), jnp.where(first_core, grad_beside, grad_rows[1])),
        ]
    )
    hidden, in_grads = outputs[0], outputs[1].astype(F32)
    first, second_sums, in_grads = barrier(first, second_sums, in_grads)
    first_sums = [first, to_keeper(first, 0)]

    outs = run(
        final_kernel,
        at,
        (
            *first_sums, *second_sums,
            w_qkv[0], w_up[0], norm1_gain, norm1_shift, norm2_gain, norm2_shift,
        ),
        [((128, 3072), F32), ((128, 4096), F32), ((512, 1024), F32), ((128, 1024), F32)]
        + [((1, 256), F32), ((1, 128), F32), ((1, 512), F32)]
        + [((1, 128), F32)] * 5,
        [
            pltpu.VMEM((2, 4, 144, 1536), BF),
            pltpu.VMEM((24, 128), F32),
            pltpu.VMEM((32, 128), F32),
            pltpu.VMEM((8, 128), F32),
            pltpu.SemaphoreType.DMA((8,)),
        ],
        spaces=[anywhere] * 10 + [vmem] * 6,
    )
    grad_qkv, grad_up, grad_down, grad_dense, bias_qk, bias_v, bias_up, bias_out, *norms = outs
    return (
        hidden[None], in_grads[None], grad_qkv[None], bias_qk, bias_v, grad_dense[None], bias_out,
        grad_up[None], bias_up, grad_down[None], bias_out, *norms,
    )


def solution(mesh):
    mesh = Mesh(mesh.devices.reshape(2, 4, 2, 4, 2), AXES)
    rows = P("core", SHARDS, None)
    vector = P("core", SHARDS)
    tokens = P(SHARDS, ("x", "z_hi"), None)
    layered = P("core", SHARDS, ("x", "z_hi"), None)
    in_specs = (
        tokens, P(SHARDS, None),
        rows, vector, rows, vector, rows, vector, rows, vector, vector, vector, vector, vector,
        tokens,
    )
    out_specs = (
        layered, layered,
        rows, vector, vector, rows, vector, rows, vector, rows, vector, vector, vector, vector, vector,
    )
    return jax.shard_map(shards, mesh=mesh, in_specs=in_specs, out_specs=out_specs, check_vma=False)
```

time: 604 us -> 465 us (0.77)
  Pallas kernels: 22.5 us -> 132 us
  blocking collectives: 101 us -> 0 us
  waiting for transfers between devices: 160 us -> 97.2 us
  local copies, waits for them, and re-layouts: 89.5 us -> 37.3 us
  starting transfers between devices: 115 us -> 153 us
  matrix products: 27.8 us -> 0 us
  other arithmetic: 61.2 us -> 34.9 us
  between operations: 16.3 us -> 1.98 us
    pallas_call x4 -> x40, Pallas kernels: 22.5 us -> 132 us  [the longest x23 132 us: run(): pl.pallas_call(body, out_shape=[jax.ShapeDtypeStruct(*out) for out in out...]
    all_gather x4 -> x0, blocking collectives: 101 us -> none  [the longest x2 56.3 us: gathered(): return lax.all_gather(block, 'wshard', axis=0, tiled=True)]
    ppermute x90 -> x76, waiting for transfers between devices: 160 us -> 68.6 us  [route(): return lax.ppermute(block, AXES, pairs)]
    all_to_all x0 -> x10, starting transfers between devices: none -> 55.5 us  [swapped(): return lax.all_to_all(blocks, axes, split_axis=0, concat_axis=0, tiled=True)]
    all_to_all x0 -> x10, waiting for transfers between devices: none -> 28.6 us  [swapped(): return lax.all_to_all(blocks, axes, split_axis=0, concat_axis=0, tiled=True)]
    dot_general x12 -> x0, matrix products: 27.8 us -> none  [the longest x4 11.1 us: dot_left(): lax.dot_general(left, right, (((0,), (0,)), ((), ())), preferred_element_...]
    unnamed x259 -> x159, local copies, waits for them, and re-layouts: 43 us -> 18.1 us
    ppermute x90 -> x76, starting transfers between devices: 115 us -> 97.7 us  [route(): return lax.ppermute(block, AXES, pairs)]
  transfers between devices with their start and end apart: 94 -> 86, of which waited for: 27 -> 27; matrix products, arithmetic and copies ran while one was open for 19% -> 9% of each run, Pallas kernels for 2% -> 20%
where the time goes in v2:
time: 465 us; the launch traced here: 456 us
  starting transfers between devices  153 us (33%)
  Pallas kernels  132 us (28%)
  waiting for transfers between devices  97.2 us (21%)
  local copies, waits for them, and re-layouts  37.3 us (8%)
  other arithmetic  34.9 us (8%)
    pallas_call x23, Pallas kernels, run(): pl.pallas_call(body, out_shape=[jax.ShapeDtypeStruct(*out) for out in out...  132 us
    ppermute x76, starting transfers between devices, route(): return lax.ppermute(block, AXES, pairs)  97.7 us
    ppermute x76, waiting for transfers between devices, route(): return lax.ppermute(block, AXES, pairs)  68.6 us
    all_to_all x10, starting transfers between devices, swapped(): return lax.all_to_all(blocks, axes, split_axis=0, concat_axis=0, tiled=True)  55.5 us
    all_to_all x10, waiting for transfers between devices, swapped(): return lax.all_to_all(blocks, axes, split_axis=0, concat_axis=0, tiled=True)  28.6 us
    unnamed x159, local copies, waits for them, and re-layouts  18.1 us
    broadcast_in_dim x5, local copies, waits for them, and re-layouts, from_all(): return swapped(jnp.broadcast_to(block[None], (count, *block.shape)), axes)  10.5 us
  transfers between devices with their start and end apart: 86, of which 27 were waited for; matrix products, arithmetic and copies ran while one was open for 9% of the time, Pallas kernels for 20%

profile of v2, /device:TPU:9, one launch (start us, length us, event | category | flops | bytes accessed | tf_op | source)
XLA Modules:
  0.0 456.3 jit_solution(6604768191752135722)
XLA Ops:
  27.8 14.3 %all-to-all-done.messages = bf16[8,144,640]{2,1,0:T(8,128)(2,1)S(1)} async-done(((bf16[8,144,640]{2,1,0:T(8,128)(2,1)}), bf16[8,144,640]{2,1,0:T(8,128)(2,1)S(1)}, u32[]{:S(2)}, u32[]{:S(2)}) %all-to-all-start) | async-done | bytes 1474592 | tf_op jit(solution)/shard_map/all_to_all | solution.py:44
  44.1 5.8 %all-to-all-start.1 = ((bf16[8,2,128,128]{3,2,1,0:T(8,128)(2,1)}), bf16[8,2,128,128]{3,2,1,0:T(8,128)(2,1)S(1)}, u32[]{:S(2)}, u32[]{:S(2)}) async-start(bf16[8,2,128,128]{3,2,1,0:T(8,128)(2,1)} %shard_map.266), calls=%async_computation.1 | async-start | bytes 1048576 | tf_op jit(solution)/shard_map/all_to_all | solution.py:44
  51.6 7.7 %all-to-all-done.1 = bf16[8,2,128,128]{3,2,1,0:T(8,128)(2,1)S(1)} async-done(((bf16[8,2,128,128]{3,2,1,0:T(8,128)(2,1)}), bf16[8,2,128,128]{3,2,1,0:T(8,128)(2,1)S(1)}, u32[]{:S(2)}, u32[]{:S(2)}) %all-to-all-start.1) | async-done | bytes 524320 | tf_op jit(solution)/shard_map/all_to_all | solution.py:44
  62.7 5.7 %all-to-all-start.2 = ((bf16[8,128,1024]{2,1,0:T(8,128)(2,1)}), bf16[8,128,1024]{2,1,0:T(8,128)(2,1)S(1)}, u32[]{:S(2)}, u32[]{:S(2)}) async-start(bf16[8,128,1024]{2,1,0:T(8,128)(2,1)} %broadcast_in_dim.23), calls=%async_computation.2 | async-start | bytes 4194304 | tf_op jit(solution)/shard_map/all_to_all | solution.py:44
  86.2 7.2 %shard_map.269 = (bf16[1024,128]{1,0:T(8,128)(2,1)}, bf16[1024,128]{1,0:T(8,128)(2,1)}, bf16[1024,128]{1,0:T(8,128)(2,1)}, bf16[1024,128]{1,0:T(8,128)(2,1)}, bf...) custom-call(s32[16]{0:T(128)} %fusion.32.where_ref, bf16[1024,384]{1,0:T(8,128)(2,1)} %get-tuple-element.177.proj, ...), custom_call_target="tpu_custom_call" | custom-call | flops 4000000000 | bytes 4000000 | tf_op jit(solution)/shard_map/pallas_call | solution.py:212
  102.0 5.4 %shard_map.272 = (bf16[1024,512]{1,0:T(8,128)(2,1)}, bf16[1024,512]{1,0:T(8,128)(2,1)}) custom-call(s32[10]{0:T(128)} %stack.79.at, bf16[1024,1024]{1,0:T(8,128)(2,1)} %get-tuple-element.174.unit, bf16[1024,512]{1,0:T(8,128)(2,1)} %get-tuple-element.185.up, f32[8,512]{1,0:T(8,128)} %get-tuple-element.186.bias), custom_call_target="tpu_custom_call" | custom-call | flops 1000000000 | bytes 4000000 | tf_op jit(solution)/shard_map/pallas_call | solution.py:212
  115.8 6.1 %all-to-all-start.3 = ((bf16[8,144,896]{2,1,0:T(8,128)(2,1)}), bf16[8,144,896]{2,1,0:T(8,128)(2,1)S(1)}, u32[]{:S(2)}, u32[]{:S(2)}) async-start(bf16[8,144,896]{2,1,0:T(8,128)(2,1)} %broadcast_in_dim.25), calls=%async_computation.3 | async-start | bytes 4128768 | tf_op jit(solution)/shard_map/all_to_all | solution.py:44
  149.0 5.5 %collective-permute-done.18.refs_2_.refs_4_ = bf16[128,1024]{1,0:T(8,128)(2,1)S(1)} collective-permute-done((bf16[128,1024]{1,0:T(8,128)(2,1)S(1)}, bf16[128,1024]{1,0:T(8,128)(2,1)S(1)}, u32[]{:S(2)}, u32[]{:S(2)}) %collective-permute-start.18) | collective-permute-done | bytes 262176 | tf_op jit(solution)/shard_map/ppermute | solution.py:35
  178.4 5.3 %shard_map.278 = (bf16[1024,512]{1,0:T(8,128)(2,1)}, bf16[1024,512]{1,0:T(8,128)(2,1)}) custom-call(s32[10]{0:T(128)} %stack.79.at, bf16[1024,1024]{1,0:T(8,128)(2,1)} %get-tuple-element.201.unit.refs_0_, bf16[1024,512]{1,0:T(8,128)(2,1)} %get-tuple-element.202.up, f32[8,512]{1,0:T(8,128)} %get-tuple-element.203.bias), custom_call_target="tpu_custom_call" | custom-call | flops 1000000000 | bytes 4000000 | tf_op jit(solution)/shard_map/pallas_call | solution.py:212
  183.7 7.3 %shard_map.279 = (bf16[1024,128]{1,0:T(8,128)(2,1)}, bf16[1024,128]{1,0:T(8,128)(2,1)}, bf16[1024,128]{1,0:T(8,128)(2,1)}, bf16[1024,128]{1,0:T(8,128)(2,1)}, bf...) custom-call(s32[16]{0:T(128)} %fusion.32.where_ref, bf16[1024,384]{1,0:T(8,128)(2,1)} %get-tuple-element.205.proj, ...), custom_call_target="tpu_custom_call" | custom-call | flops 4000000000 | bytes 4000000 | tf_op jit(solution)/shard_map/pallas_call | solution.py:212
  203.8 11.4 %shard_map.284 = (bf16[128,1024]{1,0:T(8,128)(2,1)}, bf16[128,1024]{1,0:T(8,128)(2,1)}, bf16[128,1024]{1,0:T(8,128)(2,1)}, bf16[128,1024]{1,0:T(8,128)(2,1)}, bf...) custom-call(s32[16]{0:T(128)} %fusion.32.where_ref, ...), custom_call_target="tpu_custom_call" | custom-call | flops 6000000000 | bytes 4000000 | tf_op jit(solution)/shard_map/pallas_call | solution.py:212
  226.0 7.1 %shard_map.286.refs_1_ = bf16[8,144,640]{2,1,0:T(8,128)(2,1)} custom-call(s32[10]{0:T(128)} %stack.79.at, bf16[1024,1024]{1,0:T(8,128)(2,1)} %shard_map.285.unit, bf16[1024,512]{1,0:T(8,128)(2,1)} %get-tuple-element.204.refs_4_.refs_0_, bf16[1024,128]{1,0:T(8,128)(2,1)} %get-tuple-element.206.refs_5_.refs_1_.mixed, ...), custom_call_target="tpu_custom_call" | custom-call | flops 1342177280 | bytes 4000000 | tf_op jit(solution)/shard_map/pallas_call | solution.py:212
  238.2 5.8 %shard_map.287.refs_2_.refs_9_ = bf16[8,144,896]{2,1,0:T(8,128)(2,1)} custom-call(s32[10]{0:T(128)} %stack.79.at, bf16[1024,1024]{1,0:T(8,128)(2,1)} %shard_map.285.unit, bf16[1024,512]{1,0:T(8,128)(2,1)} %get-tuple-element.214.grad_middle.refs_2_.refs_0_, bf16[1024,384]{1,0:T(8,128)(2,1)} %get-tuple-element.230.refs_1_), custom_call_target="tpu_custom_call" | custom-call | flops 1879048192 | bytes 4000000 | tf_op jit(solution)/shard_map/pallas_call | solution.py:212
  254.1 7.4 %collective-permute-start.45 = (bf16[128,1024]{1,0:T(8,128)(2,1)S(1)}, bf16[128,1024]{1,0:T(8,128)(2,1)S(1)}, u32[]{:S(2)}, u32[]{:S(2)}) collective-permute-start(bf16[128,1024]{1,0:T(8,128)(2,1)S(1)} %collective-permute-done.44.refs_6_), channel_id=1, source_target_pairs={{0,64},{1,65},{2,66},{3,67},{4,68},{5,69},{6,70},{7,71},{8,72},{9,... | collective-permute-start | bytes 786440 | tf_op jit(solution)/shard_map/ppermute | solution.py:35
  264.9 5.3 %all-to-all-start.6 = ((bf16[8,144,896]{2,1,0:T(8,128)(2,1)}), bf16[8,144,896]{2,1,0:T(8,128)(2,1)S(1)}, u32[]{:S(2)}, u32[]{:S(2)}) async-start(bf16[8,144,896]{2,1,0:T(8,128)(2,1)} %get-tuple-element.259), calls=%async_computation.6 | async-start | bytes 4128768 | tf_op jit(solution)/shard_map/all_to_all | solution.py:44
  280.7 8.9 %shard_map.292.refs_10_ = bf16[8,144,1152]{2,1,0:T(8,128)(2,1)} custom-call(s32[10]{0:T(128)} %stack.79.at, bf16[1024,1024]{1,0:T(8,128)(2,1)} %get-tuple-element.174.unit, bf16[1024,512]{1,0:T(8,128)(2,1)} %get-tuple-element.242.grad_middle.refs_0_.refs_3_, bf16[1024,512]{1,0:T(8,128)(2,1)} %get-tuple-element.187.active.refs_1_, ...), custom_call_target="tpu_custom_call" | custom-call | flops 2415919104 | bytes 4000000 | tf_op jit(solution)/shard_map/pallas_call | solution.py:212
  289.6 11.3 %shard_map.291 = (bf16[128,1024]{1,0:T(8,128)(2,1)}, bf16[128,1024]{1,0:T(8,128)(2,1)}, bf16[128,1024]{1,0:T(8,128)(2,1)}, bf16[128,1024]{1,0:T(8,128)(2,1)}, bf...) custom-call(s32[16]{0:T(128)} %fusion.32.where_ref, ...), custom_call_target="tpu_custom_call" | custom-call | flops 6000000000 | bytes 4000000 | tf_op jit(solution)/shard_map/pallas_call | solution.py:212
  311.6 6.1 %all-to-all-start.7 = ((bf16[8,144,1152]{2,1,0:T(8,128)(2,1)}), bf16[8,144,1152]{2,1,0:T(8,128)(2,1)S(1)}, u32[]{:S(2)}, u32[]{:S(2)}) async-start(bf16[8,144,1152]{2,1,0:T(8,128)(2,1)} %get-tuple-element.260), calls=%async_computation.7 | async-start | bytes 5308416 | tf_op jit(solution)/shard_map/all_to_all | solution.py:44
  353.3 7.4 %collective-permute-done.61.refs_5_ = bf16[144,1536]{1,0:T(8,128)(2,1)} collective-permute-done((bf16[144,1536]{1,0:T(8,128)(2,1)S(1)}, bf16[144,1536]{1,0:T(8,128)(2,1)}, u32[]{:S(2)}, u32[]{:S(2)}) %collective-permute-start.61) | collective-permute-done | bytes 442400 | tf_op jit(solution)/shard_map/ppermute | solution.py:35
  379.2 7.3 %collective-permute-done.65.refs_6_ = bf16[144,1152]{1,0:T(8,128)(2,1)S(1)} collective-permute-done((bf16[144,1152]{1,0:T(8,128)(2,1)}, bf16[144,1152]{1,0:T(8,128)(2,1)S(1)}, u32[]{:S(2)}, u32[]{:S(2)}) %collective-permute-start.65) | collective-permute-done | bytes 331808 | tf_op jit(solution)/shard_map/ppermute | solution.py:35
  386.6 7.0 %collective-permute-done.63.refs_3_ = bf16[144,1536]{1,0:T(8,128)(2,1)} collective-permute-done((bf16[144,1536]{1,0:T(8,128)(2,1)S(1)}, bf16[144,1536]{1,0:T(8,128)(2,1)}, u32[]{:S(2)}, u32[]{:S(2)}) %collective-permute-start.63) | collective-permute-done | bytes 442400 | tf_op jit(solution)/shard_map/ppermute | solution.py:35
  408.9 6.4 %all-to-all-start.9 = ((bf16[4,144,1536]{2,1,0:T(8,128)(2,1)}), bf16[4,144,1536]{2,1,0:T(8,128)(2,1)S(1)}, u32[]{:S(2)}, u32[]{:S(2)}) async-start(bf16[4,144,1536]{2,1,0:T(8,128)(2,1)} %broadcast_in_dim.27), calls=%async_computation.9 | async-start | bytes 3538944 | tf_op jit(solution)/shard_map/all_to_all | solution.py:44
  426.1 5.2 %collective-permute-done.68 = bf16[2,128,1024]{2,1,0:T(8,128)(2,1)} collective-permute-done((bf16[2,128,1024]{2,1,0:T(8,128)(2,1)}, bf16[2,128,1024]{2,1,0:T(8,128)(2,1)}, u32[]{:S(2)}, u32[]{:S(2)}) %collective-permute-start.68) | collective-permute-done | bytes 524320 | tf_op jit(solution)/shard_map/ppermute | solution.py:35
  447.0 7.9 %shard_map.301 = (f32[128,3072]{1,0:T(8,128)}, f32[128,4096]{1,0:T(8,128)}, f32[512,1024]{1,0:T(8,128)}, f32[128,1024]{1,0:T(8,128)}, f32[1,256]{1,0:T(1,128)}, ...) custom-call(s32[10]{0:T(128)} %stack.79.at, ...), custom_call_target="tpu_custom_call" | custom-call | bytes 4000000 | tf_op jit(solution)/shard_map/pallas_call | solution.py:212
  (433 shorter events, 279.6 us)
Async XLA Ops:
  17.2 24.8 %all-to-all-start = ((bf16[8,144,640]{2,1,0:T(8,128)(2,1)}), bf16[8,144,640]{2,1,0:T(8,128)(2,1)S(1)}, u32[]{:S(2)}, u32[]{:S(2)}) async-start(bf16[8,144,640]{2,1,0:T(8,128)(2,1)} %broadcast_in_dim.22), calls=%async_computation | async-start | bytes 2949120 | tf_op jit(solution)/shard_map/all_to_all | solution.py:44
  22.1 27.8 %collective-permute-start.9 = (bf16[128,1024]{1,0:T(8,128)(2,1)}, bf16[128,1024]{1,0:T(8,128)(2,1)}, u32[]{:S(2)}, u32[]{:S(2)}) collective-permute-start(bf16[128,1024]{1,0:T(8,128)(2,1)} %get-tuple-element.176), channel_id=1, source_target_pairs={{0,64},{1,65},{2,66},{3,67},{4,68},{5,69},{6,70},{7,71},{8,72},{9,... | collective-permute-start | bytes 786440 | tf_op jit(solution)/shard_map/ppermute | solution.py:35
  23.0 20.3 %collective-permute-start.6 = (bf16[128,1024]{1,0:T(8,128)(2,1)S(1)}, bf16[128,1024]{1,0:T(8,128)(2,1)S(1)}, u32[]{:S(2)}, u32[]{:S(2)}) collective-permute-start(bf16[128,1024]{1,0:T(8,128)(2,1)S(1)} %copy-done.45), channel_id=1, source_target_pairs={{0,16},{1,17},{2,18},{3,19},{4,20},{5,21},{6,22},{7,23},{8,24},{9,... | collective-permute-start | bytes 786440 | tf_op jit(solution)/shard_map/ppermute | solution.py:35
  24.2 19.1 %collective-permute-start.4 = (bf16[128,1024]{1,0:T(8,128)(2,1)S(1)}, bf16[128,1024]{1,0:T(8,128)(2,1)S(1)}, u32[]{:S(2)}, u32[]{:S(2)}) collective-permute-start(bf16[128,1024]{1,0:T(8,128)(2,1)S(1)} %copy-done.45), channel_id=1, source_target_pairs={{0,32},{1,33},{2,34},{3,35},{4,36},{5,37},{6,38},{7,39},{8,40},{9,... | collective-permute-start | bytes 786440 | tf_op jit(solution)/shard_map/ppermute | solution.py:35
  62.7 33.8 %all-to-all-start.2 = ((bf16[8,128,1024]{2,1,0:T(8,128)(2,1)}), bf16[8,128,1024]{2,1,0:T(8,128)(2,1)S(1)}, u32[]{:S(2)}, u32[]{:S(2)}) async-start(bf16[8,128,1024]{2,1,0:T(8,128)(2,1)} %broadcast_in_dim.23), calls=%async_computation.2 | async-start | bytes 4194304 | tf_op jit(solution)/shard_map/all_to_all | solution.py:44
  115.8 41.9 %all-to-all-start.3 = ((bf16[8,144,896]{2,1,0:T(8,128)(2,1)}), bf16[8,144,896]{2,1,0:T(8,128)(2,1)S(1)}, u32[]{:S(2)}, u32[]{:S(2)}) async-start(bf16[8,144,896]{2,1,0:T(8,128)(2,1)} %broadcast_in_dim.25), calls=%async_computation.3 | async-start | bytes 4128768 | tf_op jit(solution)/shard_map/all_to_all | solution.py:44
  142.9 27.3 %collective-permute-start.24 = (bf16[128,1024]{1,0:T(8,128)(2,1)S(1)}, bf16[128,1024]{1,0:T(8,128)(2,1)}, u32[]{:S(2)}, u32[]{:S(2)}) collective-permute-start(bf16[128,1024]{1,0:T(8,128)(2,1)S(1)} %get-tuple-element.332.refs_0_), channel_id=1, source_target_pairs={{0,64},{1,65},{2,66},{3,67},{4,68},{5,69},{6,70},{7,71},{8,72},{9,... | collective-permute-start | bytes 786440 | tf_op jit(solution)/shard_map/ppermute | solution.py:35
  147.3 25.5 %collective-permute-start.27 = (bf16[128,1024]{1,0:T(8,128)(2,1)S(1)}, bf16[128,1024]{1,0:T(8,128)(2,1)}, u32[]{:S(2)}, u32[]{:S(2)}) collective-permute-start(bf16[128,1024]{1,0:T(8,128)(2,1)S(1)} %collective-permute-done.19.refs_3_.refs_6_), channel_id=1, source_target_pairs={{0,64},{1,65},{2,66},{3,67},{4,68},{5,69},{6,70},{7,71},{8,72},{9,... | collective-permute-start | bytes 786440 | tf_op jit(solution)/shard_map/ppermute | solution.py:35
  154.5 18.9 %collective-permute-start.26 = (bf16[128,1024]{1,0:T(8,128)(2,1)S(1)}, bf16[128,1024]{1,0:T(8,128)(2,1)}, u32[]{:S(2)}, u32[]{:S(2)}) collective-permute-start(bf16[128,1024]{1,0:T(8,128)(2,1)S(1)} %collective-permute-done.18.refs_2_.refs_4_), channel_id=1, source_target_pairs={{0,64},{1,65},{2,66},{3,67},{4,68},{5,69},{6,70},{7,71},{8,72},{9,... | collective-permute-start | bytes 786440 | tf_op jit(solution)/shard_map/ppermute | solution.py:35
  161.0 33.0 %all-to-all-start.4 = ((bf16[8,128,512]{2,1,0:T(8,128)(2,1)}), bf16[8,128,512]{2,1,0:T(8,128)(2,1)S(1)}, u32[]{:S(2)}, u32[]{:S(2)}) async-start(bf16[8,128,512]{2,1,0:T(8,128)(2,1)} %broadcast_in_dim.26), calls=%async_computation.4 | async-start | bytes 2097152 | tf_op jit(solution)/shard_map/all_to_all | solution.py:44
  166.2 24.8 %collective-permute-start.23 = (bf16[128,1024]{1,0:T(8,128)(2,1)S(1)}, bf16[128,1024]{1,0:T(8,128)(2,1)S(1)}, u32[]{:S(2)}, u32[]{:S(2)}) collective-permute-start(bf16[128,1024]{1,0:T(8,128)(2,1)S(1)} %pad_maximum_fusion.8.refs_0_), channel_id=1, source_target_pairs={{0,16},{1,17},{2,18},{3,19},{4,20},{5,21},{6,22},{7,23},{8,24},{9,... | collective-permute-start | bytes 786440 | tf_op jit(solution)/shard_map/ppermute | solution.py:35
  170.2 20.7 %collective-permute-start.22 = (bf16[128,1024]{1,0:T(8,128)(2,1)S(1)}, bf16[128,1024]{1,0:T(8,128)(2,1)S(1)}, u32[]{:S(2)}, u32[]{:S(2)}) collective-permute-start(bf16[128,1024]{1,0:T(8,128)(2,1)S(1)} %pad_maximum_fusion.8.refs_0_), channel_id=1, source_target_pairs={{0,32},{1,33},{2,34},{3,35},{4,36},{5,37},{6,38},{7,39},{8,40},{9,... | collective-permute-start | bytes 786440 | tf_op jit(solution)/shard_map/ppermute | solution.py:35
  218.2 25.9 %collective-permute-start.36 = (bf16[128,1024]{1,0:T(8,128)(2,1)S(1)}, bf16[128,1024]{1,0:T(8,128)(2,1)S(1)}, u32[]{:S(2)}, u32[]{:S(2)}) collective-permute-start(bf16[128,1024]{1,0:T(8,128)(2,1)S(1)} %add_convert_fusion.10.refs_2_), channel_id=1, source_target_pairs={{0,16},{1,17},{2,18},{3,19},{4,20},{5,21},{6,22},{7,23},{8,24},{9,... | collective-permute-start | bytes 786440 | tf_op jit(solution)/shard_map/ppermute | solution.py:35
  221.0 23.1 %collective-permute-start.37 = (bf16[128,1024]{1,0:T(8,128)(2,1)S(1)}, bf16[128,1024]{1,0:T(8,128)(2,1)S(1)}, u32[]{:S(2)}, u32[]{:S(2)}) collective-permute-start(bf16[128,1024]{1,0:T(8,128)(2,1)S(1)} %add_convert_fusion.9.refs_3_), channel_id=1, source_target_pairs={{0,32},{1,33},{2,34},{3,35},{4,36},{5,37},{6,38},{7,39},{8,40},{9,... | collective-permute-start | bytes 786440 | tf_op jit(solution)/shard_map/ppermute | solution.py:35
  222.8 21.3 %collective-permute-start.38 = (bf16[128,1024]{1,0:T(8,128)(2,1)S(1)}, bf16[128,1024]{1,0:T(8,128)(2,1)}, u32[]{:S(2)}, u32[]{:S(2)}) collective-permute-start(bf16[128,1024]{1,0:T(8,128)(2,1)S(1)} %add_convert_fusion.8.refs_4_), channel_id=1, source_target_pairs={{0,48},{1,49},{2,50},{3,51},{4,52},{5,53},{6,54},{7,55},{8,56},{9,... | collective-permute-start | bytes 786440 | tf_op jit(solution)/shard_map/ppermute | solution.py:35
  233.1 30.5 %all-to-all-start.5 = ((bf16[8,144,640]{2,1,0:T(8,128)(2,1)}), bf16[8,144,640]{2,1,0:T(8,128)(2,1)S(1)}, u32[]{:S(2)}, u32[]{:S(2)}) async-start(bf16[8,144,640]{2,1,0:T(8,128)(2,1)} %shard_map.286.refs_1_), calls=%async_computation.5 | async-start | bytes 2949120 | tf_op jit(solution)/shard_map/all_to_all | solution.py:44
  264.9 36.1 %all-to-all-start.6 = ((bf16[8,144,896]{2,1,0:T(8,128)(2,1)}), bf16[8,144,896]{2,1,0:T(8,128)(2,1)S(1)}, u32[]{:S(2)}, u32[]{:S(2)}) async-start(bf16[8,144,896]{2,1,0:T(8,128)(2,1)} %get-tuple-element.259), calls=%async_computation.6 | async-start | bytes 4128768 | tf_op jit(solution)/shard_map/all_to_all | solution.py:44
  271.8 50.2 %collective-permute-start.60 = (bf16[128,128]{1,0:T(8,128)(2,1)S(1)}, bf16[128,128]{1,0:T(8,128)(2,1)S(1)}, u32[]{:S(2)}, u32[]{:S(2)}) collective-permute-start(bf16[128,128]{1,0:T(8,128)(2,1)S(1)} %slice.124), channel_id=1, source_target_pairs={{0,0},{1,64},{2,16},{3,80},{4,32},{5,96},{6,48},{7,112},{8,8},{9,7... | collective-permute-start | bytes 98312 | tf_op jit(solution)/shard_map/ppermute | solution.py:35
  311.6 49.0 %all-to-all-start.7 = ((bf16[8,144,1152]{2,1,0:T(8,128)(2,1)}), bf16[8,144,1152]{2,1,0:T(8,128)(2,1)S(1)}, u32[]{:S(2)}, u32[]{:S(2)}) async-start(bf16[8,144,1152]{2,1,0:T(8,128)(2,1)} %get-tuple-element.260), calls=%async_computation.7 | async-start | bytes 5308416 | tf_op jit(solution)/shard_map/all_to_all | solution.py:44
  332.1 28.5 %collective-permute-start.61 = (bf16[144,1536]{1,0:T(8,128)(2,1)S(1)}, bf16[144,1536]{1,0:T(8,128)(2,1)}, u32[]{:S(2)}, u32[]{:S(2)}) collective-permute-start(bf16[144,1536]{1,0:T(8,128)(2,1)S(1)} %pad_maximum_fusion.4.refs_4_), channel_id=1, source_target_pairs={{0,8},{1,9},{2,10},{3,11},{4,12},{5,13},{6,14},{7,15},{8,0},{9,1},... | collective-permute-start | bytes 1327112 | tf_op jit(solution)/shard_map/ppermute | solution.py:35
  362.2 31.4 %all-to-all-start.8 = ((bf16[8,144,384]{2,1,0:T(8,128)(2,1)}), bf16[8,144,384]{2,1,0:T(8,128)(2,1)}, u32[]{:S(2)}, u32[]{:S(2)}) async-start(bf16[8,144,384]{2,1,0:T(8,128)(2,1)} %get-tuple-element.283), calls=%async_computation.8 | async-start | bytes 1769472 | tf_op jit(solution)/shard_map/all_to_all | solution.py:44
  371.1 22.4 %collective-permute-start.63 = (bf16[144,1536]{1,0:T(8,128)(2,1)S(1)}, bf16[144,1536]{1,0:T(8,128)(2,1)}, u32[]{:S(2)}, u32[]{:S(2)}) collective-permute-start(bf16[144,1536]{1,0:T(8,128)(2,1)S(1)} %add_convert_fusion.refs_1_), channel_id=1, source_target_pairs={{0,32},{1,33},{2,34},{3,35},{4,36},{5,37},{6,38},{7,39},{8,40},{9,... | collective-permute-start | bytes 1327112 | tf_op jit(solution)/shard_map/ppermute | solution.py:35
  373.6 19.9 %collective-permute-start.62 = (bf16[144,1536]{1,0:T(8,128)(2,1)S(1)}, bf16[144,1536]{1,0:T(8,128)(2,1)}, u32[]{:S(2)}, u32[]{:S(2)}) collective-permute-start(bf16[144,1536]{1,0:T(8,128)(2,1)S(1)} %add_convert_fusion.refs_1_), channel_id=1, source_target_pairs={{0,48},{1,49},{2,50},{3,51},{4,52},{5,53},{6,54},{7,55},{8,56},{9,... | collective-permute-start | bytes 1327112 | tf_op jit(solution)/shard_map/ppermute | solution.py:35
  408.9 28.4 %all-to-all-start.9 = ((bf16[4,144,1536]{2,1,0:T(8,128)(2,1)}), bf16[4,144,1536]{2,1,0:T(8,128)(2,1)S(1)}, u32[]{:S(2)}, u32[]{:S(2)}) async-start(bf16[4,144,1536]{2,1,0:T(8,128)(2,1)} %broadcast_in_dim.27), calls=%async_computation.9 | async-start | bytes 3538944 | tf_op jit(solution)/shard_map/all_to_all | solution.py:44
  (141 other events, 1478.6 us)

commit v3 on v2

--- a/solution.py
+++ b/solution.py
@@ -106,7 +106,7 @@
 
 
 def unit_rows(where_ref, m):
-    return pl.ds(pl.multiple_of(where_ref[m] * UNIT, UNIT), UNIT)
+    return pl.ds(pl.multiple_of(where_ref[WHERE + m] * UNIT, UNIT), UNIT)
 
 
 def attend(where_ref, proj_ref, tables, mixed_ref, q_ref, k_ref, v_ref, o_ref, lse_ref):
@@ -207,20 +207,24 @@
     return jax.tree.unflatten(tree, flat)
 
 
-def run(body, scalars, arrays, outs, scratch=(), flops=0, bytes_accessed=4_000_000, spaces=None, limit=60):
-    vmem = pl.BlockSpec(memory_space=pltpu.VMEM)
+def run(body, scalars, arrays, outs, scratch=(), flops=0, spaces=None, others=()):
+    vmem, anywhere = pl.BlockSpec(memory_space=pltpu.VMEM), pl.BlockSpec(memory_space=pl.ANY)
+    others = jax.tree.leaves(others)
+    count = 1 + len(arrays)
     return pl.pallas_call(
-        body,
+        lambda *refs: body(*refs[:count], *refs[count + len(others) :]),
         out_shape=[jax.ShapeDtypeStruct(*out) for out in outs],
-        in_specs=[pl.BlockSpec(memory_space=pltpu.SMEM)] + (spaces or [vmem] * len(arrays)),
+        in_specs=[pl.BlockSpec(memory_space=pltpu.SMEM)]
+        + (spaces or [vmem] * len(arrays))
+        + [anywhere] * len(others),
         out_specs=[vmem] * len(outs),
         scratch_shapes=list(scratch),
-        compiler_params=pltpu.CompilerParams(vmem_limit_bytes=limit * 1024 * 1024),
-        cost_estimate=pl.CostEstimate(flops=flops, bytes_accessed=bytes_accessed, transcendentals=0),
-    )(scalars, *arrays)
-
-
-X, CORE, ZH, Y, ZL, PART, SHARD, BIAS = 0, 1, 2, 3, 4, 5, 6, 7
+        compiler_params=pltpu.CompilerParams(vmem_limit_bytes=60 * 1024 * 1024),
+        cost_estimate=pl.CostEstimate(flops=flops, bytes_accessed=4_000_000, transcendentals=0),
+    )(scalars, *arrays, *others)
+
+
+X, CORE, ZH, Y, ZL, PART, SHARD, BIAS, WHERE = 0, 1, 2, 3, 4, 5, 6, 7, 10
 
 
 def lanes(start, extent=128):
@@ -237,6 +241,10 @@
         jnp.where(low, first, pltpu.roll(second, 64, 1)),
         jnp.where(low, pltpu.roll(first, 64, 1), second),
     )
+
+
+def block_rows(number, extent):
+    return pl.ds(pl.multiple_of(extent * number, extent), extent)
 
 
 def column(row):
@@ -341,20 +349,6 @@
     up_turned[...] = jnp.transpose(up[...])
 
 
-def prepare_qkv_kernel(at, messages, *refs):
-    prepare_qkv(at, [(k, messages.at[k]) for k in range(8)], *refs)
-
-
-def prepare_rest_kernel(at, messages, vectors, up, up_turned, bias, down, down_turned):
-    prepare_up(at, [(k, messages.at[k]) for k in range(8)], vectors, up, up_turned, bias)
-    prepare_down([messages.at[k, :, 512:] for k in range(8)], down, down_turned)
-
-
-def prepare_wide_kernel(at, messages, *outs):
-    prepare_qkv(at, [(k, messages.at[k]) for k in range(8)], *outs[:5])
-    prepare_up(at, [(k, messages.at[k, :, 384:]) for k in range(8)], *outs[4:])
-
-
 def prepare_down(blocks, down, down_turned):
     for k, halves in enumerate(blocks):
         down[64 * k : 64 * k + 64, :512] = halves[:64, :]
@@ -362,17 +356,7 @@
     down_turned[...] = jnp.transpose(down[...])
 
 
-def prepare_down_kernel(at, messages, down, down_turned):
-    prepare_down([messages.at[k] for k in range(8)], down, down_turned)
-
-
-QKV = [((1024, 384), BF), ((384, 1024), BF), ((8, 384), F32), ((8, 1024), F32), ((128, 128), F32)]
-UP = [((1024, 512), BF), ((512, 1024), BF), ((8, 512), F32)]
-DOWN = [((512, 1024), BF), ((1024, 512), BF)]
-
-
-def norm_kernel(at, *refs):
-    blocks, wide, bias, unit, proj = refs[:8], *refs[8:]
+def project_rows(blocks, qkv, bias, unit, proj):
     for k in range(8):
         values = blocks[k][...].astype(F32)
         centred = values - jnp.mean(values, axis=-1, keepdims=True)
@@ -380,10 +364,10 @@
         unit[128 * k : 128 * k + 128, :] = (centred * lax.rsqrt(spread + NORM_EPS)).astype(BF)
     for k in range(4):
         here = slice(256 * k, 256 * k + 256)
-        proj[here, :] = (dot(unit[here, :], wide[...]) + bias[:1, :]).astype(BF)
-
-
-def up_kernel(at, unit, up, bias, active, slope):
+        proj[here, :] = (dot(unit[here, :], qkv[...]) + bias[:1, :]).astype(BF)
+
+
+def activate(unit, up, bias, active, slope):
     for k in range(4):
         here = slice(256 * k, 256 * k + 256)
         middle = dot(unit[here, :], up[...]) + bias[:1, :]
@@ -393,14 +377,36 @@
         slope[here, :] = (share + middle * density).astype(BF)
 
 
-def attend_kernel(where_ref, proj, cosine, low, high, begin, mixed, *kept):
-    attend(where_ref, proj, (cosine, low, high, begin), mixed, *kept)
-
-
-def project_kernel(at, active, mixed, down, dense_parts, *refs):
-    blocks, dense = refs[:8], refs[8]
-    for k in range(8):
-        dense[:, 128 * k : 128 * k + 128] = dense_parts[k]
+def attend_first_kernel(at, *refs):
+    blocks, messages, tables, outs = refs[:8], refs[8], refs[9:13], refs[13:]
+    qkv_turned, bias_out, vectors, unit, mixed, *kept = outs[:10]
+    qkv, bias, proj = outs[10:]
+    prepare_qkv(at, [(k, messages.at[k]) for k in range(8)], qkv, qkv_turned, bias, bias_out, vectors)
+    project_rows(blocks, qkv, bias, unit, proj)
+    attend(at, proj, tables, mixed, *kept)
+
+
+def attend_second_kernel(at, *refs):
+    blocks, messages, tables, outs = refs[:8], refs[8], refs[9:13], refs[13:]
+    qkv_turned, bias_out, up_turned, active, slope, unit, mixed, *kept = outs[:12]
+    qkv, bias, proj, vectors, up, up_bias = outs[12:]
+    prepare_qkv(at, [(k, messages.at[k]) for k in range(8)], qkv, qkv_turned, bias, bias_out, vectors)
+    prepare_up(at, [(k, messages.at[k, :, 384:]) for k in range(8)], vectors, up, up_turned, up_bias)
+    project_rows(blocks, qkv, bias, unit, proj)
+    activate(unit, up, up_bias, active, slope)
+    attend(at, proj, tables, mixed, *kept)
+
+
+def dense_parts_of(at, parts, layer):
+    for r in range(4):
+        for beside in range(2):
+            part = 2 * ((at[X] + 4 - r) % 4) + (at[CORE] + beside) % 2
+            yield part, parts[beside, r, :, 128 * layer : 128 * layer + 128]
+
+
+def project(at, layer, active, mixed, down, dense_parts, dense, blocks):
+    for part, columns in dense_parts_of(at, dense_parts, layer):
+        dense[:, lanes(128 * part)] = columns
     for k in (2, 1, 3, 0):
         here = slice(256 * k, 256 * k + 256)
         out = dot(active[here, :], down[...]) + dot(mixed[here, :], dense[...])
@@ -408,15 +414,37 @@
         blocks[2 * k + 1][...] = out[128:].astype(BF)
 
 
-def back_front_kernel(at, *refs):
-    blocks, down_turned, dense_parts, slope, grad_middle, grad_mixed, dense_turned = refs[:8], *refs[8:]
-    for k in range(8):
-        dense_turned[128 * k : 128 * k + 128, :] = jnp.transpose(dense_parts[k])
+def rest_first_kernel(at, messages, vectors, unit, mixed, dense_parts, up_turned, down_turned, active, slope, *refs):
+    blocks, (up, bias, down, dense) = refs[:8], refs[8:]
+    prepare_up(at, [(k, messages.at[k]) for k in range(8)], vectors, up, up_turned, bias)
+    prepare_down([messages.at[k, :, 512:] for k in range(8)], down, down_turned)
+    activate(unit, up, bias, active, slope)
+    project(at, 0, active, mixed, down, dense_parts, dense, blocks)
+
+
+def project_kernel(at, active, mixed, down, dense_parts, *refs):
+    project(at, 1, active, mixed, down, dense_parts, refs[8], refs[:8])
+
+
+def pull_back(at, layer, blocks, down_turned, dense_parts, slope, grad_middle, grad_mixed, dense_turned):
+    for part, columns in dense_parts_of(at, dense_parts, layer):
+        dense_turned[block_rows(part, 128), :] = jnp.transpose(columns)
     for k in range(8):
         here = slice(128 * k, 128 * k + 128)
         rows = blocks[k][...]
         grad_middle[here, :] = (dot(rows, down_turned[...]) * slope[here, :].astype(F32)).astype(BF)
         grad_mixed[here, :] = dot(rows, dense_turned[...]).astype(BF)
+
+
+def back_second_kernel(at, *refs):
+    rows, (messages, dense_parts, slope), qkv_turned, up_turned = refs[:8], refs[8:11], refs[11], refs[12]
+    tables, kept, blocks = refs[13:17], refs[17:22], refs[22:30]
+    grad_proj, grad_middle, down, down_turned, dense_turned, grad_mixed, *scratch = refs[30:]
+    prepare_down([messages.at[k] for k in range(8)], down, down_turned)
+    pull_back(at, 1, rows, down_turned, dense_parts, slope, grad_middle, grad_mixed, dense_turned)
+    back_attend_kernel(
+        at, grad_mixed, grad_middle, qkv_turned, up_turned, *tables, *kept, *blocks, grad_proj, *scratch
+    )
 
 
 def back_attend_kernel(where_ref, grad_mixed, grad_middle, wide_turned, up_turned, cosine, low, high, begin, *refs):
@@ -431,38 +459,32 @@
         blocks[2 * k + 1][...] = out[128:].astype(BF)
 
 
-def shard_at(at, step, beside):
-    return 2 * ((at[Y] + step) % 4) + (at[ZL] + beside) % 2
-
-
-def weight_terms(at, unit, grads, outward=None, order=None):
-    extent = sum(grad.shape[1] for grad in grads)
+def weight_terms(at, unit, grads, outward=None, pulled=None, others=()):
+    extent = 512 if pulled else sum(grad.shape[1] for grad in grads)
     start = 640 if outward else 0
-    arrays = (unit, *grads)
-    scratch = []
-    counts = {None: (1, 8), "y": (4, 2), "z": (2, 4)}[order]
-    shapes = [((counts[1], 144, start + extent), BF)] * counts[0]
+    arrays, scratch, outs = (unit, *grads), [], [((8, 144, start + extent), BF)]
     if outward:
-        active, mixed, rows, grad_middle = outward
-        arrays = (*arrays, active, mixed, grad_middle, *rows)
+        active, mixed, rows, *grad_middle = outward
+        arrays = (*arrays, active, mixed, *rows, *grad_middle)
         scratch = [pltpu.VMEM((512, 1024), F32), pltpu.VMEM((128, 1024), F32)]
+    if pulled:
+        arrays = (*arrays, *pulled)
+        outs += [((1024, 512), BF), ((1024, 128), BF)]
+        scratch.append(pltpu.VMEM((1024, 128), BF))
 
     def body(at, unit, *refs):
         grad_refs, refs = refs[: len(grads)], refs[len(grads) :]
+        if pulled:
+            (active, mixed), rows, refs = refs[:2], refs[2:10], refs[10:]
+            (down_turned, dense_parts, slope), (out, grad_middle, grad_mixed) = refs[:3], refs[3:6]
+            down, dense, dense_turned = refs[6:]
+            pull_back(at, 0, rows, down_turned, dense_parts, slope, grad_middle, grad_mixed, dense_turned)
+            grad_refs = (grad_middle,)
+        elif outward:
+            (active, mixed), rows, grad_middle, out, (down, dense) = refs[:2], refs[2:10], refs[10], refs[11], refs[12:]
+        else:
+            out = refs[0]
         if outward:
-            (active, mixed, grad_middle), rows, refs = refs[:3], refs[3:11], refs[11:]
-        outs, refs = refs[: len(shapes)], refs[len(shapes) :]
-        places = []
-        for step in range(4):
-            for beside in range(2):
-                if order == "y":
-                    places.append((outs[step].at[beside], shard_at(at, step, beside)))
-                elif order == "z":
-                    places.append((outs[beside].at[step], shard_at(at, step, beside)))
-                else:
-                    places.append((outs[0].at[2 * step + beside], 2 * step + beside))
-        if outward:
-            down, dense = refs
             sums = jnp.zeros((1, 128), F32)
             for k in range(8):
                 here = slice(128 * k, 128 * k + 128)
@@ -477,55 +499,47 @@
                     dense[...] += more_dense
                 sums = sums + jnp.sum(rows[k][:, lanes(128 * at[PART])].astype(F32), axis=0, keepdims=True)
             sums_up = jnp.sum(grad_middle[...].astype(F32), axis=0, keepdims=True)
-            for place, shard in places:
-                piece = down[pl.ds(pl.multiple_of(64 * shard, 64), 64), :].astype(BF)
-                place[:64, :512] = piece[:, :512]
-                place[64:128, :512] = piece[:, 512:]
-                place[:128, 512:640] = dense[:, lanes(128 * shard)].astype(BF)
-                place[128:, :128] = jnp.broadcast_to(sums, (16, 128)).astype(BF)
-                place[128:, 128:640] = jnp.broadcast_to(sums_up, (16, 512)).astype(BF)
+            for shard in range(8):
+                for half in range(2):
+                    piece = down[64 * shard : 64 * shard + 64, 512 * half : 512 * half + 512]
+                    out[shard, 64 * half : 64 * half + 64, :512] = piece.astype(BF)
+                out[shard, :128, 512:640] = dense[:, 128 * shard : 128 * shard + 128].astype(BF)
+                out[shard, 128:, :128] = jnp.broadcast_to(sums, (16, 128)).astype(BF)
+                out[shard, 128:, 128:640] = jnp.broadcast_to(sums_up, (16, 512)).astype(BF)
         at_column = start
         for grad in grad_refs:
             columns = grad.shape[1]
             here = slice(at_column, at_column + columns)
             sums = jnp.sum(grad[...].astype(F32), axis=0, keepdims=True)
-            for place, shard in places:
-                terms = dot_left(unit[:, lanes(128 * shard)], grad[...])
-                place[:128, here] = terms.astype(BF)
-                place[128:, here] = jnp.broadcast_to(sums, (16, columns)).astype(BF)
+            for shard in range(8):
+                terms = dot_left(unit[:, 128 * shard : 128 * shard + 128], grad[...])
+                out[shard, :128, here] = terms.astype(BF)
+                out[shard, 128:, here] = jnp.broadcast_to(sums, (16, columns)).astype(BF)
             at_column += columns
 
-    outs = run(body, at, arrays, shapes, scratch, flops=2 * 1024 * 1024 * (extent + start))
-    return outs if order else outs[0]
+    outs = run(body, at, arrays, outs, scratch, flops=2 * 1024 * 1024 * (extent + start), others=others)
+    return outs if pulled else outs[0]
 
 
 def final_kernel(at, *refs):
-    firsts, seconds = refs[:2], refs[2:10]
-    qkv, up, gain_one, shift_one, gain_two, shift_two = refs[10:16]
-    grad_qkv, grad_up, grad_down, grad_dense = refs[16:20]
-    bias_qk, bias_v, bias_up, bias_out, gain_a, shift_a, gain_b, shift_b = refs[20:28]
-    sums, sums_qkv, sums_up, sums_out, sems = refs[28:]
+    sources = refs[:8], refs[8:16]
+    qkv, up, gain_one, shift_one, gain_two, shift_two = refs[16:22]
+    grad_qkv, grad_up, grad_down, grad_dense = refs[22:26]
+    bias_qk, bias_v, bias_up, bias_out, gain_a, shift_a, gain_b, shift_b = refs[26:34]
+    sums, sums_qkv, sums_up, sums_out, sems = refs[34:]
     x, core, shard = at[X], at[CORE], at[SHARD]
-
-    @pl.when(core == 0)
-    def _():
-        copies = [pltpu.make_async_copy(firsts[k], sums.at[k], sems.at[k]) for k in range(2)]
-        for copy in copies:
-            copy.start()
-        for copy in copies:
-            copy.wait()
-
-    @pl.when(core == 1)
-    def _():
-        copies = []
-        for k in range(2):
-            for r in range(4):
-                target = sums.at[k, (x + r) % 4]
-                copies.append(pltpu.make_async_copy(seconds[4 * k + r], target, sems.at[len(copies)]))
-        for copy in copies:
-            copy.start()
-        for copy in copies:
-            copy.wait()
+    for layer in range(2):
+
+        @pl.when(core == layer)
+        def _():
+            copies = []
+            for k in range(8):
+                target = sums.at[k // 4, (x + k % 4) % 4]
+                copies.append(pltpu.make_async_copy(sources[layer][k], target, sems.at[k]))
+            for copy in copies:
+                copy.start()
+            for copy in copies:
+                copy.wait()
 
     def whole(beside, r, columns):
         return sums[beside, r, :128, columns].astype(F32)
@@ -639,13 +653,15 @@
         + jnp.bitwise_xor(unit_no % 2, core) * 2
         + jnp.bitwise_xor((unit_no // 2) % 2, zh)
     ).astype(jnp.int32)
-
-    def own_rows(array):
-        own = lax.dynamic_slice_in_dim(pick(array, zh), core * UNIT, UNIT, 0)
-        lent = lax.dynamic_slice_in_dim(pick(array, 1 - zh), core * UNIT, UNIT, 0)
-        return jnp.concatenate([own, across_high(lent)], axis=0)
-
-    own_tokens = own_rows(tokens)
+    at = jnp.concatenate([at, where])
+
+    own, lent = [], []
+    for array in (tokens, cotangent):
+        own.append(lax.dynamic_slice_in_dim(pick(array, zh), core * UNIT, UNIT, 0))
+        lent.append(lax.dynamic_slice_in_dim(pick(array, 1 - zh), core * UNIT, UNIT, 0))
+    lent = across_high(jnp.stack(lent))
+    own_tokens = jnp.concatenate([own[0], lent[0]], axis=0)
+    own_cotangent = jnp.concatenate([own[1], lent[1]], axis=0)
 
     sliced = run(
         slice_kernel,
@@ -685,108 +701,115 @@
         [((LENGTH, 128), F32)] * 3 + [((LENGTH, 128), jnp.int32)],
     )
 
-    def front(rows, wide, bias):
-        return run(
-            norm_kernel, at, (*rows, wide, bias), [((1024, 1024), BF), ((1024, 384), BF)], flops=1_000_000_000
-        )
-
-    def front_up(unit, up, bias):
-        return run(up_kernel, at, (unit, up, bias), [((1024, 512), BF)] * 2, flops=1_000_000_000)
-
-    def attention(proj):
-        outs = run(
-            attend_kernel,
-            where,
-            (proj, *tables),
-            [((1024, 128), BF)] * 5 + [((1024, 128), F32)],
-            flops=4_000_000_000,
-        )
-        return outs[0], outs[1:]
-
-    def project(active, mixed, down, dense):
-        return run(
-            project_kernel,
-            at,
-            (active, mixed, down, dense),
-            [((128, 1024), BF)] * 8,
-            [pltpu.VMEM((128, 1024), BF)],
-            flops=1_500_000_000,
-        )
-
-    def back_front(rows, down_turned, dense, slope):
-        return run(
-            back_front_kernel,
-            at,
-            (*rows, down_turned, dense, slope),
-            [((1024, 512), BF), ((1024, 128), BF)],
-            [pltpu.VMEM((1024, 128), BF)],
-            flops=1_500_000_000,
-        )
+    big, head = ((1024, 1024), BF), ((1024, 128), BF)
+    kept_outs = [head] * 4 + [((1024, 128), F32)]
+    qkv_scratch = [pltpu.VMEM((1024, 384), BF), pltpu.VMEM((8, 384), F32), pltpu.VMEM((1024, 384), BF)]
+    grad_scratch = [pltpu.VMEM((1024, 128), BF)] + [pltpu.VMEM((1024, 128), F32)] * 3
+    hidden_outs = [((1024, 512), BF)] * 2
+    block_outs = [((128, 1024), BF)] * 8
+    qkv_outs = [((384, 1024), BF), ((8, 1024), F32)]
 
     def back_attend(grad_mixed, grad_middle, qkv_turned, up_turned, kept):
         outs = run(
             back_attend_kernel,
-            where,
+            at,
             (grad_mixed, grad_middle, qkv_turned, up_turned, *tables, *kept),
             [((128, 1024), BF)] * 8 + [((1024, 384), BF)],
-            [pltpu.VMEM((1024, 128), BF)] + [pltpu.VMEM((1024, 128), F32)] * 3,
+            grad_scratch,
             flops=6_000_000_000,
         )
         return outs[:8], outs[8]
 
     qkvs = from_all(after(qkv, own_tokens), SHARDS)
     rows_one = gather_rows(own_tokens)
-    qkv_one, qkv_turned_one, qkv_bias, bias_out_one, vectors = run(prepare_qkv_kernel, at, (qkvs,), QKV)
-    dense = jnp.stack([qkvs[:, :128, 384:512], qkvs[:, :128, 512:]], axis=1)
-    dense = swapped(after(dense, rows_one[2::2]), ("x", "core"))
-    dense_one, dense_two = dense[:, 0], dense[:, 1]
-    rests = from_all(after(rest, dense_one, dense_two), SHARDS)
-    unit_one, proj = front(rows_one, qkv_one, qkv_bias)
-    mixed_one, kept_one = attention(proj)
-    rests, wide_two = after((rests, wide_two), mixed_one)
-
-    up_one, up_turned_one, up_bias, down_one, down_turned_one = run(
-        prepare_rest_kernel, at, (rests, vectors), UP + DOWN
-    )
-    active_one, slope_one = front_up(unit_one, up_one, up_bias)
+    rests = from_all(after(rest, qkvs, rows_one[2::2]), SHARDS)
+    held = [lax.dynamic_slice(qkvs, (2 * ((x + r) % 4), 0, 384), (2, 128, 256)) for r in range(4)]
+    held = [held[0]] + [along_x(held[r], r) for r in (1, 2, 3)]
+    dense = jnp.stack([pick(block, core) for block in held])
+    dense = jnp.stack([dense, across_cores(jnp.stack([pick(block, 1 - core) for block in held]))])
+    qkv_turned_one, bias_out_one, vectors, unit_one, mixed_one, *kept_one = run(
+        attend_first_kernel,
+        at,
+        (*rows_one, qkvs, *tables),
+        qkv_outs + [((128, 128), F32), big, head] + kept_outs,
+        qkv_scratch,
+        flops=5_000_000_000,
+    )
+    rests, wide_two, dense = after((rests, wide_two, dense), mixed_one)
+
     wides = from_all(after(wide_two, rests), SHARDS)
-    blocks = project(active_one, mixed_one, down_one, dense_one)
+    up_turned_one, down_turned_one, active_one, slope_one, *blocks = run(
+        rest_first_kernel,
+        at,
+        (rests, vectors, unit_one, mixed_one, dense),
+        [((512, 1024), BF), ((1024, 512), BF)] + hidden_outs + block_outs,
+        [
+            pltpu.VMEM((1024, 512), BF),
+            pltpu.VMEM((8, 512), F32),
+            pltpu.VMEM((512, 1024), BF),
+            pltpu.VMEM((128, 1024), BF),
+        ],
+        flops=3_000_000_000,
+    )
     joined = joined_cores(blocks)
     hidden_one = own_tokens.astype(F32) + joined_chips(joined) + bias_out_one[:1, :]
     hidden_one = hidden_one.astype(BF)
     rows_two = gather_rows(hidden_one)
     downs = from_all(after(down_two, wides), SHARDS)
-    own_cotangent = own_rows(after(cotangent, rows_two[2::2]))
-    qkv_two, qkv_turned_two, qkv_bias, bias_out_two, _, up_two, up_turned_two, up_bias = run(
-        prepare_wide_kernel, at, (wides,), QKV + UP
-    )
+    own_cotangent = after(own_cotangent, rows_two[2::2])
 
     grad_own = [own_cotangent] + [along_x(own_cotangent, -r) for r in (1, 2, 3)]
-    unit_two, proj = front(rows_two, qkv_two, qkv_bias)
-    mixed_two, kept_two = attention(proj)
-    active_two, slope_two = front_up(unit_two, up_two, up_bias)
-    grad_own = after(grad_own, active_two, mixed_two)
+    qkv_turned_two, bias_out_two, up_turned_two, active_two, slope_two, unit_two, mixed_two, *kept_two = run(
+        attend_second_kernel,
+        at,
+        (*rows_two, wides, *tables),
+        qkv_outs + [((512, 1024), BF)] + hidden_outs + [big, head] + kept_outs,
+        qkv_scratch
+        + [pltpu.VMEM((128, 128), F32), pltpu.VMEM((1024, 512), BF), pltpu.VMEM((8, 512), F32)],
+        flops=8_000_000_000,
+    )
+    grad_own = after(grad_own, mixed_two)
     grad_rows = [rows for block in grad_own for rows in (block, across_cores(block))]
-    down_two, down_turned_two = run(prepare_down_kernel, at, (downs,), DOWN)
-
-    grad_middle, grad_mixed = back_front(grad_rows, down_turned_two, dense_two, slope_two)
-    blocks, grad_proj = back_attend(grad_mixed, grad_middle, qkv_turned_two, up_turned_two, kept_two)
+
+    *blocks, grad_proj, grad_middle, down_two = run(
+        back_second_kernel,
+        at,
+        (*grad_rows, downs, dense, slope_two, qkv_turned_two, up_turned_two, *tables, *kept_two),
+        block_outs + [((1024, 384), BF), ((1024, 512), BF), ((512, 1024), BF)],
+        [pltpu.VMEM((1024, 512), BF), pltpu.VMEM((1024, 128), BF), pltpu.VMEM((1024, 128), BF)] + grad_scratch,
+        flops=8_000_000_000,
+    )
     joined = joined_cores(blocks)
-    unit_late = after(unit_two, joined)
-    out_sums = weight_terms(at, unit_late, (), (active_two, mixed_two, grad_rows, grad_middle))
-    wide_sums = weight_terms(at, unit_late, (grad_middle, grad_proj))
-    joined[0] = after(joined[0], out_sums, wide_sums)
+    out_sums = weight_terms(
+        at, unit_two, (), (active_two, mixed_two, grad_rows, grad_middle), others=joined
+    )
+    joined[0] = after(joined[0], out_sums)
     out_sums = swapped(out_sums, SHARDS)
-    grad_two = own_cotangent.astype(F32) + norm_back(joined_chips(joined), hidden_one)
+    grad_two = grad_rows[0].astype(F32) + norm_back(joined_chips(joined), hidden_one)
     grad_mid = grad_two.astype(BF)
+    wide_sums = weight_terms(at, unit_two, (grad_middle, grad_proj), others=[grad_mid])
     grad_rows = gather_rows(grad_mid)
     grad_rows, out_sums, wide_sums = barrier(grad_rows, out_sums, wide_sums)
+    grad_mid = grad_rows[0]
 
     wide_sums = swapped(wide_sums, SHARDS)
-    grad_middle, grad_mixed = back_front(grad_rows, down_turned_one, dense_one, slope_one)
-    early_sums = weight_terms(at, unit_one, (grad_middle,), (active_one, mixed_one, grad_rows, grad_middle))
+    early_sums, grad_middle, grad_mixed = weight_terms(
+        at, unit_one, (), (active_one, mixed_one, grad_rows), (down_turned_one, dense, slope_one)
+    )
     blocks, grad_proj = back_attend(grad_mixed, grad_middle, qkv_turned_one, up_turned_one, kept_one)
-    blocks, grad_proj, wide_sums, early_sums = barrier(blocks, grad_proj, wide_sums, early_sums)
+    blocks_hidden = run(
+        project_kernel,
+        at,
+        (active_two, mixed_two, down_two, dense),
+        block_outs,
+        [pltpu.VMEM((128, 1024), BF)],
+        flops=1_500_000_000,
+        others=[grad_proj],
+    )
+    joined_hidden = joined_cores(blocks_hidden)
+    blocks, grad_proj, out_sums, wide_sums, early_sums, joined_hidden = barrier(
+        blocks, grad_proj, out_sums, wide_sums, early_sums, joined_hidden
+    )
 
     def turned_dense(total):
         dense = jnp.concatenate([transposed(total[:128, 512:640]), total[128:, 512:640]], axis=0)
@@ -797,11 +820,11 @@
 
     early_sums = swapped(early_sums, SHARDS)
     joined = joined_cores(blocks)
-    late_sums = weight_terms(at, unit_one, (grad_proj,))
+    late_sums = weight_terms(at, unit_one, (grad_proj,), others=joined[1:])
     grad_one = grad_mid.astype(F32) + norm_back(joined_chips(joined), own_tokens)
     grad_low = grad_one.astype(BF)
-    joined = joined_cores(project(after(active_two, late_sums), mixed_two, down_two, dense_two))
-    hidden_two = hidden_one.astype(F32) + joined_chips(joined) + bias_out_two[:1, :]
+    out_sums, wide_sums = after((out_sums, wide_sums), joined[1:])
+    hidden_two = hidden_one.astype(F32) + joined_chips(joined_hidden) + bias_out_two[:1, :]
     hidden_two = hidden_two.astype(BF)
     second = turned_dense(jnp.concatenate([summed(out_sums), summed(wide_sums)], axis=1).astype(BF))
     second_high = across_high(second)
@@ -811,17 +834,13 @@
     late_sums = swapped(late_sums, SHARDS)
     second = added(second, second_high).astype(BF)
     second = [second] + [along_x(second, -r) for r in (1, 2, 3)]
-    early = summed(early_sums).astype(BF)
-    early_high = across_high(early)
+    early = turned_dense(summed(after(early_sums, second[1])).astype(BF))
     grad_beside, hidden_beside = across_cores(grad_low), across_cores(hidden_two)
-    late_sums, second, early, early_high, grad_beside, hidden_beside = barrier(
-        late_sums, second, early, early_high, grad_beside, hidden_beside
-    )
-    late = summed(late_sums).astype(BF)
-    late = added(late, across_high(late)).astype(BF)
-    early = turned_dense(added(early, early_high).astype(BF))
-    late, early, second = barrier(late, early, second)
-    first = from_all(jnp.concatenate([early, late], axis=1), ("x",))
+    late_sums, second, early, grad_beside, hidden_beside = barrier(late_sums, second, early, grad_beside, hidden_beside)
+    first = jnp.concatenate([early, summed(late_sums).astype(BF)], axis=1)
+    first = added(first, across_high(first)).astype(BF)
+    first = [first] + [along_x(first, -r) for r in (1, 2, 3)]
+    first_sums = first + [to_keeper(block, 0) for block in first]
     second_sums = second + [to_keeper(block, 1) for block in second]
 
     def placed(pairs):
@@ -841,9 +860,6 @@
         ]
     )
     hidden, in_grads = outputs[0], outputs[1].astype(F32)
-    first, second_sums, in_grads = barrier(first, second_sums, in_grads)
-    first_sums = [first, to_keeper(first, 0)]
-
     outs = run(
         final_kernel,
         at,
@@ -861,7 +877,7 @@
             pltpu.VMEM((8, 128), F32),
             pltpu.SemaphoreType.DMA((8,)),
         ],
-        spaces=[anywhere] * 10 + [vmem] * 6,
+        spaces=[anywhere] * 16 + [vmem] * 6,
     )
     grad_qkv, grad_up, grad_down, grad_dense, bias_qk, bias_v, bias_up, bias_out, *norms = outs
     return (

time: 465 us -> 441 us (0.948)
  Pallas kernels: 132 us -> 105 us
  waiting for transfers between devices: 97.2 us -> 83.1 us
  other arithmetic: 34.9 us -> 43.6 us
  starting transfers between devices: 153 us -> 161 us
    all_to_all x10 -> x8, waiting for transfers between devices: 28.6 us -> 1.63 us  [swapped(): return lax.all_to_all(blocks, axes, split_axis=0, concat_axis=0, tiled=True)]
    pallas_call x23 -> x13, Pallas kernels: 132 us -> 105 us  [run(): pl.pallas_call(lambda *refs: body(*refs[:count], *refs[count + len(others...]
    ppermute x76 -> x84, starting transfers between devices: 97.7 us -> 120 us  [route(): return lax.ppermute(block, AXES, pairs)]
    all_to_all x10 -> x8, starting transfers between devices: 55.5 us -> 40.9 us  [swapped(): return lax.all_to_all(blocks, axes, split_axis=0, concat_axis=0, tiled=True)]
    ppermute x76 -> x84, waiting for transfers between devices: 68.6 us -> 81.4 us  [route(): return lax.ppermute(block, AXES, pairs)]
    convert_element_type x12, other arithmetic: 4.75 us -> 13.8 us  [joined_cores(): return [joined[0]] + [joined[r].astype(BF) for r in (1, 2, 3)]]
    unnamed x159 -> x153, local copies, waits for them, and re-layouts: 18.1 us -> 19.6 us
    broadcast_in_dim x5 -> x4, local copies, waits for them, and re-layouts: 10.5 us -> 9.23 us  [from_all(): return swapped(jnp.broadcast_to(block[None], (count, *block.shape)), axes)]
  transfers between devices with their start and end apart: 86 -> 92, of which waited for: 27 -> 25; matrix products, arithmetic and copies ran while one was open for 9% -> 12% of each run, Pallas kernels for 20% -> 17%
where the time goes in v3:
time: 441 us; the launch traced here: 433 us
  starting transfers between devices  161 us (37%)
  Pallas kernels  105 us (24%)
  waiting for transfers between devices  83.1 us (19%)
  other arithmetic  43.6 us (10%)
  local copies, waits for them, and re-layouts  38.3 us (9%)
    ppermute x84, starting transfers between devices, route(): return lax.ppermute(block, AXES, pairs)  120 us
    pallas_call x13, Pallas kernels, run(): pl.pallas_call(lambda *refs: body(*refs[:count], *refs[count + len(others...  105 us
    ppermute x84, waiting for transfers between devices, route(): return lax.ppermute(block, AXES, pairs)  81.4 us
    all_to_all x8, starting transfers between devices, swapped(): return lax.all_to_all(blocks, axes, split_axis=0, concat_axis=0, tiled=True)  40.9 us
    unnamed x153, local copies, waits for them, and re-layouts  19.6 us
    convert_element_type x12, other arithmetic, joined_cores(): return [joined[0]] + [joined[r].astype(BF) for r in (1, 2, 3)]  13.8 us
    broadcast_in_dim x4, local copies, waits for them, and re-layouts, from_all(): return swapped(jnp.broadcast_to(block[None], (count, *block.shape)), axes)  9.23 us
  transfers between devices with their start and end apart: 92, of which 25 were waited for; matrix products, arithmetic and copies ran while one was open for 12% of the time, Pallas kernels for 17%

profile of v3, /device:TPU:9, one launch (start us, length us, event | category | flops | bytes accessed | tf_op | source)
XLA Modules:
  0.0 433.0 jit_solution(406599625041489597)
XLA Ops:
  35.0 6.6 %collective-permute-done.4.refs_3_.refs_5_ = bf16[128,1024]{1,0:T(8,128)(2,1)} collective-permute-done((bf16[128,1024]{1,0:T(8,128)(2,1)S(1)}, bf16[128,1024]{1,0:T(8,128)(2,1)}, u32[]{:S(2)}, u32[]{:S(2)}) %collective-permute-start.4) | collective-permute-done | bytes 262176 | tf_op jit(solution)/shard_map/ppermute | solution.py:35
  46.8 5.5 %all-to-all-start.1 = ((bf16[8,128,1024]{2,1,0:T(8,128)(2,1)}), bf16[8,128,1024]{2,1,0:T(8,128)(2,1)S(1)}, u32[]{:S(2)}, u32[]{:S(2)}) async-start(bf16[8,128,1024]{2,1,0:T(8,128)(2,1)} %broadcast_in_dim.19), calls=%async_computation.1 | async-start | bytes 4194304 | tf_op jit(solution)/shard_map/all_to_all | solution.py:44
  77.8 10.1 %shard_map.266 = (bf16[384,1024]{1,0:T(8,128)(2,1)}, f32[8,1024]{1,0:T(8,128)}, f32[128,128]{1,0:T(8,128)}, bf16[1024,1024]{1,0:T(8,128)(2,1)}, bf16[1024,128]{1...) custom-call(s32[26]{0:T(128)} %concatenate.48.refs_0_, ...), custom_call_target="tpu_custom_call" | custom-call | flops 5000000000 | bytes 4000000 | tf_op jit(solution)/shard_map/pallas_call | solution.py:214
  90.2 8.2 %shard_map.268 = (bf16[512,1024]{1,0:T(8,128)(2,1)}, bf16[1024,512]{1,0:T(8,128)(2,1)}, bf16[1024,512]{1,0:T(8,128)(2,1)}, bf16[1024,512]{1,0:T(8,128)(2,1)}, bf...) custom-call(s32[26]{0:T(128)} %concatenate.48.refs_0_, ...), custom_call_target="tpu_custom_call" | custom-call | flops 3000000000 | bytes 4000000 | tf_op jit(solution)/shard_map/pallas_call | solution.py:214
  101.0 5.3 %all-to-all-start.2 = ((bf16[8,144,896]{2,1,0:T(8,128)(2,1)}), bf16[8,144,896]{2,1,0:T(8,128)(2,1)S(1)}, u32[]{:S(2)}, u32[]{:S(2)}) async-start(bf16[8,144,896]{2,1,0:T(8,128)(2,1)} %broadcast_in_dim.21), calls=%async_computation.2 | async-start | bytes 4128768 | tf_op jit(solution)/shard_map/all_to_all | solution.py:44
  135.0 5.5 %collective-permute-done.22.refs_2_.refs_5_ = bf16[128,1024]{1,0:T(8,128)(2,1)} collective-permute-done((bf16[128,1024]{1,0:T(8,128)(2,1)S(1)}, bf16[128,1024]{1,0:T(8,128)(2,1)}, u32[]{:S(2)}, u32[]{:S(2)}) %collective-permute-start.22) | collective-permute-done | bytes 262176 | tf_op jit(solution)/shard_map/ppermute | solution.py:35
  154.7 13.9 %shard_map.271 = (bf16[384,1024]{1,0:T(8,128)(2,1)}, f32[8,1024]{1,0:T(8,128)}, bf16[512,1024]{1,0:T(8,128)(2,1)}, bf16[1024,512]{1,0:T(8,128)(2,1)}, bf16[1024,...) custom-call(s32[26]{0:T(128)} %concatenate.48.refs_0_, ...), custom_call_target="tpu_custom_call" | custom-call | flops 8000000000 | bytes 4000000 | tf_op jit(solution)/shard_map/pallas_call | solution.py:214
  174.5 14.3 %shard_map.274 = (bf16[128,1024]{1,0:T(8,128)(2,1)}, bf16[128,1024]{1,0:T(8,128)(2,1)}, bf16[128,1024]{1,0:T(8,128)(2,1)}, bf16[128,1024]{1,0:T(8,128)(2,1)}, bf...) custom-call(s32[26]{0:T(128)} %concatenate.48.refs_0_, ...), custom_call_target="tpu_custom_call" | custom-call | flops 8000000000 | bytes 4000000 | tf_op jit(solution)/shard_map/pallas_call | solution.py:214
  199.5 7.1 %shard_map.275.refs_1_ = bf16[8,144,640]{2,1,0:T(8,128)(2,1)} custom-call(s32[26]{0:T(128)} %concatenate.48.refs_0_, bf16[1024,1024]{1,0:T(8,128)(2,1)} %get-tuple-element.188.refs_1_, bf16[1024,512]{1,0:T(8,128)(2,1)} %get-tuple-element.189.refs_2_.refs_1_, bf16[1024,128]{1,0:T(8,128)(2,1)} %get-tuple-element.173.refs_4_.refs_3_.refs_2_, ...), custom_call_target="tpu_custom_call" | custom-call | flops 1342177280 | bytes 4000000 | tf_op jit(solution)/shard_map/pallas_call | solution.py:214
  206.6 5.3 %all-to-all-start.4 = ((bf16[8,144,640]{2,1,0:T(8,128)(2,1)}), bf16[8,144,640]{2,1,0:T(8,128)(2,1)S(1)}, u32[]{:S(2)}, u32[]{:S(2)}) async-start(bf16[8,144,640]{2,1,0:T(8,128)(2,1)} %shard_map.275.refs_1_), calls=%async_computation.4 | async-start | bytes 2949120 | tf_op jit(solution)/shard_map/all_to_all | solution.py:44
  222.5 6.8 %collective-permute-start.48 = (bf16[128,1024]{1,0:T(8,128)(2,1)S(1)}, bf16[128,1024]{1,0:T(8,128)(2,1)S(1)}, u32[]{:S(2)}, u32[]{:S(2)}) collective-permute-start(bf16[128,1024]{1,0:T(8,128)(2,1)S(1)} %collective-permute-done.47.refs_6_), channel_id=1, source_target_pairs={{0,64},{1,65},{2,66},{3,67},{4,68},{5,69},{6,70},{7,71},{8,72},{9,... | collective-permute-start | bytes 786440 | tf_op jit(solution)/shard_map/ppermute | solution.py:35
  229.9 5.8 %shard_map.277.refs_9_ = bf16[8,144,896]{2,1,0:T(8,128)(2,1)} custom-call(s32[26]{0:T(128)} %concatenate.48.refs_0_, bf16[1024,1024]{1,0:T(8,128)(2,1)} %get-tuple-element.188.refs_1_, bf16[1024,512]{1,0:T(8,128)(2,1)} %get-tuple-element.190.refs_12_.refs_2_, bf16[1024,384]{1,0:T(8,128)(2,1)} %get-tuple-element.197.refs_3_, bf16[128,1024]{1,0:T(8,128)(2,1)} %copy-done.21), custom_call_target="tpu_custom_call" | custom-call | flops 1879048192 | bytes 4000000 | tf_op jit(solution)/shard_map/pallas_call | solution.py:214
  237.8 5.5 %all-to-all-start.5 = ((bf16[8,144,896]{2,1,0:T(8,128)(2,1)}), bf16[8,144,896]{2,1,0:T(8,128)(2,1)S(1)}, u32[]{:S(2)}, u32[]{:S(2)}) async-start(bf16[8,144,896]{2,1,0:T(8,128)(2,1)} %get-tuple-element.227), calls=%async_computation.5 | async-start | bytes 4128768 | tf_op jit(solution)/shard_map/all_to_all | solution.py:44
  243.3 10.5 %shard_map.279 = (bf16[8,144,1152]{2,1,0:T(8,128)(2,1)}, bf16[1024,512]{1,0:T(8,128)(2,1)}, bf16[1024,128]{1,0:T(8,128)(2,1)}) custom-call(s32[26]{0:T(128)} %concatenate.48.refs_0_, bf16[1024,1024]{1,0:T(8,128)(2,1)} %get-tuple-element.160.refs_3_.refs_1_, bf16[1024,512]{1,0:T(8,128)(2,1)} %get-tuple-element.171.refs_2_, ...), custom_call_target="tpu_custom_call" | custom-call | flops 2415919104 | bytes 4000000 | tf_op jit(solution)/shard_map/pallas_call | solution.py:214
  253.8 11.4 %shard_map.280 = (bf16[128,1024]{1,0:T(8,128)(2,1)}, bf16[128,1024]{1,0:T(8,128)(2,1)}, bf16[128,1024]{1,0:T(8,128)(2,1)}, bf16[128,1024]{1,0:T(8,128)(2,1)}, bf...) custom-call(s32[26]{0:T(128)} %concatenate.48.refs_0_, ...), custom_call_target="tpu_custom_call" | custom-call | flops 6000000000 | bytes 4000000 | tf_op jit(solution)/shard_map/pallas_call | solution.py:214
  279.8 5.3 %all-to-all-start.6 = ((bf16[8,144,1152]{2,1,0:T(8,128)(2,1)}), bf16[8,144,1152]{2,1,0:T(8,128)(2,1)S(1)}, u32[]{:S(2)}, u32[]{:S(2)}) async-start(bf16[8,144,1152]{2,1,0:T(8,128)(2,1)} %get-tuple-element.238), calls=%async_computation.6 | async-start | bytes 5308416 | tf_op jit(solution)/shard_map/all_to_all | solution.py:44
  302.7 5.6 %collective-permute-start.63 = (bf16[128,128]{1,0:T(8,128)(2,1)S(1)}, bf16[128,128]{1,0:T(8,128)(2,1)S(1)}, u32[]{:S(2)}, u32[]{:S(2)}) collective-permute-start(bf16[128,128]{1,0:T(8,128)(2,1)S(1)} %slice.114), channel_id=1, source_target_pairs={{0,0},{1,64},{2,16},{3,80},{4,32},{5,96},{6,48},{7,112},{8,8},{9,7... | collective-permute-start | bytes 98312 | tf_op jit(solution)/shard_map/ppermute | solution.py:35
  324.9 7.1 %collective-permute-done.64.refs_5_ = bf16[144,1536]{1,0:T(8,128)(2,1)} collective-permute-done((bf16[144,1536]{1,0:T(8,128)(2,1)S(1)}, bf16[144,1536]{1,0:T(8,128)(2,1)}, u32[]{:S(2)}, u32[]{:S(2)}) %collective-permute-start.64) | collective-permute-done | bytes 442400 | tf_op jit(solution)/shard_map/ppermute | solution.py:35
  346.0 12.0 %collective-permute-done.65.refs_1_.refs_2_ = bf16[144,1536]{1,0:T(8,128)(2,1)S(1)} collective-permute-done((bf16[144,1536]{1,0:T(8,128)(2,1)S(1)}, bf16[144,1536]{1,0:T(8,128)(2,1)S(1)}, u32[]{:S(2)}, u32[]{:S(2)}) %collective-permute-start.65) | collective-permute-done | bytes 442400 | tf_op jit(solution)/shard_map/ppermute | solution.py:35
  382.9 5.4 %collective-permute-done.72 = bf16[144,1536]{1,0:T(8,128)(2,1)S(1)} collective-permute-done((bf16[144,1536]{1,0:T(8,128)(2,1)S(1)}, bf16[144,1536]{1,0:T(8,128)(2,1)S(1)}, u32[]{:S(2)}, u32[]{:S(2)}) %collective-permute-start.72) | collective-permute-done | bytes 442400 | tf_op jit(solution)/shard_map/ppermute | solution.py:35
  388.5 7.8 %collective-permute-start.74 = (bf16[144,1536]{1,0:T(8,128)(2,1)S(1)}, bf16[144,1536]{1,0:T(8,128)(2,1)S(1)}, u32[]{:S(2)}, u32[]{:S(2)}) collective-permute-start(bf16[144,1536]{1,0:T(8,128)(2,1)S(1)} %add_convert_fusion.refs_1_), channel_id=1, source_target_pairs={{0,32},{1,33},{2,34},{3,35},{4,36},{5,37},{6,38},{7,39},{8,40},{9,... | collective-permute-start | bytes 1327112 | tf_op jit(solution)/shard_map/ppermute | solution.py:35
  404.4 5.6 %collective-permute-start.79 = (bf16[144,1536]{1,0:T(8,128)(2,1)}, bf16[144,1536]{1,0:T(8,128)(2,1)S(1)}, u32[]{:S(2)}, u32[]{:S(2)}) collective-permute-start(bf16[144,1536]{1,0:T(8,128)(2,1)} %collective-permute-done.75.refs_4_), channel_id=1, source_target_pairs={{64,0},{65,1},{66,2},{67,3},{68,4},{69,5},{70,6},{71,7},{72,8},{73... | collective-permute-start | bytes 1327112 | tf_op jit(solution)/shard_map/ppermute | solution.py:35
  413.4 5.4 %collective-permute-start.78 = (bf16[144,1536]{1,0:T(8,128)(2,1)S(1)}, bf16[144,1536]{1,0:T(8,128)(2,1)S(1)}, u32[]{:S(2)}, u32[]{:S(2)}) collective-permute-start(bf16[144,1536]{1,0:T(8,128)(2,1)S(1)} %collective-permute-done.74.refs_3_), channel_id=1, source_target_pairs={{64,0},{65,1},{66,2},{67,3},{68,4},{69,5},{70,6},{71,7},{72,8},{73... | collective-permute-start | bytes 1327112 | tf_op jit(solution)/shard_map/ppermute | solution.py:35
  423.9 7.7 %shard_map.288 = (f32[128,3072]{1,0:T(8,128)}, f32[128,4096]{1,0:T(8,128)}, f32[512,1024]{1,0:T(8,128)}, f32[128,1024]{1,0:T(8,128)}, f32[1,256]{1,0:T(1,128)}, ...) custom-call(s32[26]{0:T(128)} %concatenate.48.refs_0_, ...), custom_call_target="tpu_custom_call" | custom-call | bytes 4000000 | tf_op jit(solution)/shard_map/pallas_call | solution.py:214
  (431 shorter events, 247.3 us)
Async XLA Ops:
  18.9 24.3 %all-to-all-start = ((bf16[8,144,640]{2,1,0:T(8,128)(2,1)}), bf16[8,144,640]{2,1,0:T(8,128)(2,1)S(1)}, u32[]{:S(2)}, u32[]{:S(2)}) async-start(bf16[8,144,640]{2,1,0:T(8,128)(2,1)} %broadcast_in_dim.18), calls=%async_computation | async-start | bytes 2949120 | tf_op jit(solution)/shard_map/all_to_all | solution.py:44
  46.8 42.1 %all-to-all-start.1 = ((bf16[8,128,1024]{2,1,0:T(8,128)(2,1)}), bf16[8,128,1024]{2,1,0:T(8,128)(2,1)S(1)}, u32[]{:S(2)}, u32[]{:S(2)}) async-start(bf16[8,128,1024]{2,1,0:T(8,128)(2,1)} %broadcast_in_dim.19), calls=%async_computation.1 | async-start | bytes 4194304 | tf_op jit(solution)/shard_map/all_to_all | solution.py:44
  101.0 42.0 %all-to-all-start.2 = ((bf16[8,144,896]{2,1,0:T(8,128)(2,1)}), bf16[8,144,896]{2,1,0:T(8,128)(2,1)S(1)}, u32[]{:S(2)}, u32[]{:S(2)}) async-start(bf16[8,144,896]{2,1,0:T(8,128)(2,1)} %broadcast_in_dim.21), calls=%async_computation.2 | async-start | bytes 4128768 | tf_op jit(solution)/shard_map/all_to_all | solution.py:44
  128.9 22.7 %collective-permute-start.27 = (bf16[128,1024]{1,0:T(8,128)(2,1)S(1)}, bf16[128,1024]{1,0:T(8,128)(2,1)}, u32[]{:S(2)}, u32[]{:S(2)}) collective-permute-start(bf16[128,1024]{1,0:T(8,128)(2,1)S(1)} %get-tuple-element.305.refs_1_), channel_id=1, source_target_pairs={{0,64},{1,65},{2,66},{3,67},{4,68},{5,69},{6,70},{7,71},{8,72},{9,... | collective-permute-start | bytes 786440 | tf_op jit(solution)/shard_map/ppermute | solution.py:35
  133.3 20.9 %collective-permute-start.30 = (bf16[128,1024]{1,0:T(8,128)(2,1)}, bf16[128,1024]{1,0:T(8,128)(2,1)}, u32[]{:S(2)}, u32[]{:S(2)}) collective-permute-start(bf16[128,1024]{1,0:T(8,128)(2,1)} %collective-permute-done.23.refs_3_.refs_7_), channel_id=1, source_target_pairs={{0,64},{1,65},{2,66},{3,67},{4,68},{5,69},{6,70},{7,71},{8,72},{9,... | collective-permute-start | bytes 786440 | tf_op jit(solution)/shard_map/ppermute | solution.py:35
  142.5 26.1 %collective-permute-start.26 = (bf16[128,1024]{1,0:T(8,128)(2,1)}, bf16[128,1024]{1,0:T(8,128)(2,1)S(1)}, u32[]{:S(2)}, u32[]{:S(2)}) collective-permute-start(bf16[128,1024]{1,0:T(8,128)(2,1)} %shard_map.269.refs_0_), channel_id=1, source_target_pairs={{0,16},{1,17},{2,18},{3,19},{4,20},{5,21},{6,22},{7,23},{8,24},{9,... | collective-permute-start | bytes 786440 | tf_op jit(solution)/shard_map/ppermute | solution.py:35
  146.4 27.1 %all-to-all-start.3 = ((bf16[8,128,512]{2,1,0:T(8,128)(2,1)}), bf16[8,128,512]{2,1,0:T(8,128)(2,1)S(1)}, u32[]{:S(2)}, u32[]{:S(2)}) async-start(bf16[8,128,512]{2,1,0:T(8,128)(2,1)} %broadcast_in_dim.22), calls=%async_computation.3 | async-start | bytes 2097152 | tf_op jit(solution)/shard_map/all_to_all | solution.py:44
  191.7 20.2 %collective-permute-start.39 = (bf16[128,1024]{1,0:T(8,128)(2,1)S(1)}, bf16[128,1024]{1,0:T(8,128)(2,1)}, u32[]{:S(2)}, u32[]{:S(2)}) collective-permute-start(bf16[128,1024]{1,0:T(8,128)(2,1)S(1)} %add_convert_fusion.10.refs_14_), channel_id=1, source_target_pairs={{0,16},{1,17},{2,18},{3,19},{4,20},{5,21},{6,22},{7,23},{8,24},{9,... | collective-permute-start | bytes 786440 | tf_op jit(solution)/shard_map/ppermute | solution.py:35
  206.6 29.9 %all-to-all-start.4 = ((bf16[8,144,640]{2,1,0:T(8,128)(2,1)}), bf16[8,144,640]{2,1,0:T(8,128)(2,1)S(1)}, u32[]{:S(2)}, u32[]{:S(2)}) async-start(bf16[8,144,640]{2,1,0:T(8,128)(2,1)} %shard_map.275.refs_1_), calls=%async_computation.4 | async-start | bytes 2949120 | tf_op jit(solution)/shard_map/all_to_all | solution.py:44
  237.8 40.3 %all-to-all-start.5 = ((bf16[8,144,896]{2,1,0:T(8,128)(2,1)}), bf16[8,144,896]{2,1,0:T(8,128)(2,1)S(1)}, u32[]{:S(2)}, u32[]{:S(2)}) async-start(bf16[8,144,896]{2,1,0:T(8,128)(2,1)} %get-tuple-element.227), calls=%async_computation.5 | async-start | bytes 4128768 | tf_op jit(solution)/shard_map/all_to_all | solution.py:44
  279.8 52.2 %all-to-all-start.6 = ((bf16[8,144,1152]{2,1,0:T(8,128)(2,1)}), bf16[8,144,1152]{2,1,0:T(8,128)(2,1)S(1)}, u32[]{:S(2)}, u32[]{:S(2)}) async-start(bf16[8,144,1152]{2,1,0:T(8,128)(2,1)} %get-tuple-element.238), calls=%async_computation.6 | async-start | bytes 5308416 | tf_op jit(solution)/shard_map/all_to_all | solution.py:44
  286.5 35.7 %collective-permute-start.56 = (bf16[128,1024]{1,0:T(8,128)(2,1)}, bf16[128,1024]{1,0:T(8,128)(2,1)}, u32[]{:S(2)}, u32[]{:S(2)}) collective-permute-start(bf16[128,1024]{1,0:T(8,128)(2,1)} %get-tuple-element.247), channel_id=1, source_target_pairs={{0,64},{1,65},{2,66},{3,67},{4,68},{5,69},{6,70},{7,71},{8,72},{9,... | collective-permute-start | bytes 786440 | tf_op jit(solution)/shard_map/ppermute | solution.py:35
  292.8 29.4 %collective-permute-start.57 = (bf16[128,1024]{1,0:T(8,128)(2,1)}, bf16[128,1024]{1,0:T(8,128)(2,1)}, u32[]{:S(2)}, u32[]{:S(2)}) collective-permute-start(bf16[128,1024]{1,0:T(8,128)(2,1)} %add_convert_fusion.4.refs_3_.refs_2_), channel_id=1, source_target_pairs={{0,16},{1,17},{2,18},{3,19},{4,20},{5,21},{6,22},{7,23},{8,24},{9,... | collective-permute-start | bytes 786440 | tf_op jit(solution)/shard_map/ppermute | solution.py:35
  299.1 23.1 %collective-permute-start.58 = (bf16[128,1024]{1,0:T(8,128)(2,1)}, bf16[128,1024]{1,0:T(8,128)(2,1)}, u32[]{:S(2)}, u32[]{:S(2)}) collective-permute-start(bf16[128,1024]{1,0:T(8,128)(2,1)} %add_convert_fusion.3.refs_4_.refs_3_), channel_id=1, source_target_pairs={{0,32},{1,33},{2,34},{3,35},{4,36},{5,37},{6,38},{7,39},{8,40},{9,... | collective-permute-start | bytes 786440 | tf_op jit(solution)/shard_map/ppermute | solution.py:35
  334.9 23.1 %collective-permute-start.65 = (bf16[144,1536]{1,0:T(8,128)(2,1)S(1)}, bf16[144,1536]{1,0:T(8,128)(2,1)S(1)}, u32[]{:S(2)}, u32[]{:S(2)}) collective-permute-start(bf16[144,1536]{1,0:T(8,128)(2,1)S(1)} %add_convert_fusion.1.refs_1_), channel_id=1, source_target_pairs={{0,48},{1,49},{2,50},{3,51},{4,52},{5,53},{6,54},{7,55},{8,56},{9,... | collective-permute-start | bytes 1327112 | tf_op jit(solution)/shard_map/ppermute | solution.py:35
  339.3 29.5 %all-to-all-start.7 = ((bf16[8,144,384]{2,1,0:T(8,128)(2,1)}), bf16[8,144,384]{2,1,0:T(8,128)(2,1)S(1)}, u32[]{:S(2)}, u32[]{:S(2)}) async-start(bf16[8,144,384]{2,1,0:T(8,128)(2,1)} %get-tuple-element.258), calls=%async_computation.7 | async-start | bytes 1769472 | tf_op jit(solution)/shard_map/all_to_all | solution.py:44
  343.3 25.5 %collective-permute-start.67 = (bf16[144,1536]{1,0:T(8,128)(2,1)S(1)}, bf16[144,1536]{1,0:T(8,128)(2,1)S(1)}, u32[]{:S(2)}, u32[]{:S(2)}) collective-permute-start(bf16[144,1536]{1,0:T(8,128)(2,1)S(1)} %add_convert_fusion.1.refs_1_), channel_id=1, source_target_pairs={{0,16},{1,17},{2,18},{3,19},{4,20},{5,21},{6,22},{7,23},{8,24},{9,... | collective-permute-start | bytes 1327112 | tf_op jit(solution)/shard_map/ppermute | solution.py:35
  343.3 25.5 %collective-permute-start.66 = (bf16[144,1536]{1,0:T(8,128)(2,1)S(1)}, bf16[144,1536]{1,0:T(8,128)(2,1)}, u32[]{:S(2)}, u32[]{:S(2)}) collective-permute-start(bf16[144,1536]{1,0:T(8,128)(2,1)S(1)} %add_convert_fusion.1.refs_1_), channel_id=1, source_target_pairs={{0,32},{1,33},{2,34},{3,35},{4,36},{5,37},{6,38},{7,39},{8,40},{9,... | collective-permute-start | bytes 1327112 | tf_op jit(solution)/shard_map/ppermute | solution.py:35
  344.5 24.3 %collective-permute-start.70 = (bf16[128,1024]{1,0:T(8,128)(2,1)S(1)}, bf16[128,1024]{1,0:T(8,128)(2,1)}, u32[]{:S(2)}, u32[]{:S(2)}) collective-permute-start(bf16[128,1024]{1,0:T(8,128)(2,1)S(1)} %copy-done.28), channel_id=1, source_target_pairs={{0,64},{1,65},{2,66},{3,67},{4,68},{5,69},{6,70},{7,71},{8,72},{9,... | collective-permute-start | bytes 786440 | tf_op jit(solution)/shard_map/ppermute | solution.py:35
  346.0 22.8 %collective-permute-start.69 = (bf16[128,1024]{1,0:T(8,128)(2,1)S(1)}, bf16[128,1024]{1,0:T(8,128)(2,1)}, u32[]{:S(2)}, u32[]{:S(2)}) collective-permute-start(bf16[128,1024]{1,0:T(8,128)(2,1)S(1)} %copy-done.29), channel_id=1, source_target_pairs={{0,64},{1,65},{2,66},{3,67},{4,68},{5,69},{6,70},{7,71},{8,72},{9,... | collective-permute-start | bytes 786440 | tf_op jit(solution)/shard_map/ppermute | solution.py:35
  388.5 24.9 %collective-permute-start.74 = (bf16[144,1536]{1,0:T(8,128)(2,1)S(1)}, bf16[144,1536]{1,0:T(8,128)(2,1)S(1)}, u32[]{:S(2)}, u32[]{:S(2)}) collective-permute-start(bf16[144,1536]{1,0:T(8,128)(2,1)S(1)} %add_convert_fusion.refs_1_), channel_id=1, source_target_pairs={{0,32},{1,33},{2,34},{3,35},{4,36},{5,37},{6,38},{7,39},{8,40},{9,... | collective-permute-start | bytes 1327112 | tf_op jit(solution)/shard_map/ppermute | solution.py:35
  397.1 21.7 %collective-permute-start.73 = (bf16[144,1536]{1,0:T(8,128)(2,1)S(1)}, bf16[144,1536]{1,0:T(8,128)(2,1)S(1)}, u32[]{:S(2)}, u32[]{:S(2)}) collective-permute-start(bf16[144,1536]{1,0:T(8,128)(2,1)S(1)} %add_convert_fusion.refs_1_), channel_id=1, source_target_pairs={{0,48},{1,49},{2,50},{3,51},{4,52},{5,53},{6,54},{7,55},{8,56},{9,... | collective-permute-start | bytes 1327112 | tf_op jit(solution)/shard_map/ppermute | solution.py:35
  398.1 24.1 %collective-permute-start.83 = (bf16[144,1536]{1,0:T(8,128)(2,1)S(1)}, bf16[144,1536]{1,0:T(8,128)(2,1)S(1)}, u32[]{:S(2)}, u32[]{:S(2)}) collective-permute-start(bf16[144,1536]{1,0:T(8,128)(2,1)S(1)} %copy-done.32), channel_id=1, source_target_pairs={{0,64},{1,65},{2,66},{3,67},{4,68},{5,69},{6,70},{7,71},{8,72},{9,... | collective-permute-start | bytes 1327112 | tf_op jit(solution)/shard_map/ppermute | solution.py:35
  399.5 22.8 %collective-permute-start.76 = (bf16[144,1536]{1,0:T(8,128)(2,1)S(1)}, bf16[144,1536]{1,0:T(8,128)(2,1)S(1)}, u32[]{:S(2)}, u32[]{:S(2)}) collective-permute-start(bf16[144,1536]{1,0:T(8,128)(2,1)S(1)} %add_convert_fusion.refs_1_), channel_id=1, source_target_pairs={{64,0},{65,1},{66,2},{67,3},{68,4},{69,5},{70,6},{71,7},{72,8},{73... | collective-permute-start | bytes 1327112 | tf_op jit(solution)/shard_map/ppermute | solution.py:35
  (144 other events, 1393.7 us)

commit v4 on v3

--- a/solution.py
+++ b/solution.py
@@ -426,12 +426,14 @@
     project(at, 1, active, mixed, down, dense_parts, refs[8], refs[:8])
 
 
-def pull_back(at, layer, blocks, down_turned, dense_parts, slope, grad_middle, grad_mixed, dense_turned):
+def pull_back(at, layer, blocks, down_turned, dense_parts, slope, grad_middle, grad_mixed, dense_turned, together):
+    for k in range(8):
+        together[128 * k : 128 * k + 128, :] = blocks[k][...]
     for part, columns in dense_parts_of(at, dense_parts, layer):
         dense_turned[block_rows(part, 128), :] = jnp.transpose(columns)
-    for k in range(8):
-        here = slice(128 * k, 128 * k + 128)
-        rows = blocks[k][...]
+    for k in range(4):
+        here = slice(256 * k, 256 * k + 256)
+        rows = together[here, :]
         grad_middle[here, :] = (dot(rows, down_turned[...]) * slope[here, :].astype(F32)).astype(BF)
         grad_mixed[here, :] = dot(rows, dense_turned[...]).astype(BF)
 
@@ -439,9 +441,9 @@
 def back_second_kernel(at, *refs):
     rows, (messages, dense_parts, slope), qkv_turned, up_turned = refs[:8], refs[8:11], refs[11], refs[12]
     tables, kept, blocks = refs[13:17], refs[17:22], refs[22:30]
-    grad_proj, grad_middle, down, down_turned, dense_turned, grad_mixed, *scratch = refs[30:]
+    grad_proj, grad_middle, down, down_turned, dense_turned, grad_mixed, together, *scratch = refs[30:]
     prepare_down([messages.at[k] for k in range(8)], down, down_turned)
-    pull_back(at, 1, rows, down_turned, dense_parts, slope, grad_middle, grad_mixed, dense_turned)
+    pull_back(at, 1, rows, down_turned, dense_parts, slope, grad_middle, grad_mixed, dense_turned, together)
     back_attend_kernel(
         at, grad_mixed, grad_middle, qkv_turned, up_turned, *tables, *kept, *blocks, grad_proj, *scratch
     )
@@ -466,7 +468,7 @@
     if outward:
         active, mixed, rows, *grad_middle = outward
         arrays = (*arrays, active, mixed, *rows, *grad_middle)
-        scratch = [pltpu.VMEM((512, 1024), F32), pltpu.VMEM((128, 1024), F32)]
+        scratch = [pltpu.VMEM((1024, 1024), BF)]
     if pulled:
         arrays = (*arrays, *pulled)
         outs += [((1024, 512), BF), ((1024, 128), BF)]
@@ -477,33 +479,28 @@
         if pulled:
             (active, mixed), rows, refs = refs[:2], refs[2:10], refs[10:]
             (down_turned, dense_parts, slope), (out, grad_middle, grad_mixed) = refs[:3], refs[3:6]
-            down, dense, dense_turned = refs[6:]
-            pull_back(at, 0, rows, down_turned, dense_parts, slope, grad_middle, grad_mixed, dense_turned)
+            together, dense_turned = refs[6:]
+            pull_back(
+                at, 0, rows, down_turned, dense_parts, slope, grad_middle, grad_mixed, dense_turned, together
+            )
             grad_refs = (grad_middle,)
         elif outward:
-            (active, mixed), rows, grad_middle, out, (down, dense) = refs[:2], refs[2:10], refs[10], refs[11], refs[12:]
+            (active, mixed), rows, grad_middle, out, together = refs[:2], refs[2:10], *refs[10:]
+            for k in range(8):
+                together[128 * k : 128 * k + 128, :] = rows[k][...]
         else:
             out = refs[0]
         if outward:
-            sums = jnp.zeros((1, 128), F32)
-            for k in range(8):
-                here = slice(128 * k, 128 * k + 128)
-                block = rows[k][...]
-                more_down = dot_left(active[here, :], block)
-                more_dense = dot_left(mixed[here, :], block)
-                if k == 0:
-                    down[...] = more_down
-                    dense[...] = more_dense
-                else:
-                    down[...] += more_down
-                    dense[...] += more_dense
-                sums = sums + jnp.sum(rows[k][:, lanes(128 * at[PART])].astype(F32), axis=0, keepdims=True)
+            sums = jnp.sum(together[:, lanes(128 * at[PART])].astype(F32), axis=0, keepdims=True)
             sums_up = jnp.sum(grad_middle[...].astype(F32), axis=0, keepdims=True)
+            dense = dot_left(mixed[...], together[...]).astype(BF)
             for shard in range(8):
+                if shard % 4 == 0:
+                    down = dot_left(active[:, 64 * shard : 64 * shard + 256], together[...]).astype(BF)
                 for half in range(2):
-                    piece = down[64 * shard : 64 * shard + 64, 512 * half : 512 * half + 512]
-                    out[shard, 64 * half : 64 * half + 64, :512] = piece.astype(BF)
-                out[shard, :128, 512:640] = dense[:, 128 * shard : 128 * shard + 128].astype(BF)
+                    piece = down[64 * (shard % 4) : 64 * (shard % 4) + 64, 512 * half : 512 * half + 512]
+                    out[shard, 64 * half : 64 * half + 64, :512] = piece
+                out[shard, :128, 512:640] = dense[:, 128 * shard : 128 * shard + 128]
                 out[shard, 128:, :128] = jnp.broadcast_to(sums, (16, 128)).astype(BF)
                 out[shard, 128:, 128:640] = jnp.broadcast_to(sums_up, (16, 512)).astype(BF)
         at_column = start
@@ -512,8 +509,9 @@
             here = slice(at_column, at_column + columns)
             sums = jnp.sum(grad[...].astype(F32), axis=0, keepdims=True)
             for shard in range(8):
-                terms = dot_left(unit[:, 128 * shard : 128 * shard + 128], grad[...])
-                out[shard, :128, here] = terms.astype(BF)
+                if shard % 2 == 0:
+                    terms = dot_left(unit[:, 128 * shard : 128 * shard + 256], grad[...]).astype(BF)
+                out[shard, :128, here] = terms[128 * (shard % 2) : 128 * (shard % 2) + 128, :]
                 out[shard, 128:, here] = jnp.broadcast_to(sums, (16, columns)).astype(BF)
             at_column += columns
 
@@ -776,7 +774,7 @@
         at,
         (*grad_rows, downs, dense, slope_two, qkv_turned_two, up_turned_two, *tables, *kept_two),
         block_outs + [((1024, 384), BF), ((1024, 512), BF), ((512, 1024), BF)],
-        [pltpu.VMEM((1024, 512), BF), pltpu.VMEM((1024, 128), BF), pltpu.VMEM((1024, 128), BF)] + grad_scratch,
+        [pltpu.VMEM((1024, 512), BF)] + [pltpu.VMEM((1024, 128), BF)] * 2 + [pltpu.VMEM((1024, 1024), BF)] + grad_scratch,
         flops=8_000_000_000,
     )
     joined = joined_cores(blocks)

time: 441 us -> 449 us (1.018)
  starting transfers between devices: 161 us -> 173 us
    ppermute x84, starting transfers between devices: 120 us -> 132 us  [route(): return lax.ppermute(block, AXES, pairs)]
  transfers between devices with their start and end apart: 92 -> 92, of which waited for: 25 -> 24; matrix products, arithmetic and copies ran while one was open for 12% -> 11% of each run, Pallas kernels for 17% -> 16%
where the time goes in v4:
time: 449 us; the launch traced here: 441 us
  starting transfers between devices  173 us (39%)
  Pallas kernels  102 us (23%)
  waiting for transfers between devices  82.1 us (18%)
  other arithmetic  43.6 us (10%)
  local copies, waits for them, and re-layouts  38.3 us (9%)
    ppermute x84, starting transfers between devices, route(): return lax.ppermute(block, AXES, pairs)  132 us
    pallas_call x13, Pallas kernels, run(): pl.pallas_call(lambda *refs: body(*refs[:count], *refs[count + len(others...  102 us
    ppermute x84, waiting for transfers between devices, route(): return lax.ppermute(block, AXES, pairs)  80.4 us
    all_to_all x8, starting transfers between devices, swapped(): return lax.all_to_all(blocks, axes, split_axis=0, concat_axis=0, tiled=True)  40.9 us
    unnamed x153, local copies, waits for them, and re-layouts  19.6 us
    convert_element_type x12, other arithmetic, joined_cores(): return [joined[0]] + [joined[r].astype(BF) for r in (1, 2, 3)]  13.8 us
    broadcast_in_dim x4, local copies, waits for them, and re-layouts, from_all(): return swapped(jnp.broadcast_to(block[None], (count, *block.shape)), axes)  9.23 us
  transfers between devices with their start and end apart: 92, of which 24 were waited for; matrix products, arithmetic and copies ran while one was open for 11% of the time, Pallas kernels for 16%

profile of v4, /device:TPU:9, one launch (start us, length us, event | category | flops | bytes accessed | tf_op | source)
XLA Modules:
  0.0 441.3 jit_solution(4240562816098121640)
XLA Ops:
  35.0 6.6 %collective-permute-done.4.refs_3_.refs_5_ = bf16[128,1024]{1,0:T(8,128)(2,1)} collective-permute-done((bf16[128,1024]{1,0:T(8,128)(2,1)S(1)}, bf16[128,1024]{1,0:T(8,128)(2,1)}, u32[]{:S(2)}, u32[]{:S(2)}) %collective-permute-start.4) | collective-permute-done | bytes 262176 | tf_op jit(solution)/shard_map/ppermute | solution.py:35
  46.8 5.5 %all-to-all-start.1 = ((bf16[8,128,1024]{2,1,0:T(8,128)(2,1)}), bf16[8,128,1024]{2,1,0:T(8,128)(2,1)S(1)}, u32[]{:S(2)}, u32[]{:S(2)}) async-start(bf16[8,128,1024]{2,1,0:T(8,128)(2,1)} %broadcast_in_dim.19), calls=%async_computation.1 | async-start | bytes 4194304 | tf_op jit(solution)/shard_map/all_to_all | solution.py:44
  73.0 13.1 %collective-permute-start.9 = (bf16[4,128,256]{2,1,0:T(8,128)(2,1)S(1)}, bf16[4,128,256]{2,1,0:T(8,128)(2,1)S(1)}, u32[]{:S(2)}, u32[]{:S(2)}) collective-permute-start(bf16[4,128,256]{2,1,0:T(8,128)(2,1)S(1)} %pad_maximum_fusion.9), channel_id=1, source_target_pairs={{0,64},{1,65},{2,66},{3,67},{4,68},{5,69},{6,70},{7,71},{8,72},{9,... | collective-permute-start | bytes 786440 | tf_op jit(solution)/shard_map/ppermute | solution.py:35
  89.1 10.1 %shard_map.266 = (bf16[384,1024]{1,0:T(8,128)(2,1)}, f32[8,1024]{1,0:T(8,128)}, f32[128,128]{1,0:T(8,128)}, bf16[1024,1024]{1,0:T(8,128)(2,1)}, bf16[1024,128]{1...) custom-call(s32[26]{0:T(128)} %concatenate.48.refs_0_, ...), custom_call_target="tpu_custom_call" | custom-call | flops 5000000000 | bytes 4000000 | tf_op jit(solution)/shard_map/pallas_call | solution.py:214
  101.4 8.2 %shard_map.268 = (bf16[512,1024]{1,0:T(8,128)(2,1)}, bf16[1024,512]{1,0:T(8,128)(2,1)}, bf16[1024,512]{1,0:T(8,128)(2,1)}, bf16[1024,512]{1,0:T(8,128)(2,1)}, bf...) custom-call(s32[26]{0:T(128)} %concatenate.48.refs_0_, ...), custom_call_target="tpu_custom_call" | custom-call | flops 3000000000 | bytes 4000000 | tf_op jit(solution)/shard_map/pallas_call | solution.py:214
  112.2 5.3 %all-to-all-start.2 = ((bf16[8,144,896]{2,1,0:T(8,128)(2,1)}), bf16[8,144,896]{2,1,0:T(8,128)(2,1)S(1)}, u32[]{:S(2)}, u32[]{:S(2)}) async-start(bf16[8,144,896]{2,1,0:T(8,128)(2,1)} %broadcast_in_dim.21), calls=%async_computation.2 | async-start | bytes 4128768 | tf_op jit(solution)/shard_map/all_to_all | solution.py:44
  146.2 5.5 %collective-permute-done.22.refs_2_.refs_5_ = bf16[128,1024]{1,0:T(8,128)(2,1)} collective-permute-done((bf16[128,1024]{1,0:T(8,128)(2,1)S(1)}, bf16[128,1024]{1,0:T(8,128)(2,1)}, u32[]{:S(2)}, u32[]{:S(2)}) %collective-permute-start.22) | collective-permute-done | bytes 262176 | tf_op jit(solution)/shard_map/ppermute | solution.py:35
  165.9 13.9 %shard_map.271 = (bf16[384,1024]{1,0:T(8,128)(2,1)}, f32[8,1024]{1,0:T(8,128)}, bf16[512,1024]{1,0:T(8,128)(2,1)}, bf16[1024,512]{1,0:T(8,128)(2,1)}, bf16[1024,...) custom-call(s32[26]{0:T(128)} %concatenate.48.refs_0_, ...), custom_call_target="tpu_custom_call" | custom-call | flops 8000000000 | bytes 4000000 | tf_op jit(solution)/shard_map/pallas_call | solution.py:214
  185.7 14.1 %shard_map.274 = (bf16[128,1024]{1,0:T(8,128)(2,1)}, bf16[128,1024]{1,0:T(8,128)(2,1)}, bf16[128,1024]{1,0:T(8,128)(2,1)}, bf16[128,1024]{1,0:T(8,128)(2,1)}, bf...) custom-call(s32[26]{0:T(128)} %concatenate.48.refs_0_, ...), custom_call_target="tpu_custom_call" | custom-call | flops 8000000000 | bytes 4000000 | tf_op jit(solution)/shard_map/pallas_call | solution.py:214
  210.6 5.7 %shard_map.275.refs_1_ = bf16[8,144,640]{2,1,0:T(8,128)(2,1)} custom-call(s32[26]{0:T(128)} %concatenate.48.refs_0_, bf16[1024,1024]{1,0:T(8,128)(2,1)} %get-tuple-element.188.refs_1_, bf16[1024,512]{1,0:T(8,128)(2,1)} %get-tuple-element.189.refs_2_.refs_1_, bf16[1024,128]{1,0:T(8,128)(2,1)} %get-tuple-element.173.refs_4_.refs_3_.refs_2_, ...), custom_call_target="tpu_custom_call" | custom-call | flops 1342177280 | bytes 4000000 | tf_op jit(solution)/shard_map/pallas_call | solution.py:214
  216.3 5.3 %all-to-all-start.4 = ((bf16[8,144,640]{2,1,0:T(8,128)(2,1)}), bf16[8,144,640]{2,1,0:T(8,128)(2,1)S(1)}, u32[]{:S(2)}, u32[]{:S(2)}) async-start(bf16[8,144,640]{2,1,0:T(8,128)(2,1)} %shard_map.275.refs_1_), calls=%async_computation.4 | async-start | bytes 2949120 | tf_op jit(solution)/shard_map/all_to_all | solution.py:44
  231.5 7.5 %collective-permute-start.48 = (bf16[128,1024]{1,0:T(8,128)(2,1)S(1)}, bf16[128,1024]{1,0:T(8,128)(2,1)S(1)}, u32[]{:S(2)}, u32[]{:S(2)}) collective-permute-start(bf16[128,1024]{1,0:T(8,128)(2,1)S(1)} %collective-permute-done.47.refs_6_), channel_id=1, source_target_pairs={{0,64},{1,65},{2,66},{3,67},{4,68},{5,69},{6,70},{7,71},{8,72},{9,... | collective-permute-start | bytes 786440 | tf_op jit(solution)/shard_map/ppermute | solution.py:35
  239.6 5.8 %shard_map.277.refs_9_ = bf16[8,144,896]{2,1,0:T(8,128)(2,1)} custom-call(s32[26]{0:T(128)} %concatenate.48.refs_0_, bf16[1024,1024]{1,0:T(8,128)(2,1)} %get-tuple-element.188.refs_1_, bf16[1024,512]{1,0:T(8,128)(2,1)} %get-tuple-element.190.refs_12_.refs_2_, bf16[1024,384]{1,0:T(8,128)(2,1)} %get-tuple-element.197.refs_3_, bf16[128,1024]{1,0:T(8,128)(2,1)} %copy-done.21), custom_call_target="tpu_custom_call" | custom-call | flops 1879048192 | bytes 4000000 | tf_op jit(solution)/shard_map/pallas_call | solution.py:214
  247.4 5.6 %all-to-all-start.5 = ((bf16[8,144,896]{2,1,0:T(8,128)(2,1)}), bf16[8,144,896]{2,1,0:T(8,128)(2,1)S(1)}, u32[]{:S(2)}, u32[]{:S(2)}) async-start(bf16[8,144,896]{2,1,0:T(8,128)(2,1)} %get-tuple-element.227), calls=%async_computation.5 | async-start | bytes 4128768 | tf_op jit(solution)/shard_map/all_to_all | solution.py:44
  253.0 9.2 %shard_map.279 = (bf16[8,144,1152]{2,1,0:T(8,128)(2,1)}, bf16[1024,512]{1,0:T(8,128)(2,1)}, bf16[1024,128]{1,0:T(8,128)(2,1)}) custom-call(s32[26]{0:T(128)} %concatenate.48.refs_0_, bf16[1024,1024]{1,0:T(8,128)(2,1)} %get-tuple-element.160.refs_3_.refs_1_, bf16[1024,512]{1,0:T(8,128)(2,1)} %get-tuple-element.171.refs_2_, ...), custom_call_target="tpu_custom_call" | custom-call | flops 2415919104 | bytes 4000000 | tf_op jit(solution)/shard_map/pallas_call | solution.py:214
  262.2 11.4 %shard_map.280 = (bf16[128,1024]{1,0:T(8,128)(2,1)}, bf16[128,1024]{1,0:T(8,128)(2,1)}, bf16[128,1024]{1,0:T(8,128)(2,1)}, bf16[128,1024]{1,0:T(8,128)(2,1)}, bf...) custom-call(s32[26]{0:T(128)} %concatenate.48.refs_0_, ...), custom_call_target="tpu_custom_call" | custom-call | flops 6000000000 | bytes 4000000 | tf_op jit(solution)/shard_map/pallas_call | solution.py:214
  311.0 5.6 %collective-permute-start.63 = (bf16[128,128]{1,0:T(8,128)(2,1)S(1)}, bf16[128,128]{1,0:T(8,128)(2,1)S(1)}, u32[]{:S(2)}, u32[]{:S(2)}) collective-permute-start(bf16[128,128]{1,0:T(8,128)(2,1)S(1)} %slice.114), channel_id=1, source_target_pairs={{0,0},{1,64},{2,16},{3,80},{4,32},{5,96},{6,48},{7,112},{8,8},{9,7... | collective-permute-start | bytes 98312 | tf_op jit(solution)/shard_map/ppermute | solution.py:35
  333.2 7.1 %collective-permute-done.64.refs_5_ = bf16[144,1536]{1,0:T(8,128)(2,1)} collective-permute-done((bf16[144,1536]{1,0:T(8,128)(2,1)S(1)}, bf16[144,1536]{1,0:T(8,128)(2,1)}, u32[]{:S(2)}, u32[]{:S(2)}) %collective-permute-start.64) | collective-permute-done | bytes 442400 | tf_op jit(solution)/shard_map/ppermute | solution.py:35
  354.3 11.9 %collective-permute-done.65.refs_1_.refs_2_ = bf16[144,1536]{1,0:T(8,128)(2,1)S(1)} collective-permute-done((bf16[144,1536]{1,0:T(8,128)(2,1)S(1)}, bf16[144,1536]{1,0:T(8,128)(2,1)S(1)}, u32[]{:S(2)}, u32[]{:S(2)}) %collective-permute-start.65) | collective-permute-done | bytes 442400 | tf_op jit(solution)/shard_map/ppermute | solution.py:35
  390.9 5.4 %collective-permute-done.72 = bf16[144,1536]{1,0:T(8,128)(2,1)S(1)} collective-permute-done((bf16[144,1536]{1,0:T(8,128)(2,1)S(1)}, bf16[144,1536]{1,0:T(8,128)(2,1)S(1)}, u32[]{:S(2)}, u32[]{:S(2)}) %collective-permute-start.72) | collective-permute-done | bytes 442400 | tf_op jit(solution)/shard_map/ppermute | solution.py:35
  396.7 7.8 %collective-permute-start.74 = (bf16[144,1536]{1,0:T(8,128)(2,1)S(1)}, bf16[144,1536]{1,0:T(8,128)(2,1)S(1)}, u32[]{:S(2)}, u32[]{:S(2)}) collective-permute-start(bf16[144,1536]{1,0:T(8,128)(2,1)S(1)} %add_convert_fusion.refs_1_), channel_id=1, source_target_pairs={{0,32},{1,33},{2,34},{3,35},{4,36},{5,37},{6,38},{7,39},{8,40},{9,... | collective-permute-start | bytes 1327112 | tf_op jit(solution)/shard_map/ppermute | solution.py:35
  412.7 5.6 %collective-permute-start.79 = (bf16[144,1536]{1,0:T(8,128)(2,1)}, bf16[144,1536]{1,0:T(8,128)(2,1)S(1)}, u32[]{:S(2)}, u32[]{:S(2)}) collective-permute-start(bf16[144,1536]{1,0:T(8,128)(2,1)} %collective-permute-done.75.refs_4_), channel_id=1, source_target_pairs={{64,0},{65,1},{66,2},{67,3},{68,4},{69,5},{70,6},{71,7},{72,8},{73... | collective-permute-start | bytes 1327112 | tf_op jit(solution)/shard_map/ppermute | solution.py:35
  421.7 5.4 %collective-permute-start.78 = (bf16[144,1536]{1,0:T(8,128)(2,1)S(1)}, bf16[144,1536]{1,0:T(8,128)(2,1)S(1)}, u32[]{:S(2)}, u32[]{:S(2)}) collective-permute-start(bf16[144,1536]{1,0:T(8,128)(2,1)S(1)} %collective-permute-done.74.refs_3_), channel_id=1, source_target_pairs={{64,0},{65,1},{66,2},{67,3},{68,4},{69,5},{70,6},{71,7},{72,8},{73... | collective-permute-start | bytes 1327112 | tf_op jit(solution)/shard_map/ppermute | solution.py:35
  432.2 7.7 %shard_map.288 = (f32[128,3072]{1,0:T(8,128)}, f32[128,4096]{1,0:T(8,128)}, f32[512,1024]{1,0:T(8,128)}, f32[128,1024]{1,0:T(8,128)}, f32[1,256]{1,0:T(1,128)}, ...) custom-call(s32[26]{0:T(128)} %concatenate.48.refs_0_, ...), custom_call_target="tpu_custom_call" | custom-call | bytes 4000000 | tf_op jit(solution)/shard_map/pallas_call | solution.py:214
  (431 shorter events, 249.8 us)
Async XLA Ops:
  18.9 24.3 %all-to-all-start = ((bf16[8,144,640]{2,1,0:T(8,128)(2,1)}), bf16[8,144,640]{2,1,0:T(8,128)(2,1)S(1)}, u32[]{:S(2)}, u32[]{:S(2)}) async-start(bf16[8,144,640]{2,1,0:T(8,128)(2,1)} %broadcast_in_dim.18), calls=%async_computation | async-start | bytes 2949120 | tf_op jit(solution)/shard_map/all_to_all | solution.py:44
  46.8 53.3 %all-to-all-start.1 = ((bf16[8,128,1024]{2,1,0:T(8,128)(2,1)}), bf16[8,128,1024]{2,1,0:T(8,128)(2,1)S(1)}, u32[]{:S(2)}, u32[]{:S(2)}) async-start(bf16[8,128,1024]{2,1,0:T(8,128)(2,1)} %broadcast_in_dim.19), calls=%async_computation.1 | async-start | bytes 4194304 | tf_op jit(solution)/shard_map/all_to_all | solution.py:44
  57.0 29.2 %collective-permute-start.10 = (bf16[128,1024]{1,0:T(8,128)(2,1)S(1)}, bf16[128,1024]{1,0:T(8,128)(2,1)S(1)}, u32[]{:S(2)}, u32[]{:S(2)}) collective-permute-start(bf16[128,1024]{1,0:T(8,128)(2,1)S(1)} %copy-done.42), channel_id=1, source_target_pairs={{0,64},{1,65},{2,66},{3,67},{4,68},{5,69},{6,70},{7,71},{8,72},{9,... | collective-permute-start | bytes 786440 | tf_op jit(solution)/shard_map/ppermute | solution.py:35
  62.8 24.1 %collective-permute-start.13 = (bf16[128,1024]{1,0:T(8,128)(2,1)}, bf16[128,1024]{1,0:T(8,128)(2,1)S(1)}, u32[]{:S(2)}, u32[]{:S(2)}) collective-permute-start(bf16[128,1024]{1,0:T(8,128)(2,1)} %collective-permute-done.5.refs_4_.refs_7_), channel_id=1, source_target_pairs={{0,64},{1,65},{2,66},{3,67},{4,68},{5,69},{6,70},{7,71},{8,72},{9,... | collective-permute-start | bytes 786440 | tf_op jit(solution)/shard_map/ppermute | solution.py:35
  63.1 24.5 %collective-permute-start.12 = (bf16[128,1024]{1,0:T(8,128)(2,1)}, bf16[128,1024]{1,0:T(8,128)(2,1)S(1)}, u32[]{:S(2)}, u32[]{:S(2)}) collective-permute-start(bf16[128,1024]{1,0:T(8,128)(2,1)} %collective-permute-done.4.refs_3_.refs_5_), channel_id=1, source_target_pairs={{0,64},{1,65},{2,66},{3,67},{4,68},{5,69},{6,70},{7,71},{8,72},{9,... | collective-permute-start | bytes 786440 | tf_op jit(solution)/shard_map/ppermute | solution.py:35
  73.0 26.3 %collective-permute-start.9 = (bf16[4,128,256]{2,1,0:T(8,128)(2,1)S(1)}, bf16[4,128,256]{2,1,0:T(8,128)(2,1)S(1)}, u32[]{:S(2)}, u32[]{:S(2)}) collective-permute-start(bf16[4,128,256]{2,1,0:T(8,128)(2,1)S(1)} %pad_maximum_fusion.9), channel_id=1, source_target_pairs={{0,64},{1,65},{2,66},{3,67},{4,68},{5,69},{6,70},{7,71},{8,72},{9,... | collective-permute-start | bytes 786440 | tf_op jit(solution)/shard_map/ppermute | solution.py:35
  112.2 42.0 %all-to-all-start.2 = ((bf16[8,144,896]{2,1,0:T(8,128)(2,1)}), bf16[8,144,896]{2,1,0:T(8,128)(2,1)S(1)}, u32[]{:S(2)}, u32[]{:S(2)}) async-start(bf16[8,144,896]{2,1,0:T(8,128)(2,1)} %broadcast_in_dim.21), calls=%async_computation.2 | async-start | bytes 4128768 | tf_op jit(solution)/shard_map/all_to_all | solution.py:44
  153.8 26.1 %collective-permute-start.26 = (bf16[128,1024]{1,0:T(8,128)(2,1)}, bf16[128,1024]{1,0:T(8,128)(2,1)S(1)}, u32[]{:S(2)}, u32[]{:S(2)}) collective-permute-start(bf16[128,1024]{1,0:T(8,128)(2,1)} %shard_map.269.refs_0_), channel_id=1, source_target_pairs={{0,16},{1,17},{2,18},{3,19},{4,20},{5,21},{6,22},{7,23},{8,24},{9,... | collective-permute-start | bytes 786440 | tf_op jit(solution)/shard_map/ppermute | solution.py:35
  157.6 27.1 %all-to-all-start.3 = ((bf16[8,128,512]{2,1,0:T(8,128)(2,1)}), bf16[8,128,512]{2,1,0:T(8,128)(2,1)S(1)}, u32[]{:S(2)}, u32[]{:S(2)}) async-start(bf16[8,128,512]{2,1,0:T(8,128)(2,1)} %broadcast_in_dim.22), calls=%async_computation.3 | async-start | bytes 2097152 | tf_op jit(solution)/shard_map/all_to_all | solution.py:44
  216.3 29.9 %all-to-all-start.4 = ((bf16[8,144,640]{2,1,0:T(8,128)(2,1)}), bf16[8,144,640]{2,1,0:T(8,128)(2,1)S(1)}, u32[]{:S(2)}, u32[]{:S(2)}) async-start(bf16[8,144,640]{2,1,0:T(8,128)(2,1)} %shard_map.275.refs_1_), calls=%async_computation.4 | async-start | bytes 2949120 | tf_op jit(solution)/shard_map/all_to_all | solution.py:44
  247.4 38.9 %all-to-all-start.5 = ((bf16[8,144,896]{2,1,0:T(8,128)(2,1)}), bf16[8,144,896]{2,1,0:T(8,128)(2,1)S(1)}, u32[]{:S(2)}, u32[]{:S(2)}) async-start(bf16[8,144,896]{2,1,0:T(8,128)(2,1)} %get-tuple-element.227), calls=%async_computation.5 | async-start | bytes 4128768 | tf_op jit(solution)/shard_map/all_to_all | solution.py:44
  288.1 52.2 %all-to-all-start.6 = ((bf16[8,144,1152]{2,1,0:T(8,128)(2,1)}), bf16[8,144,1152]{2,1,0:T(8,128)(2,1)S(1)}, u32[]{:S(2)}, u32[]{:S(2)}) async-start(bf16[8,144,1152]{2,1,0:T(8,128)(2,1)} %get-tuple-element.238), calls=%async_computation.6 | async-start | bytes 5308416 | tf_op jit(solution)/shard_map/all_to_all | solution.py:44
  294.8 35.7 %collective-permute-start.56 = (bf16[128,1024]{1,0:T(8,128)(2,1)}, bf16[128,1024]{1,0:T(8,128)(2,1)}, u32[]{:S(2)}, u32[]{:S(2)}) collective-permute-start(bf16[128,1024]{1,0:T(8,128)(2,1)} %get-tuple-element.247), channel_id=1, source_target_pairs={{0,64},{1,65},{2,66},{3,67},{4,68},{5,69},{6,70},{7,71},{8,72},{9,... | collective-permute-start | bytes 786440 | tf_op jit(solution)/shard_map/ppermute | solution.py:35
  301.1 29.4 %collective-permute-start.57 = (bf16[128,1024]{1,0:T(8,128)(2,1)}, bf16[128,1024]{1,0:T(8,128)(2,1)}, u32[]{:S(2)}, u32[]{:S(2)}) collective-permute-start(bf16[128,1024]{1,0:T(8,128)(2,1)} %add_convert_fusion.4.refs_3_.refs_2_), channel_id=1, source_target_pairs={{0,16},{1,17},{2,18},{3,19},{4,20},{5,21},{6,22},{7,23},{8,24},{9,... | collective-permute-start | bytes 786440 | tf_op jit(solution)/shard_map/ppermute | solution.py:35
  307.4 23.1 %collective-permute-start.58 = (bf16[128,1024]{1,0:T(8,128)(2,1)}, bf16[128,1024]{1,0:T(8,128)(2,1)}, u32[]{:S(2)}, u32[]{:S(2)}) collective-permute-start(bf16[128,1024]{1,0:T(8,128)(2,1)} %add_convert_fusion.3.refs_4_.refs_3_), channel_id=1, source_target_pairs={{0,32},{1,33},{2,34},{3,35},{4,36},{5,37},{6,38},{7,39},{8,40},{9,... | collective-permute-start | bytes 786440 | tf_op jit(solution)/shard_map/ppermute | solution.py:35
  343.2 23.1 %collective-permute-start.65 = (bf16[144,1536]{1,0:T(8,128)(2,1)S(1)}, bf16[144,1536]{1,0:T(8,128)(2,1)S(1)}, u32[]{:S(2)}, u32[]{:S(2)}) collective-permute-start(bf16[144,1536]{1,0:T(8,128)(2,1)S(1)} %add_convert_fusion.1.refs_1_), channel_id=1, source_target_pairs={{0,48},{1,49},{2,50},{3,51},{4,52},{5,53},{6,54},{7,55},{8,56},{9,... | collective-permute-start | bytes 1327112 | tf_op jit(solution)/shard_map/ppermute | solution.py:35
  347.6 29.5 %all-to-all-start.7 = ((bf16[8,144,384]{2,1,0:T(8,128)(2,1)}), bf16[8,144,384]{2,1,0:T(8,128)(2,1)S(1)}, u32[]{:S(2)}, u32[]{:S(2)}) async-start(bf16[8,144,384]{2,1,0:T(8,128)(2,1)} %get-tuple-element.258), calls=%async_computation.7 | async-start | bytes 1769472 | tf_op jit(solution)/shard_map/all_to_all | solution.py:44
  351.5 25.5 %collective-permute-start.67 = (bf16[144,1536]{1,0:T(8,128)(2,1)S(1)}, bf16[144,1536]{1,0:T(8,128)(2,1)S(1)}, u32[]{:S(2)}, u32[]{:S(2)}) collective-permute-start(bf16[144,1536]{1,0:T(8,128)(2,1)S(1)} %add_convert_fusion.1.refs_1_), channel_id=1, source_target_pairs={{0,16},{1,17},{2,18},{3,19},{4,20},{5,21},{6,22},{7,23},{8,24},{9,... | collective-permute-start | bytes 1327112 | tf_op jit(solution)/shard_map/ppermute | solution.py:35
  351.5 25.5 %collective-permute-start.66 = (bf16[144,1536]{1,0:T(8,128)(2,1)S(1)}, bf16[144,1536]{1,0:T(8,128)(2,1)}, u32[]{:S(2)}, u32[]{:S(2)}) collective-permute-start(bf16[144,1536]{1,0:T(8,128)(2,1)S(1)} %add_convert_fusion.1.refs_1_), channel_id=1, source_target_pairs={{0,32},{1,33},{2,34},{3,35},{4,36},{5,37},{6,38},{7,39},{8,40},{9,... | collective-permute-start | bytes 1327112 | tf_op jit(solution)/shard_map/ppermute | solution.py:35
  352.8 24.3 %collective-permute-start.70 = (bf16[128,1024]{1,0:T(8,128)(2,1)S(1)}, bf16[128,1024]{1,0:T(8,128)(2,1)}, u32[]{:S(2)}, u32[]{:S(2)}) collective-permute-start(bf16[128,1024]{1,0:T(8,128)(2,1)S(1)} %copy-done.28), channel_id=1, source_target_pairs={{0,64},{1,65},{2,66},{3,67},{4,68},{5,69},{6,70},{7,71},{8,72},{9,... | collective-permute-start | bytes 786440 | tf_op jit(solution)/shard_map/ppermute | solution.py:35
  354.3 22.8 %collective-permute-start.69 = (bf16[128,1024]{1,0:T(8,128)(2,1)S(1)}, bf16[128,1024]{1,0:T(8,128)(2,1)}, u32[]{:S(2)}, u32[]{:S(2)}) collective-permute-start(bf16[128,1024]{1,0:T(8,128)(2,1)S(1)} %copy-done.29), channel_id=1, source_target_pairs={{0,64},{1,65},{2,66},{3,67},{4,68},{5,69},{6,70},{7,71},{8,72},{9,... | collective-permute-start | bytes 786440 | tf_op jit(solution)/shard_map/ppermute | solution.py:35
  396.7 24.9 %collective-permute-start.74 = (bf16[144,1536]{1,0:T(8,128)(2,1)S(1)}, bf16[144,1536]{1,0:T(8,128)(2,1)S(1)}, u32[]{:S(2)}, u32[]{:S(2)}) collective-permute-start(bf16[144,1536]{1,0:T(8,128)(2,1)S(1)} %add_convert_fusion.refs_1_), channel_id=1, source_target_pairs={{0,32},{1,33},{2,34},{3,35},{4,36},{5,37},{6,38},{7,39},{8,40},{9,... | collective-permute-start | bytes 1327112 | tf_op jit(solution)/shard_map/ppermute | solution.py:35
  406.4 24.1 %collective-permute-start.83 = (bf16[144,1536]{1,0:T(8,128)(2,1)S(1)}, bf16[144,1536]{1,0:T(8,128)(2,1)S(1)}, u32[]{:S(2)}, u32[]{:S(2)}) collective-permute-start(bf16[144,1536]{1,0:T(8,128)(2,1)S(1)} %copy-done.32), channel_id=1, source_target_pairs={{0,64},{1,65},{2,66},{3,67},{4,68},{5,69},{6,70},{7,71},{8,72},{9,... | collective-permute-start | bytes 1327112 | tf_op jit(solution)/shard_map/ppermute | solution.py:35
  407.7 22.9 %collective-permute-start.76 = (bf16[144,1536]{1,0:T(8,128)(2,1)S(1)}, bf16[144,1536]{1,0:T(8,128)(2,1)S(1)}, u32[]{:S(2)}, u32[]{:S(2)}) collective-permute-start(bf16[144,1536]{1,0:T(8,128)(2,1)S(1)} %add_convert_fusion.refs_1_), channel_id=1, source_target_pairs={{64,0},{65,1},{66,2},{67,3},{68,4},{69,5},{70,6},{71,7},{72,8},{73... | collective-permute-start | bytes 1327112 | tf_op jit(solution)/shard_map/ppermute | solution.py:35
  (144 other events, 1450.2 us)

commit v5 on v4

--- a/solution.py
+++ b/solution.py
@@ -97,12 +97,10 @@
     )
 
 
-def masked_scores(query, keys, begin, block, reach):
-    scores = dot_right(query, keys)
+def visible(begin, block, reach):
     rows = block * QROWS + lax.broadcasted_iota(jnp.int32, (QROWS, reach), 0)
     columns = lax.broadcasted_iota(jnp.int32, (QROWS, reach), 1)
-    seen = (columns <= rows) & (columns >= begin)
-    return jnp.where(seen, scores, -1e30)
+    return (columns <= rows) & (columns >= begin)
 
 
 def unit_rows(where_ref, m):
@@ -124,16 +122,16 @@
         reach = (block + 1) * QROWS
         keys, values = k_ref[:reach, :], v_ref[:reach, :]
         query = q_ref[rows, :]
-        begin = begin_ref[rows, :1]
+        seen = visible(begin_ref[rows, :1], block, reach)
         outs, logs = [], []
         for head in range(2):
             own = head_lanes(QROWS, head)
-            scores = masked_scores(jnp.where(own, query, jnp.zeros_like(query)), keys, begin, block, reach)
+            scores = dot_right(jnp.where(own, query, jnp.zeros_like(query)), keys)
+            scores = jnp.where(seen, scores, -1e30)
             highest = jnp.max(scores, axis=-1, keepdims=True)
             exponent = jnp.exp(scores - highest)
             total = jnp.sum(exponent, axis=-1, keepdims=True)
-            probs = (exponent * (1.0 / total)).astype(BF)
-            outs.append(dot(probs, values))
+            outs.append(dot(exponent.astype(BF), values) * (1.0 / total))
             logs.append(highest + jnp.log(total))
         first = head_lanes(QROWS, 0)
         o_ref[rows, :] = jnp.where(first, outs[0], outs[1]).astype(BF)
@@ -150,13 +148,13 @@
         reach = (block + 1) * QROWS
         keys, values = k_ref[:reach, :], v_ref[:reach, :]
         query, upstream, mixed = q_ref[rows, :], do_ref[rows, :], o_ref[rows, :].astype(F32)
-        begin = begin_ref[rows, :1]
+        seen = visible(begin_ref[rows, :1], block, reach)
         grads = []
         for head in range(2):
             own = head_lanes(QROWS, head)
             query_own = jnp.where(own, query, jnp.zeros_like(query))
             up_own = jnp.where(own, upstream, jnp.zeros_like(upstream))
-            scores = masked_scores(query_own, keys, begin, block, reach)
+            scores = jnp.where(seen, dot_right(query_own, keys), -1e30)
             probs = jnp.exp(scores - lse_ref[rows, head * HEAD : head * HEAD + 1])
             centre = jnp.sum(up_own.astype(F32) * mixed, axis=-1, keepdims=True)
             moved = (probs * (dot_right(up_own, values) - centre)).astype(BF)

time: 449 us -> 439 us (0.978)
  starting transfers between devices: 173 us -> 162 us
    ppermute x84, starting transfers between devices: 132 us -> 121 us  [route(): return lax.ppermute(block, AXES, pairs)]
  transfers between devices with their start and end apart: 92 -> 92, of which waited for: 24 -> 24; matrix products, arithmetic and copies ran while one was open for 11% -> 12% of each run, Pallas kernels for 16% -> 16%
where the time goes in v5:
time: 439 us; the launch traced here: 431 us
  starting transfers between devices  162 us (37%)
  Pallas kernels  103 us (23%)
  waiting for transfers between devices  81.6 us (19%)
  other arithmetic  43.6 us (10%)
  local copies, waits for them, and re-layouts  38.3 us (9%)
    ppermute x84, starting transfers between devices, route(): return lax.ppermute(block, AXES, pairs)  121 us
    pallas_call x13, Pallas kernels, run(): pl.pallas_call(lambda *refs: body(*refs[:count], *refs[count + len(others...  103 us
    ppermute x84, waiting for transfers between devices, route(): return lax.ppermute(block, AXES, pairs)  80 us
    all_to_all x8, starting transfers between devices, swapped(): return lax.all_to_all(blocks, axes, split_axis=0, concat_axis=0, tiled=True)  40.9 us
    unnamed x153, local copies, waits for them, and re-layouts  19.6 us
    convert_element_type x12, other arithmetic, joined_cores(): return [joined[0]] + [joined[r].astype(BF) for r in (1, 2, 3)]  13.8 us
    broadcast_in_dim x4, local copies, waits for them, and re-layouts, from_all(): return swapped(jnp.broadcast_to(block[None], (count, *block.shape)), axes)  9.23 us
  transfers between devices with their start and end apart: 92, of which 24 were waited for; matrix products, arithmetic and copies ran while one was open for 12% of the time, Pallas kernels for 16%

profile of v5, /device:TPU:9, one launch (start us, length us, event | category | flops | bytes accessed | tf_op | source)
XLA Modules:
  0.0 430.8 jit_solution(1893141289098349477)
XLA Ops:
  35.0 6.6 %collective-permute-done.4.refs_3_.refs_5_ = bf16[128,1024]{1,0:T(8,128)(2,1)} collective-permute-done((bf16[128,1024]{1,0:T(8,128)(2,1)S(1)}, bf16[128,1024]{1,0:T(8,128)(2,1)}, u32[]{:S(2)}, u32[]{:S(2)}) %collective-permute-start.4) | collective-permute-done | bytes 262176 | tf_op jit(solution)/shard_map/ppermute | solution.py:35
  46.8 5.5 %all-to-all-start.1 = ((bf16[8,128,1024]{2,1,0:T(8,128)(2,1)}), bf16[8,128,1024]{2,1,0:T(8,128)(2,1)S(1)}, u32[]{:S(2)}, u32[]{:S(2)}) async-start(bf16[8,128,1024]{2,1,0:T(8,128)(2,1)} %broadcast_in_dim.19), calls=%async_computation.1 | async-start | bytes 4194304 | tf_op jit(solution)/shard_map/all_to_all | solution.py:44
  77.8 10.6 %shard_map.266 = (bf16[384,1024]{1,0:T(8,128)(2,1)}, f32[8,1024]{1,0:T(8,128)}, f32[128,128]{1,0:T(8,128)}, bf16[1024,1024]{1,0:T(8,128)(2,1)}, bf16[1024,128]{1...) custom-call(s32[26]{0:T(128)} %concatenate.48.refs_0_, ...), custom_call_target="tpu_custom_call" | custom-call | flops 5000000000 | bytes 4000000 | tf_op jit(solution)/shard_map/pallas_call | solution.py:212
  90.7 8.2 %shard_map.268 = (bf16[512,1024]{1,0:T(8,128)(2,1)}, bf16[1024,512]{1,0:T(8,128)(2,1)}, bf16[1024,512]{1,0:T(8,128)(2,1)}, bf16[1024,512]{1,0:T(8,128)(2,1)}, bf...) custom-call(s32[26]{0:T(128)} %concatenate.48.refs_0_, ...), custom_call_target="tpu_custom_call" | custom-call | flops 3000000000 | bytes 4000000 | tf_op jit(solution)/shard_map/pallas_call | solution.py:212
  101.5 5.3 %all-to-all-start.2 = ((bf16[8,144,896]{2,1,0:T(8,128)(2,1)}), bf16[8,144,896]{2,1,0:T(8,128)(2,1)S(1)}, u32[]{:S(2)}, u32[]{:S(2)}) async-start(bf16[8,144,896]{2,1,0:T(8,128)(2,1)} %broadcast_in_dim.21), calls=%async_computation.2 | async-start | bytes 4128768 | tf_op jit(solution)/shard_map/all_to_all | solution.py:44
  135.5 5.5 %collective-permute-done.22.refs_2_.refs_5_ = bf16[128,1024]{1,0:T(8,128)(2,1)} collective-permute-done((bf16[128,1024]{1,0:T(8,128)(2,1)S(1)}, bf16[128,1024]{1,0:T(8,128)(2,1)}, u32[]{:S(2)}, u32[]{:S(2)}) %collective-permute-start.22) | collective-permute-done | bytes 262176 | tf_op jit(solution)/shard_map/ppermute | solution.py:35
  154.8 14.6 %shard_map.271 = (bf16[384,1024]{1,0:T(8,128)(2,1)}, f32[8,1024]{1,0:T(8,128)}, bf16[512,1024]{1,0:T(8,128)(2,1)}, bf16[1024,512]{1,0:T(8,128)(2,1)}, bf16[1024,...) custom-call(s32[26]{0:T(128)} %concatenate.48.refs_0_, ...), custom_call_target="tpu_custom_call" | custom-call | flops 8000000000 | bytes 4000000 | tf_op jit(solution)/shard_map/pallas_call | solution.py:212
  175.4 14.1 %shard_map.274 = (bf16[128,1024]{1,0:T(8,128)(2,1)}, bf16[128,1024]{1,0:T(8,128)(2,1)}, bf16[128,1024]{1,0:T(8,128)(2,1)}, bf16[128,1024]{1,0:T(8,128)(2,1)}, bf...) custom-call(s32[26]{0:T(128)} %concatenate.48.refs_0_, ...), custom_call_target="tpu_custom_call" | custom-call | flops 8000000000 | bytes 4000000 | tf_op jit(solution)/shard_map/pallas_call | solution.py:212
  200.2 5.7 %shard_map.275.refs_1_ = bf16[8,144,640]{2,1,0:T(8,128)(2,1)} custom-call(s32[26]{0:T(128)} %concatenate.48.refs_0_, bf16[1024,1024]{1,0:T(8,128)(2,1)} %get-tuple-element.188.refs_1_, bf16[1024,512]{1,0:T(8,128)(2,1)} %get-tuple-element.189.refs_2_.refs_1_, bf16[1024,128]{1,0:T(8,128)(2,1)} %get-tuple-element.173.refs_4_.refs_3_.refs_2_, ...), custom_call_target="tpu_custom_call" | custom-call | flops 1342177280 | bytes 4000000 | tf_op jit(solution)/shard_map/pallas_call | solution.py:212
  205.9 5.3 %all-to-all-start.4 = ((bf16[8,144,640]{2,1,0:T(8,128)(2,1)}), bf16[8,144,640]{2,1,0:T(8,128)(2,1)S(1)}, u32[]{:S(2)}, u32[]{:S(2)}) async-start(bf16[8,144,640]{2,1,0:T(8,128)(2,1)} %shard_map.275.refs_1_), calls=%async_computation.4 | async-start | bytes 2949120 | tf_op jit(solution)/shard_map/all_to_all | solution.py:44
  221.1 7.5 %collective-permute-start.48 = (bf16[128,1024]{1,0:T(8,128)(2,1)S(1)}, bf16[128,1024]{1,0:T(8,128)(2,1)S(1)}, u32[]{:S(2)}, u32[]{:S(2)}) collective-permute-start(bf16[128,1024]{1,0:T(8,128)(2,1)S(1)} %collective-permute-done.47.refs_6_), channel_id=1, source_target_pairs={{0,64},{1,65},{2,66},{3,67},{4,68},{5,69},{6,70},{7,71},{8,72},{9,... | collective-permute-start | bytes 786440 | tf_op jit(solution)/shard_map/ppermute | solution.py:35
  229.2 5.8 %shard_map.277.refs_9_ = bf16[8,144,896]{2,1,0:T(8,128)(2,1)} custom-call(s32[26]{0:T(128)} %concatenate.48.refs_0_, bf16[1024,1024]{1,0:T(8,128)(2,1)} %get-tuple-element.188.refs_1_, bf16[1024,512]{1,0:T(8,128)(2,1)} %get-tuple-element.190.refs_12_.refs_2_, bf16[1024,384]{1,0:T(8,128)(2,1)} %get-tuple-element.197.refs_3_, bf16[128,1024]{1,0:T(8,128)(2,1)} %copy-done.21), custom_call_target="tpu_custom_call" | custom-call | flops 1879048192 | bytes 4000000 | tf_op jit(solution)/shard_map/pallas_call | solution.py:212
  237.0 5.6 %all-to-all-start.5 = ((bf16[8,144,896]{2,1,0:T(8,128)(2,1)}), bf16[8,144,896]{2,1,0:T(8,128)(2,1)S(1)}, u32[]{:S(2)}, u32[]{:S(2)}) async-start(bf16[8,144,896]{2,1,0:T(8,128)(2,1)} %get-tuple-element.227), calls=%async_computation.5 | async-start | bytes 4128768 | tf_op jit(solution)/shard_map/all_to_all | solution.py:44
  242.6 9.2 %shard_map.279 = (bf16[8,144,1152]{2,1,0:T(8,128)(2,1)}, bf16[1024,512]{1,0:T(8,128)(2,1)}, bf16[1024,128]{1,0:T(8,128)(2,1)}) custom-call(s32[26]{0:T(128)} %concatenate.48.refs_0_, bf16[1024,1024]{1,0:T(8,128)(2,1)} %get-tuple-element.160.refs_3_.refs_1_, bf16[1024,512]{1,0:T(8,128)(2,1)} %get-tuple-element.171.refs_2_, ...), custom_call_target="tpu_custom_call" | custom-call | flops 2415919104 | bytes 4000000 | tf_op jit(solution)/shard_map/pallas_call | solution.py:212
  251.9 11.4 %shard_map.280 = (bf16[128,1024]{1,0:T(8,128)(2,1)}, bf16[128,1024]{1,0:T(8,128)(2,1)}, bf16[128,1024]{1,0:T(8,128)(2,1)}, bf16[128,1024]{1,0:T(8,128)(2,1)}, bf...) custom-call(s32[26]{0:T(128)} %concatenate.48.refs_0_, ...), custom_call_target="tpu_custom_call" | custom-call | flops 6000000000 | bytes 4000000 | tf_op jit(solution)/shard_map/pallas_call | solution.py:212
  277.6 5.3 %all-to-all-start.6 = ((bf16[8,144,1152]{2,1,0:T(8,128)(2,1)}), bf16[8,144,1152]{2,1,0:T(8,128)(2,1)S(1)}, u32[]{:S(2)}, u32[]{:S(2)}) async-start(bf16[8,144,1152]{2,1,0:T(8,128)(2,1)} %get-tuple-element.238), calls=%async_computation.6 | async-start | bytes 5308416 | tf_op jit(solution)/shard_map/all_to_all | solution.py:44
  300.6 5.6 %collective-permute-start.63 = (bf16[128,128]{1,0:T(8,128)(2,1)S(1)}, bf16[128,128]{1,0:T(8,128)(2,1)S(1)}, u32[]{:S(2)}, u32[]{:S(2)}) collective-permute-start(bf16[128,128]{1,0:T(8,128)(2,1)S(1)} %slice.114), channel_id=1, source_target_pairs={{0,0},{1,64},{2,16},{3,80},{4,32},{5,96},{6,48},{7,112},{8,8},{9,7... | collective-permute-start | bytes 98312 | tf_op jit(solution)/shard_map/ppermute | solution.py:35
  322.8 7.1 %collective-permute-done.64.refs_5_ = bf16[144,1536]{1,0:T(8,128)(2,1)} collective-permute-done((bf16[144,1536]{1,0:T(8,128)(2,1)S(1)}, bf16[144,1536]{1,0:T(8,128)(2,1)}, u32[]{:S(2)}, u32[]{:S(2)}) %collective-permute-start.64) | collective-permute-done | bytes 442400 | tf_op jit(solution)/shard_map/ppermute | solution.py:35
  343.9 11.9 %collective-permute-done.65.refs_1_.refs_2_ = bf16[144,1536]{1,0:T(8,128)(2,1)S(1)} collective-permute-done((bf16[144,1536]{1,0:T(8,128)(2,1)S(1)}, bf16[144,1536]{1,0:T(8,128)(2,1)S(1)}, u32[]{:S(2)}, u32[]{:S(2)}) %collective-permute-start.65) | collective-permute-done | bytes 442400 | tf_op jit(solution)/shard_map/ppermute | solution.py:35
  380.5 5.4 %collective-permute-done.72 = bf16[144,1536]{1,0:T(8,128)(2,1)S(1)} collective-permute-done((bf16[144,1536]{1,0:T(8,128)(2,1)S(1)}, bf16[144,1536]{1,0:T(8,128)(2,1)S(1)}, u32[]{:S(2)}, u32[]{:S(2)}) %collective-permute-start.72) | collective-permute-done | bytes 442400 | tf_op jit(solution)/shard_map/ppermute | solution.py:35
  386.3 7.8 %collective-permute-start.74 = (bf16[144,1536]{1,0:T(8,128)(2,1)S(1)}, bf16[144,1536]{1,0:T(8,128)(2,1)S(1)}, u32[]{:S(2)}, u32[]{:S(2)}) collective-permute-start(bf16[144,1536]{1,0:T(8,128)(2,1)S(1)} %add_convert_fusion.refs_1_), channel_id=1, source_target_pairs={{0,32},{1,33},{2,34},{3,35},{4,36},{5,37},{6,38},{7,39},{8,40},{9,... | collective-permute-start | bytes 1327112 | tf_op jit(solution)/shard_map/ppermute | solution.py:35
  402.3 5.6 %collective-permute-start.79 = (bf16[144,1536]{1,0:T(8,128)(2,1)}, bf16[144,1536]{1,0:T(8,128)(2,1)S(1)}, u32[]{:S(2)}, u32[]{:S(2)}) collective-permute-start(bf16[144,1536]{1,0:T(8,128)(2,1)} %collective-permute-done.75.refs_4_), channel_id=1, source_target_pairs={{64,0},{65,1},{66,2},{67,3},{68,4},{69,5},{70,6},{71,7},{72,8},{73... | collective-permute-start | bytes 1327112 | tf_op jit(solution)/shard_map/ppermute | solution.py:35
  411.3 5.4 %collective-permute-start.78 = (bf16[144,1536]{1,0:T(8,128)(2,1)S(1)}, bf16[144,1536]{1,0:T(8,128)(2,1)S(1)}, u32[]{:S(2)}, u32[]{:S(2)}) collective-permute-start(bf16[144,1536]{1,0:T(8,128)(2,1)S(1)} %collective-permute-done.74.refs_3_), channel_id=1, source_target_pairs={{64,0},{65,1},{66,2},{67,3},{68,4},{69,5},{70,6},{71,7},{72,8},{73... | collective-permute-start | bytes 1327112 | tf_op jit(solution)/shard_map/ppermute | solution.py:35
  421.7 7.7 %shard_map.288 = (f32[128,3072]{1,0:T(8,128)}, f32[128,4096]{1,0:T(8,128)}, f32[512,1024]{1,0:T(8,128)}, f32[128,1024]{1,0:T(8,128)}, f32[1,256]{1,0:T(1,128)}, ...) custom-call(s32[26]{0:T(128)} %concatenate.48.refs_0_, ...), custom_call_target="tpu_custom_call" | custom-call | bytes 4000000 | tf_op jit(solution)/shard_map/pallas_call | solution.py:212
  (431 shorter events, 246.1 us)
Async XLA Ops:
  18.9 24.3 %all-to-all-start = ((bf16[8,144,640]{2,1,0:T(8,128)(2,1)}), bf16[8,144,640]{2,1,0:T(8,128)(2,1)S(1)}, u32[]{:S(2)}, u32[]{:S(2)}) async-start(bf16[8,144,640]{2,1,0:T(8,128)(2,1)} %broadcast_in_dim.18), calls=%async_computation | async-start | bytes 2949120 | tf_op jit(solution)/shard_map/all_to_all | solution.py:44
  46.8 42.6 %all-to-all-start.1 = ((bf16[8,128,1024]{2,1,0:T(8,128)(2,1)}), bf16[8,128,1024]{2,1,0:T(8,128)(2,1)S(1)}, u32[]{:S(2)}, u32[]{:S(2)}) async-start(bf16[8,128,1024]{2,1,0:T(8,128)(2,1)} %broadcast_in_dim.19), calls=%async_computation.1 | async-start | bytes 4194304 | tf_op jit(solution)/shard_map/all_to_all | solution.py:44
  101.5 42.0 %all-to-all-start.2 = ((bf16[8,144,896]{2,1,0:T(8,128)(2,1)}), bf16[8,144,896]{2,1,0:T(8,128)(2,1)S(1)}, u32[]{:S(2)}, u32[]{:S(2)}) async-start(bf16[8,144,896]{2,1,0:T(8,128)(2,1)} %broadcast_in_dim.21), calls=%async_computation.2 | async-start | bytes 4128768 | tf_op jit(solution)/shard_map/all_to_all | solution.py:44
  129.3 22.7 %collective-permute-start.27 = (bf16[128,1024]{1,0:T(8,128)(2,1)S(1)}, bf16[128,1024]{1,0:T(8,128)(2,1)}, u32[]{:S(2)}, u32[]{:S(2)}) collective-permute-start(bf16[128,1024]{1,0:T(8,128)(2,1)S(1)} %get-tuple-element.305.refs_1_), channel_id=1, source_target_pairs={{0,64},{1,65},{2,66},{3,67},{4,68},{5,69},{6,70},{7,71},{8,72},{9,... | collective-permute-start | bytes 786440 | tf_op jit(solution)/shard_map/ppermute | solution.py:35
  133.8 20.9 %collective-permute-start.30 = (bf16[128,1024]{1,0:T(8,128)(2,1)}, bf16[128,1024]{1,0:T(8,128)(2,1)}, u32[]{:S(2)}, u32[]{:S(2)}) collective-permute-start(bf16[128,1024]{1,0:T(8,128)(2,1)} %collective-permute-done.23.refs_3_.refs_7_), channel_id=1, source_target_pairs={{0,64},{1,65},{2,66},{3,67},{4,68},{5,69},{6,70},{7,71},{8,72},{9,... | collective-permute-start | bytes 786440 | tf_op jit(solution)/shard_map/ppermute | solution.py:35
  143.0 26.4 %collective-permute-start.26 = (bf16[128,1024]{1,0:T(8,128)(2,1)}, bf16[128,1024]{1,0:T(8,128)(2,1)S(1)}, u32[]{:S(2)}, u32[]{:S(2)}) collective-permute-start(bf16[128,1024]{1,0:T(8,128)(2,1)} %shard_map.269.refs_0_), channel_id=1, source_target_pairs={{0,16},{1,17},{2,18},{3,19},{4,20},{5,21},{6,22},{7,23},{8,24},{9,... | collective-permute-start | bytes 786440 | tf_op jit(solution)/shard_map/ppermute | solution.py:35
  146.9 27.4 %all-to-all-start.3 = ((bf16[8,128,512]{2,1,0:T(8,128)(2,1)}), bf16[8,128,512]{2,1,0:T(8,128)(2,1)S(1)}, u32[]{:S(2)}, u32[]{:S(2)}) async-start(bf16[8,128,512]{2,1,0:T(8,128)(2,1)} %broadcast_in_dim.22), calls=%async_computation.3 | async-start | bytes 2097152 | tf_op jit(solution)/shard_map/all_to_all | solution.py:44
  205.9 29.9 %all-to-all-start.4 = ((bf16[8,144,640]{2,1,0:T(8,128)(2,1)}), bf16[8,144,640]{2,1,0:T(8,128)(2,1)S(1)}, u32[]{:S(2)}, u32[]{:S(2)}) async-start(bf16[8,144,640]{2,1,0:T(8,128)(2,1)} %shard_map.275.refs_1_), calls=%async_computation.4 | async-start | bytes 2949120 | tf_op jit(solution)/shard_map/all_to_all | solution.py:44
  237.0 38.9 %all-to-all-start.5 = ((bf16[8,144,896]{2,1,0:T(8,128)(2,1)}), bf16[8,144,896]{2,1,0:T(8,128)(2,1)S(1)}, u32[]{:S(2)}, u32[]{:S(2)}) async-start(bf16[8,144,896]{2,1,0:T(8,128)(2,1)} %get-tuple-element.227), calls=%async_computation.5 | async-start | bytes 4128768 | tf_op jit(solution)/shard_map/all_to_all | solution.py:44
  277.6 52.2 %all-to-all-start.6 = ((bf16[8,144,1152]{2,1,0:T(8,128)(2,1)}), bf16[8,144,1152]{2,1,0:T(8,128)(2,1)S(1)}, u32[]{:S(2)}, u32[]{:S(2)}) async-start(bf16[8,144,1152]{2,1,0:T(8,128)(2,1)} %get-tuple-element.238), calls=%async_computation.6 | async-start | bytes 5308416 | tf_op jit(solution)/shard_map/all_to_all | solution.py:44
  284.4 35.7 %collective-permute-start.56 = (bf16[128,1024]{1,0:T(8,128)(2,1)}, bf16[128,1024]{1,0:T(8,128)(2,1)}, u32[]{:S(2)}, u32[]{:S(2)}) collective-permute-start(bf16[128,1024]{1,0:T(8,128)(2,1)} %get-tuple-element.247), channel_id=1, source_target_pairs={{0,64},{1,65},{2,66},{3,67},{4,68},{5,69},{6,70},{7,71},{8,72},{9,... | collective-permute-start | bytes 786440 | tf_op jit(solution)/shard_map/ppermute | solution.py:35
  290.7 29.4 %collective-permute-start.57 = (bf16[128,1024]{1,0:T(8,128)(2,1)}, bf16[128,1024]{1,0:T(8,128)(2,1)}, u32[]{:S(2)}, u32[]{:S(2)}) collective-permute-start(bf16[128,1024]{1,0:T(8,128)(2,1)} %add_convert_fusion.4.refs_3_.refs_2_), channel_id=1, source_target_pairs={{0,16},{1,17},{2,18},{3,19},{4,20},{5,21},{6,22},{7,23},{8,24},{9,... | collective-permute-start | bytes 786440 | tf_op jit(solution)/shard_map/ppermute | solution.py:35
  297.0 23.1 %collective-permute-start.58 = (bf16[128,1024]{1,0:T(8,128)(2,1)}, bf16[128,1024]{1,0:T(8,128)(2,1)}, u32[]{:S(2)}, u32[]{:S(2)}) collective-permute-start(bf16[128,1024]{1,0:T(8,128)(2,1)} %add_convert_fusion.3.refs_4_.refs_3_), channel_id=1, source_target_pairs={{0,32},{1,33},{2,34},{3,35},{4,36},{5,37},{6,38},{7,39},{8,40},{9,... | collective-permute-start | bytes 786440 | tf_op jit(solution)/shard_map/ppermute | solution.py:35
  300.6 19.5 %collective-permute-start.59 = (bf16[128,1024]{1,0:T(8,128)(2,1)}, bf16[128,1024]{1,0:T(8,128)(2,1)}, u32[]{:S(2)}, u32[]{:S(2)}) collective-permute-start(bf16[128,1024]{1,0:T(8,128)(2,1)} %add_convert_fusion.2.refs_5_.refs_4_), channel_id=1, source_target_pairs={{0,48},{1,49},{2,50},{3,51},{4,52},{5,53},{6,54},{7,55},{8,56},{9,... | collective-permute-start | bytes 786440 | tf_op jit(solution)/shard_map/ppermute | solution.py:35
  332.7 23.1 %collective-permute-start.65 = (bf16[144,1536]{1,0:T(8,128)(2,1)S(1)}, bf16[144,1536]{1,0:T(8,128)(2,1)S(1)}, u32[]{:S(2)}, u32[]{:S(2)}) collective-permute-start(bf16[144,1536]{1,0:T(8,128)(2,1)S(1)} %add_convert_fusion.1.refs_1_), channel_id=1, source_target_pairs={{0,48},{1,49},{2,50},{3,51},{4,52},{5,53},{6,54},{7,55},{8,56},{9,... | collective-permute-start | bytes 1327112 | tf_op jit(solution)/shard_map/ppermute | solution.py:35
  337.2 29.5 %all-to-all-start.7 = ((bf16[8,144,384]{2,1,0:T(8,128)(2,1)}), bf16[8,144,384]{2,1,0:T(8,128)(2,1)S(1)}, u32[]{:S(2)}, u32[]{:S(2)}) async-start(bf16[8,144,384]{2,1,0:T(8,128)(2,1)} %get-tuple-element.258), calls=%async_computation.7 | async-start | bytes 1769472 | tf_op jit(solution)/shard_map/all_to_all | solution.py:44
  341.1 25.5 %collective-permute-start.67 = (bf16[144,1536]{1,0:T(8,128)(2,1)S(1)}, bf16[144,1536]{1,0:T(8,128)(2,1)S(1)}, u32[]{:S(2)}, u32[]{:S(2)}) collective-permute-start(bf16[144,1536]{1,0:T(8,128)(2,1)S(1)} %add_convert_fusion.1.refs_1_), channel_id=1, source_target_pairs={{0,16},{1,17},{2,18},{3,19},{4,20},{5,21},{6,22},{7,23},{8,24},{9,... | collective-permute-start | bytes 1327112 | tf_op jit(solution)/shard_map/ppermute | solution.py:35
  341.1 25.5 %collective-permute-start.66 = (bf16[144,1536]{1,0:T(8,128)(2,1)S(1)}, bf16[144,1536]{1,0:T(8,128)(2,1)}, u32[]{:S(2)}, u32[]{:S(2)}) collective-permute-start(bf16[144,1536]{1,0:T(8,128)(2,1)S(1)} %add_convert_fusion.1.refs_1_), channel_id=1, source_target_pairs={{0,32},{1,33},{2,34},{3,35},{4,36},{5,37},{6,38},{7,39},{8,40},{9,... | collective-permute-start | bytes 1327112 | tf_op jit(solution)/shard_map/ppermute | solution.py:35
  342.3 24.3 %collective-permute-start.70 = (bf16[128,1024]{1,0:T(8,128)(2,1)S(1)}, bf16[128,1024]{1,0:T(8,128)(2,1)}, u32[]{:S(2)}, u32[]{:S(2)}) collective-permute-start(bf16[128,1024]{1,0:T(8,128)(2,1)S(1)} %copy-done.28), channel_id=1, source_target_pairs={{0,64},{1,65},{2,66},{3,67},{4,68},{5,69},{6,70},{7,71},{8,72},{9,... | collective-permute-start | bytes 786440 | tf_op jit(solution)/shard_map/ppermute | solution.py:35
  343.8 22.8 %collective-permute-start.69 = (bf16[128,1024]{1,0:T(8,128)(2,1)S(1)}, bf16[128,1024]{1,0:T(8,128)(2,1)}, u32[]{:S(2)}, u32[]{:S(2)}) collective-permute-start(bf16[128,1024]{1,0:T(8,128)(2,1)S(1)} %copy-done.29), channel_id=1, source_target_pairs={{0,64},{1,65},{2,66},{3,67},{4,68},{5,69},{6,70},{7,71},{8,72},{9,... | collective-permute-start | bytes 786440 | tf_op jit(solution)/shard_map/ppermute | solution.py:35
  386.3 24.9 %collective-permute-start.74 = (bf16[144,1536]{1,0:T(8,128)(2,1)S(1)}, bf16[144,1536]{1,0:T(8,128)(2,1)S(1)}, u32[]{:S(2)}, u32[]{:S(2)}) collective-permute-start(bf16[144,1536]{1,0:T(8,128)(2,1)S(1)} %add_convert_fusion.refs_1_), channel_id=1, source_target_pairs={{0,32},{1,33},{2,34},{3,35},{4,36},{5,37},{6,38},{7,39},{8,40},{9,... | collective-permute-start | bytes 1327112 | tf_op jit(solution)/shard_map/ppermute | solution.py:35
  394.9 21.7 %collective-permute-start.73 = (bf16[144,1536]{1,0:T(8,128)(2,1)S(1)}, bf16[144,1536]{1,0:T(8,128)(2,1)S(1)}, u32[]{:S(2)}, u32[]{:S(2)}) collective-permute-start(bf16[144,1536]{1,0:T(8,128)(2,1)S(1)} %add_convert_fusion.refs_1_), channel_id=1, source_target_pairs={{0,48},{1,49},{2,50},{3,51},{4,52},{5,53},{6,54},{7,55},{8,56},{9,... | collective-permute-start | bytes 1327112 | tf_op jit(solution)/shard_map/ppermute | solution.py:35
  395.9 24.1 %collective-permute-start.83 = (bf16[144,1536]{1,0:T(8,128)(2,1)S(1)}, bf16[144,1536]{1,0:T(8,128)(2,1)S(1)}, u32[]{:S(2)}, u32[]{:S(2)}) collective-permute-start(bf16[144,1536]{1,0:T(8,128)(2,1)S(1)} %copy-done.32), channel_id=1, source_target_pairs={{0,64},{1,65},{2,66},{3,67},{4,68},{5,69},{6,70},{7,71},{8,72},{9,... | collective-permute-start | bytes 1327112 | tf_op jit(solution)/shard_map/ppermute | solution.py:35
  397.3 22.9 %collective-permute-start.76 = (bf16[144,1536]{1,0:T(8,128)(2,1)S(1)}, bf16[144,1536]{1,0:T(8,128)(2,1)S(1)}, u32[]{:S(2)}, u32[]{:S(2)}) collective-permute-start(bf16[144,1536]{1,0:T(8,128)(2,1)S(1)} %add_convert_fusion.refs_1_), channel_id=1, source_target_pairs={{64,0},{65,1},{66,2},{67,3},{68,4},{69,5},{70,6},{71,7},{72,8},{73... | collective-permute-start | bytes 1327112 | tf_op jit(solution)/shard_map/ppermute | solution.py:35
  (144 other events, 1392.7 us)
